TPU v7x, 128 devices: a whole 4x4x4 slice. The times are simulated.
128 devices in a mesh: row: 8 (over y, z_hi), col: 16 (over x, z_lo, core).
Axes of the slice: x: 4, y: 4, z: 4 (z_hi: 2, z_lo: 2; z = z_hi * 2 + z_lo), core: 2. Of those that a mesh axis runs over, the one named last changes fastest.
Arguments:
- amps: bfloat16 [8, 16, 2, 2, 768, 768], P('row', 'col'), may hold values from -6 to 6
- x_factor: bfloat16 [16, 64, 768], P('row'), may hold values from -0.21875 to 0.21875
- core: bfloat16 [768, 768], replicated, may hold values from -6 to 6
- cycle_w: bfloat16 [8, 2, 2, 1024, 1024], P('row', None, None, 'col'), may hold values from -0.15625 to 0.15625
- domain_tiles: int32 [8, 16, 12], P('row', 'col'), may hold values from 0 to 15, as said below
- domain_count: int32 [8, 16], P('row', 'col'), may hold values from 6 to 12, as said below
- tile_slot: int32 [16], replicated, may hold values from 0 to 15, each once
- occ_energy: float32 [8, 16, 2, 2], P('row', 'col'), may hold values from -2 to -0.5
- virt_energy: float32 [1024], replicated, may hold values from 0.5 to 3
Outputs:
- residual: float32 [8, 16, 2, 2, 768, 768], P('row', 'col')
- updated: bfloat16 [8, 16, 2, 2, 768, 768], P('row', 'col')
Inputs may be any that keep to these rules, and one draw needn't show every extreme that they name: `domain_tiles`: each block's 12 entries are distinct tile numbers; the first domain_count of them form its domain. Blocks (r, c) and (r, c + 8) have the same list. `domain_count`: blocks (r, c) and (r, c + 8) have the same count. `tile_slot`: A permutation of the tile numbers.
All inputs are finite; a program needn't handle non-finite values.
Results may differ from a plain program's by a relative error of at most 0.0085.
Values may be sent and summed in bfloat16 or wider, within the bound.
A program may use at most 192 MiB of HBM per device.

v0:
```python
import functools

import jax
import jax.numpy as jnp
from jax import lax
from jax.experimental import pallas as pl
from jax.experimental.pallas import tpu as pltpu
from jax.sharding import PartitionSpec as P

MESH = pl.DeviceIdType.MESH
VMEM_LIMIT = 56 * 1024 * 1024


def gather_kernel(x_ref, w_ref, xall_ref, wall_ref, wsend, wrecv, xsend, xrecv, local):
    r = lax.axis_index("row")
    c = lax.axis_index("col")
    rows = lax.axis_size("row")
    cols = lax.axis_size("col")
    forth = (c + 4) % cols
    back = (c + cols - 4) % cols
    zside = c + 2 - 4 * ((c // 2) % 2)
    twin = c + 1 - 2 * (c % 2)
    core = c % 2

    barrier = pltpu.get_barrier_semaphore()
    for other in (forth, back, zside, twin):
        pl.semaphore_signal(barrier, inc=1, device_id=(r, other), device_id_type=MESH)
    for step in range(1, rows):
        pl.semaphore_signal(barrier, inc=1, device_id=((r + step) % rows, c), device_id_type=MESH)
    pl.semaphore_wait(barrier, 4 + rows - 1)

    started = []

    def send(src, dst, sems, index, device):
        copy = pltpu.make_async_remote_copy(
            src_ref=src, dst_ref=dst, send_sem=sems[0].at[index], recv_sem=sems[1].at[index],
            device_id=device, device_id_type=MESH,
        )
        copy.start()
        started.append(copy)

    def arrived(dst, sems, index):
        pltpu.make_async_remote_copy(
            src_ref=dst, dst_ref=dst, send_sem=sems[0].at[index], recv_sem=sems[1].at[index],
            device_id=(r, twin), device_id_type=MESH,
        ).wait_recv()

    wsems = (wsend, wrecv)
    xsems = (xsend, xrecv)
    half = w_ref.shape[0] // 2

    def shard(offset, plane, side):
        x = (c // 4 + offset) % (cols // 4)
        z = (c // 2) % 2
        z = z + plane * (1 - 2 * z)
        k = core + side * (1 - 2 * core)
        return x * 4 + z * 2 + k

    send(w_ref, wall_ref.at[c], wsems, 0, (r, forth))
    send(w_ref, wall_ref.at[c], wsems, 1, (r, back))
    send(w_ref, wall_ref.at[c], wsems, 4, (r, zside))
    for step in range(1, rows):
        send(x_ref.at[core], xall_ref.at[r, core], xsems, step - 1, ((r + step) % rows, c))
    send(w_ref, wall_ref.at[c], wsems, 8, (r, twin))
    own_w = pltpu.make_async_copy(w_ref, wall_ref.at[c], local.at[0])
    own_x = pltpu.make_async_copy(x_ref, xall_ref.at[r], local.at[1])
    own_w.start()
    own_x.start()

    slot = shard(3, 0, 0)
    arrived(wall_ref.at[slot], wsems, 0)
    send(wall_ref.at[slot, :half], wall_ref.at[slot, :half], wsems, 2, (r, forth))
    send(wall_ref.at[slot], wall_ref.at[slot], wsems, 7, (r, zside))
    send(wall_ref.at[slot], wall_ref.at[slot], wsems, 11, (r, twin))
    slot = shard(1, 0, 0)
    arrived(wall_ref.at[slot], wsems, 1)
    send(wall_ref.at[slot, half:], wall_ref.at[slot, half:], wsems, 3, (r, back))
    send(wall_ref.at[slot], wall_ref.at[slot], wsems, 5, (r, zside))
    send(wall_ref.at[slot], wall_ref.at[slot], wsems, 9, (r, twin))
    for step in range(1, rows):
        origin = (r + rows - step) % rows
        arrived(xall_ref.at[origin, core], xsems, step - 1)
        send(xall_ref.at[origin, core], xall_ref.at[origin, core], xsems, rows - 2 + step, (r, twin))
    slot = shard(2, 0, 0)
    arrived(wall_ref.at[slot, :half], wsems, 2)
    arrived(wall_ref.at[slot, half:], wsems, 3)
    send(wall_ref.at[slot], wall_ref.at[slot], wsems, 6, (r, zside))
    send(wall_ref.at[slot], wall_ref.at[slot], wsems, 10, (r, twin))
    for offset in (0, 3, 1, 2):
        slot = shard(offset, 1, 0)
        arrived(wall_ref.at[slot], wsems, 4 + offset)
        send(wall_ref.at[slot], wall_ref.at[slot], wsems, 12 + offset, (r, twin))
    for plane in range(2):
        for offset in range(4):
            arrived(wall_ref.at[shard(offset, plane, 1)], wsems, 8 + 4 * plane + offset)
    for step in range(1, rows):
        origin = (r + rows - step) % rows
        arrived(xall_ref.at[origin, 1 - core], xsems, rows - 2 + step)
    for copy in started:
        copy.wait_send()
    own_w.wait()
    own_x.wait()


def gather_parts(x_factor, cycle_shard):
    rows = lax.axis_size("row")
    cols = lax.axis_size("col")
    any_spec = pl.BlockSpec(memory_space=pl.ANY)
    return pl.pallas_call(
        gather_kernel,
        out_shape=(
            jax.ShapeDtypeStruct((rows,) + x_factor.shape, x_factor.dtype),
            jax.ShapeDtypeStruct((cols,) + cycle_shard.shape, cycle_shard.dtype),
        ),
        in_specs=[any_spec, any_spec],
        out_specs=(any_spec, any_spec),
        scratch_shapes=[
            pltpu.SemaphoreType.DMA((16,)),
            pltpu.SemaphoreType.DMA((16,)),
            pltpu.SemaphoreType.DMA((2 * (rows - 1),)),
            pltpu.SemaphoreType.DMA((2 * (rows - 1),)),
            pltpu.SemaphoreType.DMA((2,)),
        ],
        compiler_params=pltpu.CompilerParams(collective_id=0, has_side_effects=True),
        name="gather_parts",
    )(x_factor, cycle_shard)


def dot(a, b):
    return jnp.dot(a, b, preferred_element_type=jnp.float32)


def dot_nt(a, b):
    return lax.dot_general(a, b, (((1,), (1,)), ((), ())), preferred_element_type=jnp.float32)


STRIP = 256


def strips(width):
    return [pl.ds(start, STRIP) for start in range(0, width, STRIP)]


def own_kernel(
    tiles_ref, wall_ref, amps_ref, x_ref, xt_ref, core_ref, pick_ref, pickt_ref,
    wd_ref, wdt_ref, wt_ref, cyc_ref, wsel, proj, sem,
):
    slots = tiles_ref.shape[0]
    tile = wall_ref.shape[2]
    width = x_ref.shape[0]
    copies = []
    for s in range(slots):
        copy = pltpu.make_async_copy(
            wall_ref.at[tiles_ref[s]], wsel.at[:, pl.ds(s * tile, tile), :], sem.at[s]
        )
        copy.start()
        copies.append(copy)

    def own_ladder(p, carry):
        for rows in strips(width):
            proj[rows, :] = dot(xt_ref[rows, :], amps_ref[p]).astype(proj.dtype)
            inner = dot(proj[rows, :], x_ref[...])
            wt_ref[p, rows, :] = (core_ref[rows, :].astype(jnp.float32) * inner).astype(wt_ref.dtype)
        return carry

    lax.fori_loop(0, 4, own_ladder, 0)
    for copy in copies:
        copy.wait()

    def pick(p, carry):
        for rows in strips(width):
            wd_ref[p, rows, :] = dot(wsel[p, rows, :], pick_ref[...]).astype(wd_ref.dtype)
        for rows in strips(width):
            wdt_ref[p, rows, :] = dot_nt(pickt_ref[rows, :], wsel[p]).astype(wdt_ref.dtype)
        return carry

    lax.fori_loop(0, 4, pick, 0)

    def own_cycle(p, carry):
        i, j = p // 2, p % 2
        for rows in strips(width):
            cyc_ref[p, rows, :] = dot(wd_ref[2 * i, rows, :], amps_ref[j]) + dot(
                wd_ref[2 * i + 1, rows, :], amps_ref[2 + j]
            )
        return carry

    lax.fori_loop(0, 4, own_cycle, 0)


def own_terms(tile_list, wall, amp4, x, xt, core, pick, pickt):
    width, points = x.shape
    vmem = pl.BlockSpec(memory_space=pltpu.VMEM)
    square = (4, width, width)
    return pl.pallas_call(
        own_kernel,
        out_shape=(
            jax.ShapeDtypeStruct(square, jnp.bfloat16),
            jax.ShapeDtypeStruct(square, jnp.bfloat16),
            jax.ShapeDtypeStruct((4, points, points), jnp.bfloat16),
            jax.ShapeDtypeStruct(square, jnp.float32),
        ),
        in_specs=[pl.BlockSpec(memory_space=pltpu.SMEM), pl.BlockSpec(memory_space=pl.ANY)] + [vmem] * 6,
        out_specs=(vmem,) * 4,
        scratch_shapes=[
            pltpu.VMEM((4, width, wall.shape[3]), jnp.bfloat16),
            pltpu.VMEM((points, width), jnp.bfloat16),
            pltpu.SemaphoreType.DMA((tile_list.shape[0],)),
        ],
        compiler_params=pltpu.CompilerParams(vmem_limit_bytes=VMEM_LIMIT),
        name="own_terms",
    )(tile_list, wall, amp4, x, xt, core, pick, pickt)


def finish_kernel(
    first, occ_ref, vcol_ref, vrow_ref, mcol_ref, mrow_ref, *refs,
):
    (b0_hbm, b1_hbm, xt_hbm, x_hbm, coret_hbm, wt_hbm, wdt_hbm, cyc_hbm, amps_hbm) = refs[:9]
    res_hbm, upd_hbm = refs[-18:-16]
    (b0, b1, xt, x, coret, wt, wdt, cyc, amps, proj, total, spread, res, upd, sem, osem) = refs[-16:]
    width = x.shape[0]
    pairs = pl.ds(2 * first, 2)
    plan = {
        "b0": (b0_hbm, b0), "xt": (xt_hbm, xt), "x": (x_hbm, x), "coret": (coret_hbm, coret),
        "wt": (wt_hbm.at[pairs], wt), "b1": (b1_hbm, b1), "wdt": (wdt_hbm, wdt),
        "cyc": (cyc_hbm.at[pairs], cyc), "amps": (amps_hbm.at[pairs], amps),
    }
    loads = {}
    for at, (name, (src, dst)) in enumerate(plan.items()):
        loads[name] = pltpu.make_async_copy(src, dst, sem.at[at])
        loads[name].start()

    def need(*names):
        for name in names:
            if name in loads:
                loads.pop(name).wait()

    outs = []
    for j, b in enumerate((b0, b1)):
        need("b0" if j == 0 else "b1", "xt", "x", "coret", "wt")
        for rows in strips(width):
            proj[rows, :] = dot(xt[rows, :], b[...]).astype(proj.dtype)
            inner = dot(proj[rows, :], x[...])
            total[rows, :] = (
                wt[j, rows, :].astype(jnp.float32) + coret[rows, :].astype(jnp.float32) * inner
            ).astype(total.dtype)
        need("b1", "wdt", "cyc", "amps")
        for at, rows in enumerate(strips(width)):
            spread[rows, :] = dot(x[rows, :], total[...]).astype(spread.dtype)
            raw = (
                dot(spread[rows, :], xt[...])
                + dot(b0[rows, :], wdt[2 * j])
                + dot(b1[rows, :], wdt[2 * j + 1])
                + cyc[j, rows, :]
            )
            live = (mcol_ref[rows, :] * mrow_ref[...]) > 0.0
            raw = jnp.where(live, raw, 0.0)
            own = jnp.where(live, amps[j, rows, :].astype(jnp.float32), 0.0)
            gap = (occ_ref[0, first] + occ_ref[1, j]) - vcol_ref[rows, :] - vrow_ref[...]
            res[j, rows, :] = raw
            upd[j, rows, :] = (own + raw / gap).astype(upd.dtype)
            pair = 2 * first + j
            for k, (src, dst) in enumerate(((res, res_hbm), (upd, upd_hbm))):
                copy = pltpu.make_async_copy(
                    src.at[j, rows, :], dst.at[pair, rows, :], osem.at[k, j, at]
                )
                copy.start()
                outs.append(copy)
    for copy in outs:
        copy.wait()


def finish(first, occ, vcol, vrow, mcol, mrow, b0, b1, xt, x, coret, wt, wdt, cyc, amp4, before):
    width, points = x.shape
    vmem = pl.BlockSpec(memory_space=pltpu.VMEM)
    hbm = pl.BlockSpec(memory_space=pl.ANY)
    square = (4, width, width)
    bf16 = jnp.bfloat16
    operands = [occ, vcol, vrow, mcol, mrow, b0, b1, xt, x, coret, wt, wdt, cyc, amp4]
    alias = {}
    if before is not None:
        alias = {len(operands): 0, len(operands) + 1: 1}
        operands += list(before)
    return pl.pallas_call(
        functools.partial(finish_kernel, first),
        out_shape=(
            jax.ShapeDtypeStruct(square, jnp.float32),
            jax.ShapeDtypeStruct(square, bf16),
        ),
        in_specs=[pl.BlockSpec(memory_space=pltpu.SMEM)] + [vmem] * 4 + [hbm] * (len(operands) - 5),
        out_specs=(hbm, hbm),
        scratch_shapes=[
            pltpu.VMEM((width, width), bf16),
            pltpu.VMEM((width, width), bf16),
            pltpu.VMEM((points, width), bf16),
            pltpu.VMEM((width, points), bf16),
            pltpu.VMEM((points, points), bf16),
            pltpu.VMEM((2, points, points), bf16),
            pltpu.VMEM((4, width, width), bf16),
            pltpu.VMEM((2, width, width), jnp.float32),
            pltpu.VMEM((2, width, width), bf16),
            pltpu.VMEM((points, width), bf16),
            pltpu.VMEM((points, points), bf16),
            pltpu.VMEM((width, points), bf16),
            pltpu.VMEM((2, width, width), jnp.float32),
            pltpu.VMEM((2, width, width), bf16),
            pltpu.SemaphoreType.DMA((9,)),
            pltpu.SemaphoreType.DMA((2, 2, width // STRIP)),
        ],
        input_output_aliases=alias,
        compiler_params=pltpu.CompilerParams(vmem_limit_bytes=VMEM_LIMIT),
        name="finish_%d" % first,
    )(*operands)


def per_device(
    amps, x_factor, core, cycle_w, domain_tiles, domain_count, tile_slot, occ_energy, virt_energy
):
    occ = amps.shape[2]
    width = amps.shape[4]
    slot_count = domain_tiles.shape[2]
    tile_width = x_factor.shape[1]
    grid_points = x_factor.shape[2]
    window = cycle_w.shape[4]
    cols = lax.axis_size("col")
    mirror = [(i, (i + cols // 2) % cols) for i in range(cols)]
    amp = amps[0, 0]
    amp4 = amp.reshape(occ * occ, width, width)

    turned = [[jnp.transpose(amp[j, i]) for j in range(occ)] for i in range(occ)]
    pieces = [[lax.ppermute(turned[i][j], "col", mirror) for j in range(occ)] for i in range(occ)]

    shard = cycle_w[0].reshape(occ * occ, tile_width, window)
    shard, _ = lax.optimization_barrier((shard, turned))
    xall, wall = gather_parts(x_factor, shard)
    xall = xall.reshape(-1, tile_width, grid_points)

    tile_list = domain_tiles[0, 0]
    live_slots = jnp.arange(slot_count, dtype=jnp.int32) < domain_count[0, 0]
    row_live = jnp.repeat(live_slots, tile_width)
    window_index = (
        tile_list[:, None] * tile_width + jnp.arange(tile_width, dtype=jnp.int32)[None, :]
    ).reshape(width)
    picked = jnp.where(row_live, window_index, -1)
    window_at = jnp.arange(window, dtype=jnp.int32)
    pick = (window_at[:, None] == picked[None, :]).astype(jnp.bfloat16)
    pickt = (picked[:, None] == window_at[None, :]).astype(jnp.bfloat16)
    virt_levels = virt_energy[window_index]
    mask = row_live.astype(jnp.float32)

    x = xall[tile_slot[tile_list]].reshape(width, grid_points)
    x = jnp.where(row_live[:, None], x, jnp.zeros_like(x))
    xt = jnp.transpose(x)
    coret = jnp.transpose(core)

    wd, wdt, wt, cyc = own_terms(tile_list, wall, amp4, x, xt, core, pick, pickt)
    out = None
    for i in range(occ):
        out = finish(
            i, occ_energy[0, 0], virt_levels[:, None], virt_levels[None, :], mask[:, None], mask[None, :],
            pieces[i][0], pieces[i][1], xt, x, coret, wt, wdt, cyc, amp4, out,
        )
    residual, updated = out
    return residual.reshape(amps.shape), updated.reshape(amps.shape)


def solution(mesh):
    in_specs = (
        P("row", "col", None, None, None, None),
        P("row", None, None),
        P(),
        P("row", None, None, "col", None),
        P("row", "col", None),
        P("row", "col"),
        P(),
        P("row", "col", None, None),
        P(),
    )
    out_specs = (P("row", "col", None, None, None, None), P("row", "col", None, None, None, None))
    return jax.shard_map(
        per_device, mesh=mesh, in_specs=in_specs, out_specs=out_specs, check_vma=False
    )
```

profile of v0, /device:TPU:6, one launch (start us, length us, event | category | flops | bytes accessed | tf_op | source)
XLA Modules:
  0.0 247.0 jit_solution(10240478029301565372)
XLA Ops:
  0.6 0.0 copy-start
  0.6 6.6 %copy.18 = bf16[1,1,2,2,768,768]{4,5,3,2,1,0:T(8,128)(2,1)} copy(bf16[1,1,2,2,768,768]{5,4,3,2,1,0:T(8,128)(2,1)} %param.9) | data formatting | bytes 9437184 | tf_op args[0]
  7.3 0.0 copy-start.5
  7.3 0.0 copy-start.2
  7.3 4.2 %slice_bitcast_fusion = (bf16[768,768]{1,0:T(8,128)(2,1)}, bf16[768,768]{1,0:T(8,128)(2,1)}, bf16[768,768]{1,0:T(8,128)(2,1)}, bf16[768,768]{1,0:T(8,128)(2,1)S(1)}) fusion(bf16[2,2,768,768]{2,3,1,0:T(8,128)(2,1)} %bitcast.43), kind=kLoop, calls=%fused_computation.7 | loop fusion | bytes 9437184 | tf_op jit(solution)/shard_map/transpose | solution.py:329
  11.5 1.4 collective-permute-start.3
  12.9 2.1 collective-permute-start.2
  15.0 1.4 collective-permute-start.1
  16.4 2.1 collective-permute-start
  18.6 0.0 copy-done.5
  19.2 0.0 copy-done.2
  19.2 0.7 gather_fusion.1
  19.9 0.1 iota_add_fusion
  20.0 0.1 add.70
  20.1 0.1 add.75
  20.2 0.1 broadcast_in_dim.44
  20.3 0.7 convert_element_type.33.mrow_ref
  20.9 1.1 convert_element_type.36.mcol_ref
  22.0 0.0 copy-done
  22.0 0.0 copy-start.4
  22.0 3.2 %gather_fusion = f32[768]{0:T(1024)S(1)} fusion(f32[1024]{0:T(1024)S(1)} %copy-done, s32[1024]{0:T(1024)S(1)} %pad_clamp_fusion.2), kind=kCustom, calls=%fused_computation | custom fusion | bytes 9216 | tf_op jit(solution)/shard_map/gather | solution.py:347
  25.2 0.6 broadcast_in_dim.25.vrow_ref
  25.8 0.9 broadcast_in_dim.50.vcol_ref
  26.7 0.1 broadcast_in_dim.45
  26.8 0.1 broadcast_in_dim.46
  26.9 0.0 copy-done.4
  26.9 1.5 copy.19
  28.3 135.8 %gather_parts.1 = (bf16[8,2,64,768]{3,2,1,0:T(8,128)(2,1)}, bf16[16,4,64,1024]{3,2,1,0:T(8,128)(2,1)}) custom-call(bf16[2,64,768]{2,1,0:T(8,128)(2,1)} %x_ref.1, bf16[4,64,1024]{2,1,0:T(8,128)(2,1)} %bitcast.49), custom_call_target="tpu_custom_call" | custom-call | tf_op jit(solution)/shard_map/gather_parts/pallas_call | solution.py:109
  164.2 2.0 gather_fusion.2
  166.2 0.2 bitcast_select_fusion.x_ref.refs_3_
  166.5 0.0 copy-start.3
  166.5 1.4 copy.26.xt_ref.refs_2_
  167.9 0.0 copy-done.3
  167.9 1.5 fusion.1.pickt_ref
  169.4 1.8 fusion.pick_ref
  171.2 37.7 %own_terms.1 = (bf16[4,768,768]{2,1,0:T(8,128)(2,1)}, bf16[4,768,768]{2,1,0:T(8,128)(2,1)}, bf16[4,768,768]{2,1,0:T(8,128)(2,1)}, f32[4,768,768]{2,1,0:T(8,128)}) custom-call(s32[12]{0:T(128)} %bitcast.52, bf16[16,4,64,1024]{3,2,1,0:T(8,128)(2,1)} %get-tuple-element.14.wall_ref, bf16[4,768,768]{2,1,0:T(8,128)(2,1)} %bitcast.39, bf16[768,768]{1,0:T(8,128)(2,1)} %copy-done.3, ...), custom_call_target="tpu_custom_call" | custom-call | tf_op jit(solution)/shard_map/own_terms/pallas_call | solution.py:194
  208.9 0.0 collective-permute-done.3.refs_1_
  208.9 0.0 collective-permute-done.2.refs_0_
  208.9 18.9 %finish_0.1 = (f32[4,768,768]{2,1,0:T(8,128)}, bf16[4,768,768]{2,1,0:T(8,128)(2,1)}) custom-call(f32[2,2]{1,0:T(2,128)} %bitcast.50, f32[768,1]{1,0:T(8,128)} %broadcast_in_dim.50.vcol_ref, f32[1,768]{1,0:T(1,128)} %broadcast_in_dim.25.vrow_ref, f32[768,1]{1,0:T(8,128)} %convert_element_type.36.mcol_ref, f32[1,768]{1,0:T(1,128)} %convert_element_type.33.mrow_ref, ...), custom_call_target="tpu_custom_call" | custom-call | tf_op jit(solution)/shard_map/finish_0/pallas_call | solution.py:283
  227.8 0.0 collective-permute-done.1.refs_1_
  227.8 0.0 collective-permute-done.refs_0_
  227.8 0.0 copy-start.1
  227.8 19.0 %finish_1.1 = (f32[4,768,768]{2,1,0:T(8,128)}, bf16[4,768,768]{2,1,0:T(8,128)(2,1)}) custom-call(f32[2,2]{1,0:T(2,128)} %bitcast.51, f32[768,1]{1,0:T(8,128)} %broadcast_in_dim.50.vcol_ref, f32[1,768]{1,0:T(1,128)} %broadcast_in_dim.25.vrow_ref, f32[768,1]{1,0:T(8,128)} %convert_element_type.36.mcol_ref, ...), custom_call_target="tpu_custom_call", output_to_operand_aliasing={{0}: (14, {}), {1}: (15, {})} | custom-call | tf_op jit(solution)/shard_map/finish_1/pallas_call | solution.py:283
  246.9 0.0 copy-done.1
  (9 shorter events, 0.1 us)
Async XLA Ops:
  0.6 21.4 %copy-start = (f32[1024]{0:T(1024)S(1)}, f32[1024]{0:T(1024)}, u32[]{:S(2)}) copy-start(f32[1024]{0:T(1024)} %param.17) | copy-start | bytes 12292
  7.3 11.3 %copy-start.5 = (s32[1,1,12]{2,1,0:T(1,128)S(1)}, s32[1,1,12]{2,1,0:T(1,128)}, u32[]{:S(2)}) copy-start(s32[1,1,12]{2,1,0:T(1,128)} %param.13) | copy-start | bytes 148
  7.3 12.0 %copy-start.2 = (s32[16]{0:T(128)S(1)}, s32[16]{0:T(128)}, u32[]{:S(2)}) copy-start(s32[16]{0:T(128)} %param.15) | copy-start | bytes 196
  11.5 197.4 %collective-permute-start.3 = (bf16[768,768]{1,0:T(8,128)(2,1)}, bf16[768,768]{1,0:T(8,128)(2,1)}, u32[]{:S(2)}, u32[]{:S(2)}) collective-permute-start(bf16[768,768]{1,0:T(8,128)(2,1)} %get-tuple-element.22), channel_id=1, source_target_pairs={{0,8},{1,9},{2,10},{3,11},{4,12},{5,13},{6,14},{7,15},{8,0},{9,1},... | collective-permute-start | bytes 3538952 | tf_op jit(solution)/shard_map/ppermute | solution.py:330
  12.9 196.0 %collective-permute-start.2 = (bf16[768,768]{1,0:T(8,128)(2,1)}, bf16[768,768]{1,0:T(8,128)(2,1)}, u32[]{:S(2)}, u32[]{:S(2)}) collective-permute-start(bf16[768,768]{1,0:T(8,128)(2,1)} %get-tuple-element.23), channel_id=1, source_target_pairs={{0,8},{1,9},{2,10},{3,11},{4,12},{5,13},{6,14},{7,15},{8,0},{9,1},... | collective-permute-start | bytes 3538952 | tf_op jit(solution)/shard_map/ppermute | solution.py:330
  15.0 212.8 %collective-permute-start.1 = (bf16[768,768]{1,0:T(8,128)(2,1)}, bf16[768,768]{1,0:T(8,128)(2,1)}, u32[]{:S(2)}, u32[]{:S(2)}) collective-permute-start(bf16[768,768]{1,0:T(8,128)(2,1)} %get-tuple-element.24), channel_id=1, source_target_pairs={{0,8},{1,9},{2,10},{3,11},{4,12},{5,13},{6,14},{7,15},{8,0},{9,1},... | collective-permute-start | bytes 3538952 | tf_op jit(solution)/shard_map/ppermute | solution.py:330
  16.4 211.4 %collective-permute-start = (bf16[768,768]{1,0:T(8,128)(2,1)S(1)}, bf16[768,768]{1,0:T(8,128)(2,1)}, u32[]{:S(2)}, u32[]{:S(2)}) collective-permute-start(bf16[768,768]{1,0:T(8,128)(2,1)S(1)} %get-tuple-element.25), channel_id=1, source_target_pairs={{0,8},{1,9},{2,10},{3,11},{4,12},{5,13},{6,14},{7,15},{8,0},{9,1},... | collective-permute-start | bytes 3538952 | tf_op jit(solution)/shard_map/ppermute | solution.py:330
  22.0 4.9 %copy-start.4 = (bf16[768,768]{1,0:T(8,128)(2,1)S(1)}, bf16[768,768]{1,0:T(8,128)(2,1)}, u32[]{:S(2)}) copy-start(bf16[768,768]{1,0:T(8,128)(2,1)} %core_ref.1) | copy-start | bytes 3538948
  166.5 1.4 copy-start.3
  227.8 19.0 %copy-start.1 = (f32[1024]{0:T(1024)S(1)}, f32[1024]{0:T(1024)}, u32[]{:S(2)}) copy-start(f32[1024]{0:T(1024)} %param.17) | copy-start | bytes 12292
where the time goes:
time: 252 us; the launch traced here: 247 us
  Pallas kernels  211 us (84%)
  local copies, waits for them, and re-layouts  23.3 us (9%)
  starting transfers between devices  7.06 us (3%)
  other arithmetic  3.61 us (1%)
    pallas_call x1, Pallas kernels, gather_parts(): pl.pallas_call(gather_kernel, out_shape=(jax.ShapeDtypeStruct((rows,) + x...  136 us
    pallas_call x2, Pallas kernels, finish(): pl.pallas_call(functools.partial(finish_kernel, first), out_shape=(jax.Sh...  37.9 us
    pallas_call x1, Pallas kernels, own_terms(): pl.pallas_call(own_kernel, out_shape=(jax.ShapeDtypeStruct(square, jnp.bf...  37.7 us
    unnamed x14, local copies, waits for them, and re-layouts  8.11 us
    ppermute x4, starting transfers between devices, per_device(): lax.ppermute(turned[i][j], 'col', mirror)  7.06 us
  transfers between devices with their start and end apart: 4, of which 0 were waited for; matrix products, arithmetic and copies ran while one was open for 6% of the time, Pallas kernels for 78%

commit v1 on v0

v1 whole, which is shorter than its diff:
```python
import functools

import jax
import jax.numpy as jnp
from jax import lax
from jax.experimental import pallas as pl
from jax.experimental.pallas import tpu as pltpu
from jax.sharding import PartitionSpec as P

MESH = pl.DeviceIdType.MESH
VMEM_LIMIT = 56 * 1024 * 1024
STRIP = 384


def dot(a, b):
    return jnp.dot(a, b, preferred_element_type=jnp.float32)


def dot_nt(a, b):
    return lax.dot_general(a, b, (((1,), (1,)), ((), ())), preferred_element_type=jnp.float32)


def strips(width, step):
    return [pl.ds(start, step) for start in range(0, width, step)]


def gather_kernel(
    x_ref, w_ref, amps_ref, xall_ref, wall_ref, far_ref, turned0_ref, turned1_ref, turned2_ref, turned3_ref,
    plain, turn, wsend, wrecv, xsend, xrecv, local, tsem,
):
    r = lax.axis_index("row")
    c = lax.axis_index("col")
    rows = lax.axis_size("row")
    cols = lax.axis_size("col")
    forth = (c + 4) % cols
    back = (c + cols - 4) % cols
    zside = c + 2 - 4 * ((c // 2) % 2)
    twin = c + 1 - 2 * (c % 2)
    core = c % 2
    half = w_ref.shape[0] // 2

    amps_in = pltpu.make_async_copy(amps_ref, plain, local.at[2])
    amps_in.start()

    barrier = pltpu.get_barrier_semaphore()
    for other in (forth, back, zside, twin):
        pl.semaphore_signal(barrier, inc=1, device_id=(r, other), device_id_type=MESH)
    for step in range(1, rows):
        pl.semaphore_signal(barrier, inc=1, device_id=((r + step) % rows, c), device_id_type=MESH)
    pl.semaphore_wait(barrier, 4 + rows - 1)

    started = []
    wsems = (wsend, wrecv)
    xsems = (xsend, xrecv)

    def send(src, dst, sems, index, device):
        copy = pltpu.make_async_remote_copy(
            src_ref=src, dst_ref=dst, send_sem=sems[0].at[index], recv_sem=sems[1].at[index],
            device_id=device, device_id_type=MESH,
        )
        copy.start()
        started.append(copy)

    def arrived(dst, sems, index):
        pltpu.make_async_remote_copy(
            src_ref=dst, dst_ref=dst, send_sem=sems[0].at[index], recv_sem=sems[1].at[index],
            device_id=(r, twin), device_id_type=MESH,
        ).wait_recv()

    def shard(offset, plane, side):
        x = (c // 4 + offset) % (cols // 4)
        z = (c // 2) % 2
        z = z + plane * (1 - 2 * z)
        k = core + side * (1 - 2 * core)
        return x * 4 + z * 2 + k

    send(w_ref, wall_ref.at[c], wsems, 0, (r, forth))
    send(w_ref, far_ref.at[0], wsems, 1, (r, back))
    send(w_ref, wall_ref.at[c], wsems, 4, (r, zside))
    for step in range(1, rows):
        send(x_ref.at[core], xall_ref.at[r, core], xsems, step - 1, ((r + step) % rows, c))
    send(w_ref, wall_ref.at[c], wsems, 6, (r, twin))
    own_w = pltpu.make_async_copy(w_ref, wall_ref.at[c], local.at[0])
    own_x = pltpu.make_async_copy(x_ref, xall_ref.at[r], local.at[1])
    own_w.start()
    own_x.start()

    turned_refs = (turned0_ref, turned1_ref, turned2_ref, turned3_ref)
    amps_in.wait()
    turned_out = []
    for p, q in enumerate((0, 2, 1, 3)):
        for cut in strips(turn.shape[1], 256):
            turn[p, :, cut] = plain[q, cut, :].T
        copy = pltpu.make_async_copy(turn.at[p], turned_refs[p], tsem.at[p])
        copy.start()
        turned_out.append(copy)

    slot = shard(3, 0, 0)
    arrived(wall_ref.at[slot], wsems, 0)
    send(wall_ref.at[slot, :half], far_ref.at[1, :half], wsems, 2, (r, forth))
    send(wall_ref.at[slot], wall_ref.at[slot], wsems, 5, (r, zside))
    send(wall_ref.at[slot], wall_ref.at[slot], wsems, 7, (r, twin))
    arrived(far_ref.at[0], wsems, 1)
    send(far_ref.at[0, half:], far_ref.at[1, half:], wsems, 3, (r, back))
    slot = shard(1, 0, 0)
    send(far_ref.at[0], wall_ref.at[slot], wsems, 8, (r, twin))
    slot = shard(0, 1, 0)
    arrived(wall_ref.at[slot], wsems, 4)
    send(wall_ref.at[slot], wall_ref.at[slot], wsems, 9, (r, twin))
    for step in range(1, rows):
        origin = (r + rows - step) % rows
        arrived(xall_ref.at[origin, core], xsems, step - 1)
        send(xall_ref.at[origin, core], xall_ref.at[origin, core], xsems, rows - 2 + step, (r, twin))
    arrived(far_ref.at[1, :half], wsems, 2)
    arrived(far_ref.at[1, half:], wsems, 3)
    slot = shard(2, 0, 0)
    send(far_ref.at[1], wall_ref.at[slot], wsems, 10, (r, twin))
    slot = shard(3, 1, 0)
    arrived(wall_ref.at[slot], wsems, 5)
    send(wall_ref.at[slot], wall_ref.at[slot], wsems, 11, (r, twin))
    for step in range(1, rows):
        origin = (r + rows - step) % rows
        arrived(xall_ref.at[origin, 1 - core], xsems, rows - 2 + step)
    arrived(wall_ref.at[shard(0, 0, 1)], wsems, 6)
    arrived(wall_ref.at[shard(3, 0, 1)], wsems, 7)
    arrived(wall_ref.at[shard(1, 0, 1)], wsems, 8)
    arrived(wall_ref.at[shard(0, 1, 1)], wsems, 9)
    arrived(wall_ref.at[shard(2, 0, 1)], wsems, 10)
    arrived(wall_ref.at[shard(3, 1, 1)], wsems, 11)
    for copy in started:
        copy.wait_send()
    own_w.wait()
    own_x.wait()
    for copy in turned_out:
        copy.wait()


def gather_parts(x_factor, cycle_shard, amp4):
    rows = lax.axis_size("row")
    cols = lax.axis_size("col")
    hbm = pl.BlockSpec(memory_space=pl.ANY)
    bf16 = jnp.bfloat16
    return pl.pallas_call(
        gather_kernel,
        out_shape=(
            jax.ShapeDtypeStruct((rows,) + x_factor.shape, bf16),
            jax.ShapeDtypeStruct((cols,) + cycle_shard.shape, bf16),
            jax.ShapeDtypeStruct((2,) + cycle_shard.shape, bf16),
        ) + (jax.ShapeDtypeStruct(amp4.shape[1:], bf16),) * 4,
        in_specs=[hbm] * 3,
        out_specs=(hbm,) * 7,
        scratch_shapes=[
            pltpu.VMEM(amp4.shape, bf16),
            pltpu.VMEM(amp4.shape, bf16),
            pltpu.SemaphoreType.DMA((12,)),
            pltpu.SemaphoreType.DMA((12,)),
            pltpu.SemaphoreType.DMA((2 * (rows - 1),)),
            pltpu.SemaphoreType.DMA((2 * (rows - 1),)),
            pltpu.SemaphoreType.DMA((3,)),
            pltpu.SemaphoreType.DMA((4,)),
        ],
        compiler_params=pltpu.CompilerParams(
            collective_id=0, has_side_effects=True, vmem_limit_bytes=VMEM_LIMIT
        ),
        name="gather_parts",
    )(x_factor, cycle_shard, amp4)


def own_ladder_kernel(
    slots_ref, mask_ref, xall_ref, amps_ref, core_ref, x_ref, xt_ref, wt_ref, gathered, proj, sem
):
    tile = xall_ref.shape[1]
    copies = []
    for s in range(slots_ref.shape[0]):
        copy = pltpu.make_async_copy(
            xall_ref.at[slots_ref[s]], gathered.at[pl.ds(s * tile, tile), :], sem.at[s]
        )
        copy.start()
        copies.append(copy)
    for copy in copies:
        copy.wait()
    x_ref[...] = jnp.where(mask_ref[...] > 0.0, gathered[...].astype(jnp.float32), 0.0).astype(x_ref.dtype)
    for cut in strips(x_ref.shape[0], 256):
        xt_ref[:, cut] = x_ref[cut, :].T

    def one(p, carry):
        proj[...] = dot(xt_ref[...], amps_ref[p]).astype(proj.dtype)
        inner = dot(proj[...], x_ref[...])
        wt_ref[p] = (core_ref[...].astype(jnp.float32) * inner).astype(wt_ref.dtype)
        return carry

    lax.fori_loop(0, 4, one, 0)


def own_ladder(slots, mcol, xall, amp4, core):
    width = amp4.shape[1]
    points = core.shape[0]
    vmem = pl.BlockSpec(memory_space=pltpu.VMEM)
    smem = pl.BlockSpec(memory_space=pltpu.SMEM)
    bf16 = jnp.bfloat16
    return pl.pallas_call(
        own_ladder_kernel,
        out_shape=(
            jax.ShapeDtypeStruct((width, points), bf16),
            jax.ShapeDtypeStruct((points, width), bf16),
            jax.ShapeDtypeStruct((4, points, points), bf16),
        ),
        in_specs=[smem, vmem, pl.BlockSpec(memory_space=pl.ANY), vmem, vmem],
        out_specs=(vmem,) * 3,
        scratch_shapes=[
            pltpu.VMEM((width, points), bf16),
            pltpu.VMEM((points, width), bf16),
            pltpu.SemaphoreType.DMA((slots.shape[0],)),
        ],
        compiler_params=pltpu.CompilerParams(vmem_limit_bytes=VMEM_LIMIT),
        name="own_ladder",
    )(slots, mcol, xall, amp4, core)


def own_cycle_kernel(
    kind_ref, at_ref, picked_ref, wall_ref, far_ref, side_ref, twin_ref, amps_ref,
    wd_ref, cyc_ref, wsel, pick, sem,
):
    tile = wall_ref.shape[2]
    slots = kind_ref.shape[0]
    for s in range(slots):
        for kind, source in enumerate((wall_ref, far_ref, side_ref, twin_ref)):

            @pl.when(kind_ref[s] == kind)
            def _(s=s, source=source):
                pltpu.make_async_copy(
                    source.at[at_ref[s]], wsel.at[:, pl.ds(s * tile, tile), :], sem.at[s]
                ).start()

    window = lax.broadcasted_iota(jnp.int32, pick.shape, 0)
    pick[...] = jnp.where(window == picked_ref[...], 1.0, 0.0).astype(pick.dtype)
    for s in range(slots):
        pltpu.make_async_copy(
            wall_ref.at[0], wsel.at[:, pl.ds(s * tile, tile), :], sem.at[s]
        ).wait()

    def select(p, carry):
        wd_ref[p] = dot(wsel[p], pick[...]).astype(wd_ref.dtype)
        return carry

    lax.fori_loop(0, 4, select, 0)

    def one(p, carry):
        i, j = p // 2, p % 2
        cyc_ref[p] = dot(wd_ref[2 * i], amps_ref[j]) + dot(wd_ref[2 * i + 1], amps_ref[2 + j])
        return carry

    lax.fori_loop(0, 4, one, 0)


def own_cycle(kind, at, picked, wall, far, side, twin, amp4):
    width = amp4.shape[1]
    slots, window = kind.shape[0], wall.shape[3]
    vmem = pl.BlockSpec(memory_space=pltpu.VMEM)
    smem = pl.BlockSpec(memory_space=pltpu.SMEM)
    hbm = pl.BlockSpec(memory_space=pl.ANY)
    return pl.pallas_call(
        own_cycle_kernel,
        out_shape=(
            jax.ShapeDtypeStruct((4, width, width), jnp.bfloat16),
            jax.ShapeDtypeStruct((4, width, width), jnp.float32),
        ),
        in_specs=[smem, smem, vmem, hbm, hbm, hbm, hbm, vmem],
        out_specs=(vmem,) * 2,
        scratch_shapes=[
            pltpu.VMEM((4, width, window), jnp.bfloat16),
            pltpu.VMEM((window, width), jnp.bfloat16),
            pltpu.SemaphoreType.DMA((slots,)),
        ],
        compiler_params=pltpu.CompilerParams(vmem_limit_bytes=VMEM_LIMIT),
        name="own_cycle",
    )(kind, at, picked, wall, far, side, twin, amp4)


def piece_kernel(i, k, last, occ_ref, vcol_ref, vrow_ref, mcol_ref, mrow_ref, *refs):
    (b_hbm, xt_hbm, x_hbm, coret_hbm, wt_hbm, wd_hbm, amps_hbm, part_hbm) = refs[:8]
    (xt, coret, wt, right, left, part, amps, proj, total, upd, sem, osem) = refs[-12:]
    outs_at = refs[8:-12]
    res_hbm = outs_at[-2] if last else outs_at[-1]
    upd_hbm = outs_at[-1] if last else None
    width, points = x_hbm.shape
    head, rest = pl.ds(0, points), pl.ds(points, width)
    plan = {
        "b": (b_hbm, left.at[:, rest]),
        "xt": (xt_hbm, xt),
        "x": (x_hbm, right.at[k, :, head]),
        "coret": (coret_hbm, coret),
        "wt": (wt_hbm.at[2 * i + k], wt),
        "w0": (wd_hbm.at[k], right.at[0, :, rest]),
        "w1": (wd_hbm.at[2 + k], right.at[1, :, rest]),
        "part": (part_hbm.at[pl.ds(2 * i, 2)], part),
    }
    if last:
        plan["amps"] = (amps_hbm.at[pl.ds(2 * i, 2)], amps)
    loads = {}
    for at, (name, (src, dst)) in enumerate(plan.items()):
        loads[name] = pltpu.make_async_copy(src, dst, sem.at[at])
        loads[name].start()

    outs = []

    def put(src, dst, at):
        copy = pltpu.make_async_copy(src, dst, osem.at[at])
        copy.start()
        outs.append(copy)

    def emit(j, rows, at, raw):
        raw = raw + part[j, rows, :]
        pair = 2 * i + j
        if last:
            live = (mcol_ref[rows, :] * mrow_ref[...]) > 0.0
            raw = jnp.where(live, raw, 0.0)
            own = jnp.where(live, amps[j, rows, :].astype(jnp.float32), 0.0)
            gap = (occ_ref[0, i] + occ_ref[1, j]) - vcol_ref[rows, :] - vrow_ref[...]
            upd[j, rows, :] = (own + raw / gap).astype(upd.dtype)
            put(upd.at[j, rows, :], upd_hbm.at[pair, rows, :], 4 + 2 * j + at)
        part[j, rows, :] = raw
        put(part.at[j, rows, :], res_hbm.at[pair, rows, :], 2 * j + at)

    loads["b"].wait()
    loads["xt"].wait()
    proj[...] = dot(xt[...], left[:, rest]).astype(proj.dtype)
    loads["x"].wait()
    loads["coret"].wait()
    loads["wt"].wait()
    inner = dot(proj[...], right[k, :, head])
    total[...] = (wt[...].astype(jnp.float32) + coret[...].astype(jnp.float32) * inner).astype(total.dtype)
    for name in ("w0", "w1", "part", "amps"):
        if name in loads:
            loads[name].wait()
    other = 1 - k
    for at, rows in enumerate(strips(width, STRIP)):
        emit(other, rows, at, dot_nt(left[rows, rest], right[other, :, rest]))
    left[:, head] = dot(right[k, :, head], total[...]).astype(left.dtype)
    for at, rows in enumerate(strips(width, STRIP)):
        emit(k, rows, at, dot_nt(left[rows, :], right[k]))
    for copy in outs:
        copy.wait()


def piece(i, k, occ, vcol, vrow, mcol, mrow, b, xt, x, coret, wt, wd, amp4, part, updated):
    width, points = x.shape
    last = k == 1
    vmem = pl.BlockSpec(memory_space=pltpu.VMEM)
    hbm = pl.BlockSpec(memory_space=pl.ANY)
    f32, bf16 = jnp.float32, jnp.bfloat16
    operands = [occ, vcol, vrow, mcol, mrow, b, xt, x, coret, wt, wd, amp4, part]
    out_shape = [jax.ShapeDtypeStruct(part.shape, f32)]
    alias = {len(operands) - 1: 0}
    if last:
        out_shape.append(jax.ShapeDtypeStruct(part.shape, bf16))
        if updated is not None:
            alias[len(operands)] = 1
            operands.append(updated)
    return pl.pallas_call(
        functools.partial(piece_kernel, i, k, last),
        out_shape=out_shape,
        in_specs=[pl.BlockSpec(memory_space=pltpu.SMEM)] + [vmem] * 4 + [hbm] * (len(operands) - 5),
        out_specs=[hbm] * len(out_shape),
        scratch_shapes=[
            pltpu.VMEM((points, width), bf16),
            pltpu.VMEM((points, points), bf16),
            pltpu.VMEM((points, points), bf16),
            pltpu.VMEM((2, width, points + width), bf16),
            pltpu.VMEM((width, points + width), bf16),
            pltpu.VMEM((2, width, width), f32),
            pltpu.VMEM((2, width, width), bf16),
            pltpu.VMEM((points, width), bf16),
            pltpu.VMEM((points, points), bf16),
            pltpu.VMEM((2, width, width), bf16),
            pltpu.SemaphoreType.DMA((9,)),
            pltpu.SemaphoreType.DMA((8,)),
        ],
        input_output_aliases=alias,
        compiler_params=pltpu.CompilerParams(vmem_limit_bytes=VMEM_LIMIT),
        name="piece_%d%d" % (i, k),
    )(*operands)


def per_device(
    amps, x_factor, core, cycle_w, domain_tiles, domain_count, tile_slot, occ_energy, virt_energy
):
    occ = amps.shape[2]
    width = amps.shape[4]
    slot_count = domain_tiles.shape[2]
    tile_width = x_factor.shape[1]
    grid_points = x_factor.shape[2]
    window = cycle_w.shape[4]
    cols = lax.axis_size("col")
    amp4 = amps[0, 0].reshape(occ * occ, width, width)
    shard = cycle_w[0].reshape(occ * occ, tile_width, window)
    xall, wall, far, *turned = gather_parts(x_factor, shard, amp4)
    xall = xall.reshape(-1, tile_width, grid_points)

    side = lax.ppermute(far, "col", [(i, i ^ 2) for i in range(cols)])
    mirror = [(i, (i + cols // 2) % cols) for i in range(cols)]
    pieces = [lax.ppermute(turned[p], "col", mirror) for p in range(occ * occ)]

    tile_list, count, tile_slot, virt_energy, core, _ = lax.optimization_barrier(
        (domain_tiles[0, 0], domain_count[0, 0], tile_slot, virt_energy, core, turned)
    )
    live_slots = jnp.arange(slot_count, dtype=jnp.int32) < count
    row_live = jnp.repeat(live_slots, tile_width)
    window_index = (
        tile_list[:, None] * tile_width + jnp.arange(tile_width, dtype=jnp.int32)[None, :]
    ).reshape(width)
    picked = jnp.where(row_live, window_index, -1)[None, :]
    virt_levels = virt_energy[window_index]
    mask = row_live.astype(jnp.float32)
    vcol, vrow, mcol, mrow = virt_levels[:, None], virt_levels[None, :], mask[:, None], mask[None, :]
    coret = jnp.transpose(core)

    me = lax.axis_index("col")
    offset = (tile_list // 4 + cols // 4 - me // 4) % (cols // 4)
    same_plane = (tile_list // 2) % 2 == (me // 2) % 2
    same_core = tile_list % 2 == me % 2
    apart = (offset == 1) | (offset == 2)
    kind = jnp.where(
        apart & same_core,
        jnp.where(same_plane, 1, 2),
        jnp.where(apart & ~same_plane, 3, 0),
    ).astype(jnp.int32)
    at = jnp.where(kind == 0, tile_list, offset - 1).astype(jnp.int32)

    x, xt, wt = own_ladder(tile_slot[tile_list], mcol, xall, amp4, core)
    side, wt = lax.optimization_barrier((side, wt))
    twin = lax.ppermute(side, "col", [(i, i ^ 1) for i in range(cols)])
    wd, part = own_cycle(kind, at, picked, wall, far, side, twin, amp4)
    updated = None
    for i in range(occ):
        for k in range(occ):
            out = piece(
                i, k, occ_energy[0, 0], vcol, vrow, mcol, mrow,
                pieces[occ * i + k], xt, x, coret, wt, wd, amp4, part, updated,
            )
            part = out[0]
        updated = out[1]
    return part.reshape(amps.shape), updated.reshape(amps.shape)


def solution(mesh):
    in_specs = (
        P("row", "col", None, None, None, None),
        P("row", None, None),
        P(),
        P("row", None, None, "col", None),
        P("row", "col", None),
        P("row", "col"),
        P(),
        P("row", "col", None, None),
        P(),
    )
    out_specs = (P("row", "col", None, None, None, None), P("row", "col", None, None, None, None))
    return jax.shard_map(
        per_device, mesh=mesh, in_specs=in_specs, out_specs=out_specs, check_vma=False
    )
```

time: 252 us -> 163 us (0.65); the launches traced: 247 us -> 163 us
  Pallas kernels: 211 us -> 127 us
  waiting for transfers between devices: 0.01 us -> 12.2 us
  local copies, waits for them, and re-layouts: 23.3 us -> 12.3 us
    pallas_call x1, Pallas kernels: 136 us -> 41.8 us  [gather_parts(): pl.pallas_call(gather_kernel, out_shape=(jax.ShapeDtypeStruct((rows,) + x...]
    ppermute x4 -> x6, waiting for transfers between devices: 0.01 us -> 12.2 us  [the longest x4 12.2 us: per_device(): pieces = [lax.ppermute(turned[p], 'col', mirror) for p in range(occ * occ)]]
    pallas_call x3 -> x6, Pallas kernels: 75.6 us -> 85.3 us  [the longest x4 47.1 us: piece(): pl.pallas_call(functools.partial(piece_kernel, i, k, last), out_shape=out...]
    unnamed x14 -> x12, local copies, waits for them, and re-layouts: 8.11 us -> 2.09 us
    transpose x2 -> x0, local copies, waits for them, and re-layouts: 5.66 us -> none  [the longest x1 4.23 us: per_device(): jnp.transpose(amp[j, i])]
    convert_element_type x2 -> x0, other arithmetic: 3.25 us -> none  [the longest x1 1.77 us: per_device(): pick = (window_at[:, None] == picked[None, :]).astype(jnp.bfloat16)]
    ppermute x4 -> x6, starting transfers between devices: 7.06 us -> 8.23 us  [the longest x4 7.06 us: per_device(): pieces = [lax.ppermute(turned[p], 'col', mirror) for p in range(occ * occ)]]
  transfers between devices with their start and end apart: 4 -> 6, of which waited for: 0 -> 1; matrix products, arithmetic and copies ran while one was open for 6% -> 7% of each run, Pallas kernels for 78% -> 45%
where the time goes in v1:
time: 163 us
  Pallas kernels  127 us (78%)
  local copies, waits for them, and re-layouts  12.3 us (8%)
  waiting for transfers between devices  12.2 us (7%)
  starting transfers between devices  8.23 us (5%)
    pallas_call x4, Pallas kernels, piece(): pl.pallas_call(functools.partial(piece_kernel, i, k, last), out_shape=out...  47.1 us
    pallas_call x1, Pallas kernels, gather_parts(): pl.pallas_call(gather_kernel, out_shape=(jax.ShapeDtypeStruct((rows,) + x...  41.8 us
    pallas_call x1, Pallas kernels, own_cycle(): pl.pallas_call(own_cycle_kernel, out_shape=(jax.ShapeDtypeStruct((4, widt...  22.7 us
    pallas_call x1, Pallas kernels, own_ladder(): pl.pallas_call(own_ladder_kernel, out_shape=(jax.ShapeDtypeStruct((width,...  15.5 us
    ppermute x4, waiting for transfers between devices, per_device(): pieces = [lax.ppermute(turned[p], 'col', mirror) for p in range(occ * occ)]  12.2 us
    ppermute x4, starting transfers between devices, per_device(): pieces = [lax.ppermute(turned[p], 'col', mirror) for p in range(occ * occ)]  7.06 us
    gather x1, local copies, waits for them, and re-layouts, per_device(): virt_levels = virt_energy[window_index]  3.45 us
  transfers between devices with their start and end apart: 6, of which 1 were waited for; matrix products, arithmetic and copies ran while one was open for 7% of the time, Pallas kernels for 45%

profile of v1, /device:TPU:6, one launch (start us, length us, event | category | flops | bytes accessed | tf_op | source)
XLA Modules:
  0.0 162.7 jit_solution(12620482043152506844)
XLA Ops:
  0.6 0.0 copy-start
  0.6 0.0 copy-start.5
  0.7 0.0 copy-start.1
  0.7 41.8 %gather_parts.1 = (bf16[8,2,64,768]{3,2,1,0:T(8,128)(2,1)}, bf16[16,4,64,1024]{3,2,1,0:T(8,128)(2,1)}, bf16[2,4,64,1024]{3,2,1,0:T(8,128)(2,1)}, bf16[768,768]{1...) custom-call(bf16[2,64,768]{2,1,0:T(8,128)(2,1)} %x_ref.1, ...), custom_call_target="tpu_custom_call" | custom-call | tf_op jit(solution)/shard_map/gather_parts/pallas_call | solution.py:143
  42.5 1.1 collective-permute-start.1
  43.5 1.4 collective-permute-start.5
  45.0 2.1 %collective-permute-start.4 = (bf16[768,768]{1,0:T(8,128)(2,1)}, bf16[768,768]{1,0:T(8,128)(2,1)}, u32[]{:S(2)}, u32[]{:S(2)}) collective-permute-start(bf16[768,768]{1,0:T(8,128)(2,1)} %get-tuple-element.26), channel_id=1, source_target_pairs={{0,8},{1,9},{2,10},{3,11},{4,12},{5,13},{6,14},{7,15},{8,0},{9,1},... | collective-permute-start | bytes 3538952 | tf_op jit(solution)/shard_map/ppermute | solution.py:402
  47.1 1.4 collective-permute-start.3
  48.5 2.1 %collective-permute-start = (bf16[768,768]{1,0:T(8,128)(2,1)}, bf16[768,768]{1,0:T(8,128)(2,1)S(1)}, u32[]{:S(2)}, u32[]{:S(2)}) collective-permute-start(bf16[768,768]{1,0:T(8,128)(2,1)} %get-tuple-element.28), channel_id=1, source_target_pairs={{0,8},{1,9},{2,10},{3,11},{4,12},{5,13},{6,14},{7,15},{8,0},{9,1},... | collective-permute-start | bytes 3538952 | tf_op jit(solution)/shard_map/ppermute | solution.py:402
  51.3 0.0 copy-done.5
  51.3 0.5 compare_select_fusion.5
  51.8 0.1 broadcast_in_dim.32
  51.9 1.1 convert_element_type.28.mask_ref.mcol_ref
  53.0 0.0 copy-done.1
  53.0 1.2 gather_fusion.1
  54.2 15.5 %own_ladder.1 = (bf16[768,768]{1,0:T(8,128)(2,1)}, bf16[768,768]{1,0:T(8,128)(2,1)}, bf16[4,768,768]{2,1,0:T(8,128)(2,1)}) custom-call(s32[12]{0:T(128)} %gather_fusion.1, f32[768,1]{1,0:T(8,128)} %convert_element_type.28.mask_ref.mcol_ref, bf16[16,64,768]{2,1,0:T(8,128)(2,1)} %bitcast.23, bf16[4,768,768]{2,1,0:T(8,128)(2,1)} %bitcast.11, ...), custom_call_target="tpu_custom_call" | custom-call | tf_op jit(solution)/shard_map/own_ladder/pallas_call | solution.py:201
  69.7 0.0 collective-permute-done.1.side_ref
  69.7 0.1 collective-permute-start.2
  69.8 0.7 convert_element_type.27.mrow_ref
  70.4 0.1 broadcast_select_fusion
  70.5 0.1 add.80
  70.6 0.6 pad_clamp_fusion.1
  71.2 0.0 copy-done
  71.2 0.0 copy-start.2
  71.2 3.4 %gather_fusion = f32[768]{0:T(1024)S(1)} fusion(f32[1024]{0:T(1024)S(1)} %copy-done, s32[1024]{0:T(1024)} %pad_clamp_fusion.1), kind=kCustom, calls=%fused_computation | custom fusion | bytes 9216 | tf_op jit(solution)/shard_map/gather | solution.py:413
  74.7 0.6 broadcast_in_dim.31.vrow_ref
  75.3 0.9 broadcast_in_dim.36.vcol_ref
  76.2 0.0 copy-done.2
  76.2 1.5 copy.18
  77.7 0.7 select_n.97.picked_ref
  78.3 0.0 collective-permute-done.2.twin_ref
  78.3 22.7 %own_cycle.1 = (bf16[4,768,768]{2,1,0:T(8,128)(2,1)}, f32[4,768,768]{2,1,0:T(8,128)}) custom-call(s32[12]{0:T(128)} %get-tuple-element.49.kind_ref, s32[12]{0:T(128)} %get-tuple-element.48.at_ref, s32[1,768]{1,0:T(1,128)} %select_n.97.picked_ref, bf16[16,4,64,1024]{3,2,1,0:T(8,128)(2,1)} %get-tuple-element.40.wall_ref, ...), custom_call_target="tpu_custom_call" | custom-call | tf_op jit(solution)/shard_map/own_cycle/pallas_call | solution.py:262
  101.0 0.0 collective-permute-done.5.refs_0_
  101.1 11.3 %piece_00.1.refs_7_ = f32[4,768,768]{2,1,0:T(8,128)} custom-call(f32[2,2]{1,0:T(2,128)} %bitcast.25, f32[768,1]{1,0:T(8,128)} %broadcast_in_dim.36.vcol_ref, f32[1,768]{1,0:T(1,128)} %broadcast_in_dim.31.vrow_ref, f32[768,1]{1,0:T(8,128)} %convert_element_type.28.mask_ref.mcol_ref, ...), custom_call_target="tpu_custom_call", output_to_operand_aliasing={{}: (12, {})} | custom-call | tf_op jit(solution)/shard_map/piece_00/pallas_call | solution.py:360
  112.3 0.0 collective-permute-done.4.refs_0_
  112.3 12.3 %piece_01.1 = (f32[4,768,768]{2,1,0:T(8,128)}, bf16[4,768,768]{2,1,0:T(8,128)(2,1)}) custom-call(f32[2,2]{1,0:T(2,128)} %bitcast.26, f32[768,1]{1,0:T(8,128)} %broadcast_in_dim.36.vcol_ref, f32[1,768]{1,0:T(1,128)} %broadcast_in_dim.31.vrow_ref, f32[768,1]{1,0:T(8,128)} %convert_element_type.28.mask_ref.mcol_ref, ...), custom_call_target="tpu_custom_call", output_to_operand_aliasing={{0}: (12, {})} | custom-call | tf_op jit(solution)/shard_map/piece_01/pallas_call | solution.py:360
  124.7 0.0 collective-permute-done.3.refs_0_
  124.7 0.0 copy-start.4
  124.7 1.0 copy-done.4
  125.7 11.2 %piece_10.1.refs_7_ = f32[4,768,768]{2,1,0:T(8,128)} custom-call(f32[2,2]{1,0:T(2,128)} %bitcast.27, f32[768,1]{1,0:T(8,128)} %broadcast_in_dim.36.vcol_ref, f32[1,768]{1,0:T(1,128)} %broadcast_in_dim.31.vrow_ref, f32[768,1]{1,0:T(8,128)} %convert_element_type.28.mask_ref.mcol_ref, ...), custom_call_target="tpu_custom_call", output_to_operand_aliasing={{}: (12, {})} | custom-call | tf_op jit(solution)/shard_map/piece_10/pallas_call | solution.py:360
  137.0 12.2 %collective-permute-done.refs_0_ = bf16[768,768]{1,0:T(8,128)(2,1)S(1)} collective-permute-done((bf16[768,768]{1,0:T(8,128)(2,1)}, bf16[768,768]{1,0:T(8,128)(2,1)S(1)}, u32[]{:S(2)}, u32[]{:S(2)}) %collective-permute-start) | collective-permute-done | bytes 1179680 | tf_op jit(solution)/shard_map/ppermute | solution.py:402
  149.1 0.0 copy-start.3
  149.1 1.0 copy-done.3
  150.2 12.3 %piece_11.1 = (f32[4,768,768]{2,1,0:T(8,128)}, bf16[4,768,768]{2,1,0:T(8,128)(2,1)}) custom-call(f32[2,2]{1,0:T(2,128)} %bitcast.28, f32[768,1]{1,0:T(8,128)} %broadcast_in_dim.36.vcol_ref, f32[1,768]{1,0:T(1,128)} %broadcast_in_dim.31.vrow_ref, f32[768,1]{1,0:T(8,128)} %convert_element_type.28.mask_ref.mcol_ref, ...), custom_call_target="tpu_custom_call", output_to_operand_aliasing={{0}: (12, {}), {1}: (13, {})} | custom-call | tf_op jit(solution)/shard_map/piece_11/pallas_call | solution.py:360
  (3 shorter events, 0.0 us)
Async XLA Ops:
  0.6 70.6 %copy-start = (f32[1024]{0:T(1024)S(1)}, f32[1024]{0:T(1024)}, u32[]{:S(2)}) copy-start(f32[1024]{0:T(1024)} %param.17) | copy-start | bytes 12292
  0.6 50.6 %copy-start.5 = (s32[1,1,12]{2,1,0:T(1,128)S(1)}, s32[1,1,12]{2,1,0:T(1,128)}, u32[]{:S(2)}) copy-start(s32[1,1,12]{2,1,0:T(1,128)} %param.13) | copy-start | bytes 148
  0.7 52.4 %copy-start.1 = (s32[16]{0:T(128)S(1)}, s32[16]{0:T(128)}, u32[]{:S(2)}) copy-start(s32[16]{0:T(128)} %param.15) | copy-start | bytes 196
  42.5 27.2 %collective-permute-start.1 = (bf16[2,4,64,1024]{3,2,1,0:T(8,128)(2,1)}, bf16[2,4,64,1024]{3,2,1,0:T(8,128)(2,1)}, u32[]{:S(2)}, u32[]{:S(2)}) collective-permute-start(bf16[2,4,64,1024]{3,2,1,0:T(8,128)(2,1)} %get-tuple-element.37.far_ref), channel_id=1, source_target_pairs={{0,2},{1,3},{2,0},{3,1},{4,6},{5,7},{6,4},{7,5},{8,10},{9,11},{10,... | collective-permute-start | bytes 3145736 | tf_op jit(solution)/shard_map/ppermute | solution.py:400
  43.5 57.5 %collective-permute-start.5 = (bf16[768,768]{1,0:T(8,128)(2,1)}, bf16[768,768]{1,0:T(8,128)(2,1)}, u32[]{:S(2)}, u32[]{:S(2)}) collective-permute-start(bf16[768,768]{1,0:T(8,128)(2,1)} %get-tuple-element.25), channel_id=1, source_target_pairs={{0,8},{1,9},{2,10},{3,11},{4,12},{5,13},{6,14},{7,15},{8,0},{9,1},... | collective-permute-start | bytes 3538952 | tf_op jit(solution)/shard_map/ppermute | solution.py:402
  45.0 67.4 %collective-permute-start.4 = (bf16[768,768]{1,0:T(8,128)(2,1)}, bf16[768,768]{1,0:T(8,128)(2,1)}, u32[]{:S(2)}, u32[]{:S(2)}) collective-permute-start(bf16[768,768]{1,0:T(8,128)(2,1)} %get-tuple-element.26), channel_id=1, source_target_pairs={{0,8},{1,9},{2,10},{3,11},{4,12},{5,13},{6,14},{7,15},{8,0},{9,1},... | collective-permute-start | bytes 3538952 | tf_op jit(solution)/shard_map/ppermute | solution.py:402
  47.1 77.6 %collective-permute-start.3 = (bf16[768,768]{1,0:T(8,128)(2,1)}, bf16[768,768]{1,0:T(8,128)(2,1)S(1)}, u32[]{:S(2)}, u32[]{:S(2)}) collective-permute-start(bf16[768,768]{1,0:T(8,128)(2,1)} %get-tuple-element.27), channel_id=1, source_target_pairs={{0,8},{1,9},{2,10},{3,11},{4,12},{5,13},{6,14},{7,15},{8,0},{9,1},... | collective-permute-start | bytes 3538952 | tf_op jit(solution)/shard_map/ppermute | solution.py:402
  48.5 100.6 %collective-permute-start = (bf16[768,768]{1,0:T(8,128)(2,1)}, bf16[768,768]{1,0:T(8,128)(2,1)S(1)}, u32[]{:S(2)}, u32[]{:S(2)}) collective-permute-start(bf16[768,768]{1,0:T(8,128)(2,1)} %get-tuple-element.28), channel_id=1, source_target_pairs={{0,8},{1,9},{2,10},{3,11},{4,12},{5,13},{6,14},{7,15},{8,0},{9,1},... | collective-permute-start | bytes 3538952 | tf_op jit(solution)/shard_map/ppermute | solution.py:402
  69.7 8.7 %collective-permute-start.2 = (bf16[2,4,64,1024]{3,2,1,0:T(8,128)(2,1)}, bf16[2,4,64,1024]{3,2,1,0:T(8,128)(2,1)}, u32[]{:S(2)}, u32[]{:S(2)}) collective-permute-start(bf16[2,4,64,1024]{3,2,1,0:T(8,128)(2,1)} %collective-permute-done.1.side_ref), channel_id=1, source_target_pairs={{0,1},{1,0},{2,3},{3,2},{4,5},{5,4},{6,7},{7,6},{8,9},{9,8},{10,11... | collective-permute-start | bytes 3145736 | tf_op jit(solution)/shard_map/ppermute | solution.py:432
  71.2 5.0 %copy-start.2 = (bf16[768,768]{1,0:T(8,128)(2,1)S(1)}, bf16[768,768]{1,0:T(8,128)(2,1)}, u32[]{:S(2)}) copy-start(bf16[768,768]{1,0:T(8,128)(2,1)} %core_ref) | copy-start | bytes 3538948
  124.7 1.0 copy-start.4
  149.1 1.0 copy-start.3

commit v2 on v1

v2 whole, which is shorter than its diff:
```python
import functools

import jax
import jax.numpy as jnp
from jax import lax
from jax.experimental import pallas as pl
from jax.experimental.pallas import tpu as pltpu
from jax.sharding import PartitionSpec as P

MESH = pl.DeviceIdType.MESH
VMEM_LIMIT = 56 * 1024 * 1024
STRIP = 384


def dot(a, b):
    return jnp.dot(a, b, preferred_element_type=jnp.float32)


def dot_nt(a, b):
    return lax.dot_general(a, b, (((1,), (1,)), ((), ())), preferred_element_type=jnp.float32)


def strips(width, step):
    return [pl.ds(start, step) for start in range(0, width, step)]


def remote(src, dst, sems, index, device):
    return pltpu.make_async_remote_copy(
        src_ref=src, dst_ref=dst, send_sem=sems[0].at[index], recv_sem=sems[1].at[index],
        device_id=device, device_id_type=MESH,
    )


def greet(devices):
    barrier = pltpu.get_barrier_semaphore()
    for device in devices:
        pl.semaphore_signal(barrier, inc=1, device_id=device, device_id_type=MESH)
    pl.semaphore_wait(barrier, len(devices))


def gather_kernel(
    x_ref, w_ref, amps_ref, xall_ref, wall_ref, first_ref, *refs
):
    cuts, (plain, turned, wsend, wrecv, xsend, xrecv, msend, mrecv, local, tsem) = refs[:-10], refs[-10:]
    r = lax.axis_index("row")
    c = lax.axis_index("col")
    rows = lax.axis_size("row")
    cols = lax.axis_size("col")
    forth = (r, (c + 4) % cols)
    back = (r, (c + cols - 4) % cols)
    mirror = (r, (c + cols // 2) % cols)
    zside = (r, c + 2 - 4 * ((c // 2) % 2))
    twin = (r, c + 1 - 2 * (c % 2))
    beside = r + 1 - 2 * (r % 2)
    core = c % 2
    half = w_ref.shape[0] // 2
    width = plain.shape[1]
    y_steps = range(1, rows // 2)

    amps_in = [pltpu.make_async_copy(amps_ref.at[q], plain.at[q], tsem.at[q]) for q in range(4)]
    for copy in amps_in:
        copy.start()
    greet(
        [forth, back, mirror, zside, twin, (beside, c)]
        + [((r + 2 * step) % rows, c) for step in y_steps]
    )
    wsems, xsems = (wsend, wrecv), (xsend, xrecv)
    started = []

    def send(*args):
        copy = remote(*args)
        copy.start()
        started.append(copy)

    def arrived(part, sems, index):
        remote(part, part, sems, index, twin).wait_recv()

    def shard(offset, plane, side):
        x = (c // 4 + offset) % (cols // 4)
        z = (c // 2) % 2
        z = z + plane * (1 - 2 * z)
        k = core + side * (1 - 2 * core)
        return wall_ref.at[x * 4 + z * 2 + k]

    def pass_on(offset):
        part = shard(offset, 0, 0)
        send(part, part, wsems, 4 + offset, zside)
        send(part, part, wsems, 8 + offset, twin)

    def transpose(q, p):
        amps_in[q].wait()
        for cut in strips(width, 256):
            turned[p, :, cut] = plain[q, cut, :].T

    own = wall_ref.at[c]
    send(w_ref, own, wsems, 0, forth)
    send(w_ref, own, wsems, 1, back)
    send(w_ref, own, wsems, 4, zside)
    send(x_ref.at[core], xall_ref.at[r, core], xsems, 0, (beside, c))
    for step in y_steps:
        send(x_ref.at[core], xall_ref.at[r, core], xsems, step, ((r + 2 * step) % rows, c))
    send(w_ref, own, wsems, 8, twin)
    own_w = pltpu.make_async_copy(w_ref, own, local.at[0])
    own_x = pltpu.make_async_copy(x_ref, xall_ref.at[r], local.at[1])
    own_w.start()
    own_x.start()
    transpose(0, 0)

    part = xall_ref.at[beside, core]
    arrived(part, xsems, 0)
    for step in y_steps:
        send(part, part, xsems, 3 + step, ((r + 2 * step) % rows, c))
    send(part, part, xsems, 7, twin)

    arrived(shard(3, 0, 0), wsems, 0)
    part = shard(3, 0, 0).at[:half]
    send(part, part, wsems, 2, forth)
    arrived(shard(1, 0, 0), wsems, 1)
    part = shard(1, 0, 0).at[half:]
    send(part, part, wsems, 3, back)
    send(turned.at[0], first_ref, (msend, mrecv), 0, mirror)
    pass_on(3)
    pass_on(1)
    transpose(2, 1)
    for step in y_steps:
        origin = (r + rows - 2 * step) % rows
        arrived(xall_ref.at[origin, core], xsems, step)
        send(xall_ref.at[origin, core], xall_ref.at[origin, core], xsems, 7 + step, twin)
    transpose(1, 2)
    arrived(shard(2, 0, 0).at[:half], wsems, 2)
    arrived(shard(2, 0, 0).at[half:], wsems, 3)
    pass_on(2)
    transpose(3, 3)
    outs = [
        pltpu.make_async_copy(
            turned.at[p, :, pl.ds(low, out.shape[1])], out, local.at[2 + at]
        )
        for at, ((p, low), out) in enumerate(zip(((1, 0), (2, 0), (3, 0), (3, cuts[2].shape[1])), cuts))
    ]
    for copy in outs:
        copy.start()
    for step in y_steps:
        origin = (r + rows - 2 * step) % rows
        origin = origin + 1 - 2 * (origin % 2)
        arrived(xall_ref.at[origin, core], xsems, 3 + step)
        send(xall_ref.at[origin, core], xall_ref.at[origin, core], xsems, 10 + step, twin)
    for offset in (0, 3, 1, 2):
        part = shard(offset, 1, 0)
        arrived(part, wsems, 4 + offset)
        send(part, part, wsems, 12 + offset, twin)

    for offset in range(4):
        arrived(shard(offset, 0, 1), wsems, 8 + offset)
        arrived(shard(offset, 1, 1), wsems, 12 + offset)
    arrived(xall_ref.at[beside, 1 - core], xsems, 7)
    for step in y_steps:
        origin = (r + rows - 2 * step) % rows
        arrived(xall_ref.at[origin, 1 - core], xsems, 7 + step)
        origin = origin + 1 - 2 * (origin % 2)
        arrived(xall_ref.at[origin, 1 - core], xsems, 10 + step)
    remote(turned.at[0], first_ref, (msend, mrecv), 0, mirror).wait_recv()
    for copy in started:
        copy.wait_send()
    for copy in outs + [own_w, own_x]:
        copy.wait()


def gather_parts(x_factor, shard, amp4, split):
    rows = lax.axis_size("row")
    cols = lax.axis_size("col")
    width = amp4.shape[1]
    hbm = pl.BlockSpec(memory_space=pl.ANY)
    bf16 = jnp.bfloat16
    dma = pltpu.SemaphoreType.DMA
    shapes = [(rows,) + x_factor.shape, (cols,) + shard.shape] + [(width, width)] * 3
    shapes += [(width, split), (width, width - split)]
    return pl.pallas_call(
        gather_kernel,
        out_shape=[jax.ShapeDtypeStruct(shape, bf16) for shape in shapes],
        in_specs=[hbm] * 3,
        out_specs=[hbm] * len(shapes),
        scratch_shapes=[
            pltpu.VMEM(amp4.shape, bf16),
            pltpu.VMEM(amp4.shape, bf16),
            dma((16,)),
            dma((16,)),
            dma((14,)),
            dma((14,)),
            dma((1,)),
            dma((1,)),
            dma((6,)),
            dma((4,)),
        ],
        compiler_params=pltpu.CompilerParams(
            collective_id=0, has_side_effects=True, vmem_limit_bytes=VMEM_LIMIT
        ),
        name="gather_parts",
    )(x_factor, shard, amp4)


def own_ladder_kernel(
    slots_ref, mask_ref, xall_ref, amps_ref, core_ref, x_ref, xt_ref, wt_ref, gathered, proj, sem
):
    @pl.when(pl.program_id(0) == 0)
    def _():
        tile = xall_ref.shape[1]
        copies = []
        for s in range(slots_ref.shape[0]):
            copy = pltpu.make_async_copy(
                xall_ref.at[slots_ref[s]], gathered.at[pl.ds(s * tile, tile), :], sem.at[s]
            )
            copy.start()
            copies.append(copy)
        for copy in copies:
            copy.wait()
        x_ref[...] = jnp.where(
            mask_ref[...] > 0.0, gathered[...].astype(jnp.float32), 0.0
        ).astype(x_ref.dtype)
        for cut in strips(x_ref.shape[0], 256):
            xt_ref[:, cut] = x_ref[cut, :].T

    proj[...] = dot(xt_ref[...], amps_ref[0]).astype(proj.dtype)
    inner = dot(proj[...], x_ref[...])
    wt_ref[0] = (core_ref[...].astype(jnp.float32) * inner).astype(wt_ref.dtype)


def own_ladder(slots, mcol, xall, amp4, core):
    width = amp4.shape[1]
    points = core.shape[0]
    smem = pl.BlockSpec(memory_space=pltpu.SMEM)
    bf16 = jnp.bfloat16

    def whole(shape):
        return pl.BlockSpec(shape, lambda p: (0, 0))

    return pl.pallas_call(
        own_ladder_kernel,
        out_shape=(
            jax.ShapeDtypeStruct((width, points), bf16),
            jax.ShapeDtypeStruct((points, width), bf16),
            jax.ShapeDtypeStruct((4, points, points), bf16),
        ),
        grid=(4,),
        in_specs=[
            smem, whole((width, 1)), pl.BlockSpec(memory_space=pl.ANY),
            pl.BlockSpec((1, width, width), lambda p: (p, 0, 0)), whole((points, points)),
        ],
        out_specs=(
            whole((width, points)), whole((points, width)),
            pl.BlockSpec((1, points, points), lambda p: (p, 0, 0)),
        ),
        scratch_shapes=[
            pltpu.VMEM((width, points), bf16),
            pltpu.VMEM((points, width), bf16),
            pltpu.SemaphoreType.DMA((slots.shape[0],)),
        ],
        compiler_params=pltpu.CompilerParams(vmem_limit_bytes=VMEM_LIMIT),
        name="own_ladder",
    )(slots, mcol, xall, amp4, core)


def own_cycle_kernel(
    tiles_ref, picked_ref, wall_ref, a0_ref, a1_ref, wd_ref, cyc_ref, wsel, pick, sem
):
    p = pl.program_id(0)
    tile = wall_ref.shape[2]
    slots = tiles_ref.shape[0]

    def fetch(first, s):
        return pltpu.make_async_copy(
            wall_ref.at[tiles_ref[s], pl.ds(2 * first, 2)],
            wsel.at[pl.ds(2 * first, 2), pl.ds(s * tile, tile), :],
            sem.at[first, s],
        )

    @pl.when(p == 0)
    def _():
        for first in range(2):
            for s in range(slots):
                fetch(first, s).start()

        window = lax.broadcasted_iota(jnp.int32, pick.shape, 0)
        pick[...] = jnp.where(window == picked_ref[...], 1.0, 0.0).astype(pick.dtype)

    for first in range(2):

        @pl.when(p == 2 * first)
        def _(first=first):
            for s in range(slots):
                fetch(first, s).wait()
            for k in range(2):
                wd_ref[k] = dot(wsel[2 * first + k], pick[...]).astype(wd_ref.dtype)

    cyc_ref[0] = dot(wd_ref[0], a0_ref[0]) + dot(wd_ref[1], a1_ref[0])


def own_cycle(tiles, picked, wall, amp4):
    width = amp4.shape[1]
    slots, window = tiles.shape[0], wall.shape[3]
    smem = pl.BlockSpec(memory_space=pltpu.SMEM)
    hbm = pl.BlockSpec(memory_space=pl.ANY)
    return pl.pallas_call(
        own_cycle_kernel,
        out_shape=(
            jax.ShapeDtypeStruct((4, width, width), jnp.bfloat16),
            jax.ShapeDtypeStruct((4, width, width), jnp.float32),
        ),
        grid=(4,),
        in_specs=[
            smem,
            pl.BlockSpec((1, width), lambda p: (0, 0)),
            hbm,
            pl.BlockSpec((1, width, width), lambda p: (p % 2, 0, 0)),
            pl.BlockSpec((1, width, width), lambda p: (2 + p % 2, 0, 0)),
        ],
        out_specs=(
            pl.BlockSpec((2, width, width), lambda p: (p // 2, 0, 0)),
            pl.BlockSpec((1, width, width), lambda p: (p, 0, 0)),
        ),
        scratch_shapes=[
            pltpu.VMEM((4, width, window), jnp.bfloat16),
            pltpu.VMEM((window, width), jnp.bfloat16),
            pltpu.SemaphoreType.DMA((2, slots)),
        ],
        compiler_params=pltpu.CompilerParams(vmem_limit_bytes=VMEM_LIMIT),
        name="own_cycle",
    )(tiles, picked, wall, amp4, amp4)


def piece_kernel(i, k, low, high, end, occ_ref, vcol_ref, vrow_ref, mcol_ref, mrow_ref, *refs):
    last = k == 1 and end
    scratch = 13
    refs, (xt, coret, wt, right, left, part, amps, acc, proj, total, upd, sem, osem) = (
        refs[:-scratch], refs[-scratch:]
    )
    (b_hbm, xt_hbm, x_hbm, coret_hbm, wt_hbm, wd_hbm, amps_hbm, part_hbm) = refs[:8]
    refs = list(refs[8:])
    acc_in = refs.pop(0) if low > 0 else None
    if last:
        upd_hbm = refs.pop()
    acc_out = None if end else refs.pop()
    res_hbm = refs.pop()
    width, points = x_hbm.shape
    head, rest = pl.ds(0, points), pl.ds(points, high - low)
    cut = pl.ds(low, high - low)
    plan = {
        "b": (b_hbm, left.at[:, rest]),
        "xt": (xt_hbm, xt),
        "x": (x_hbm, right.at[k, :, head]),
    }
    if low > 0:
        plan["acc"] = (acc_in, acc)
    if end:
        plan["coret"] = (coret_hbm, coret)
        plan["wt"] = (wt_hbm.at[2 * i + k], wt)
    plan["w0"] = (wd_hbm.at[k, :, cut], right.at[0, :, rest])
    plan["w1"] = (wd_hbm.at[2 + k, :, cut], right.at[1, :, rest])
    plan["part"] = (part_hbm.at[pl.ds(2 * i, 2)], part)
    if last:
        plan["amps"] = (amps_hbm.at[pl.ds(2 * i, 2)], amps)
    loads = {}
    for at, (name, (src, dst)) in enumerate(plan.items()):
        loads[name] = pltpu.make_async_copy(src, dst, sem.at[at])
        loads[name].start()

    def need(*names):
        for name in names:
            if name in loads:
                loads.pop(name).wait()

    outs = []

    def put(src, dst, at):
        copy = pltpu.make_async_copy(src, dst, osem.at[at])
        copy.start()
        outs.append(copy)

    def emit(j, rows, at, raw):
        raw = raw + part[j, rows, :]
        pair = 2 * i + j
        if last:
            live = (mcol_ref[rows, :] * mrow_ref[...]) > 0.0
            raw = jnp.where(live, raw, 0.0)
            own = jnp.where(live, amps[j, rows, :].astype(jnp.float32), 0.0)
            gap = (occ_ref[0, i] + occ_ref[1, j]) - vcol_ref[rows, :] - vrow_ref[...]
            upd[j, rows, :] = (own + raw / gap).astype(upd.dtype)
            put(upd.at[j, rows, :], upd_hbm.at[pair, rows, :], 4 + 2 * j + at)
        part[j, rows, :] = raw
        put(part.at[j, rows, :], res_hbm.at[pair, rows, :], 2 * j + at)

    def cycle_alone(j):
        for at, rows in enumerate(strips(width, STRIP)):
            emit(j, rows, at, dot_nt(left[rows, rest], right[j, :, rest]))

    need("b", "xt")
    proj[...] = dot(xt[...], left[:, rest]).astype(proj.dtype)
    need("x", "acc", "coret", "wt")
    inner = dot(proj[...], right[k, cut, head])
    if low > 0:
        inner = inner + acc[...]
    if end:
        total[...] = (
            wt[...].astype(jnp.float32) + coret[...].astype(jnp.float32) * inner
        ).astype(total.dtype)
        need("w0", "w1", "part", "amps")
        cycle_alone(1 - k)
        left[:, head] = dot(right[k, :, head], total[...]).astype(left.dtype)
        for at, rows in enumerate(strips(width, STRIP)):
            emit(k, rows, at, dot_nt(left[rows, :], right[k]))
    else:
        acc[...] = inner
        put(acc, acc_out, 8)
        need("w0", "w1", "part")
        for j in range(2):
            cycle_alone(j)
    for copy in outs:
        copy.wait()


def piece(i, k, low, high, occ, vcol, vrow, mcol, mrow, b, xt, x, coret, wt, wd, amp4, part, acc, updated):
    width, points = x.shape
    end = high == width
    last = k == 1 and end
    vmem = pl.BlockSpec(memory_space=pltpu.VMEM)
    hbm = pl.BlockSpec(memory_space=pl.ANY)
    f32, bf16 = jnp.float32, jnp.bfloat16
    operands = [occ, vcol, vrow, mcol, mrow, b, xt, x, coret, wt, wd, amp4, part]
    out_shape = [jax.ShapeDtypeStruct(part.shape, f32)]
    alias = {len(operands) - 1: 0}
    if low > 0:
        operands.append(acc)
    if not end:
        out_shape.append(jax.ShapeDtypeStruct((points, points), f32))
    if last:
        out_shape.append(jax.ShapeDtypeStruct(part.shape, bf16))
        if updated is not None:
            alias[len(operands)] = 1
            operands.append(updated)
    return pl.pallas_call(
        functools.partial(piece_kernel, i, k, low, high, end),
        out_shape=out_shape,
        in_specs=[pl.BlockSpec(memory_space=pltpu.SMEM)] + [vmem] * 4 + [hbm] * (len(operands) - 5),
        out_specs=[hbm] * len(out_shape),
        scratch_shapes=[
            pltpu.VMEM((points, width), bf16),
            pltpu.VMEM((points, points), bf16),
            pltpu.VMEM((points, points), bf16),
            pltpu.VMEM((2, width, points + high - low), bf16),
            pltpu.VMEM((width, points + high - low), bf16),
            pltpu.VMEM((2, width, width), f32),
            pltpu.VMEM((2, width, width), bf16),
            pltpu.VMEM((points, points), f32),
            pltpu.VMEM((points, high - low), bf16),
            pltpu.VMEM((points, points), bf16),
            pltpu.VMEM((2, width, width), bf16),
            pltpu.SemaphoreType.DMA((10,)),
            pltpu.SemaphoreType.DMA((9,)),
        ],
        input_output_aliases=alias,
        compiler_params=pltpu.CompilerParams(vmem_limit_bytes=VMEM_LIMIT),
        name="piece_%d%d_%d" % (i, k, low),
    )(*operands)


def per_device(
    amps, x_factor, core, cycle_w, domain_tiles, domain_count, tile_slot, occ_energy, virt_energy
):
    occ = amps.shape[2]
    width = amps.shape[4]
    slot_count = domain_tiles.shape[2]
    tile_width = x_factor.shape[1]
    grid_points = x_factor.shape[2]
    window = cycle_w.shape[4]
    cols = lax.axis_size("col")
    amp4 = amps[0, 0].reshape(occ * occ, width, width)
    shard = cycle_w[0].reshape(occ * occ, tile_width, window)

    split = 512
    xall, wall, first, *turned = gather_parts(x_factor, shard, amp4, split)
    xall = xall.reshape(-1, tile_width, grid_points)
    mirror = [(i, (i + cols // 2) % cols) for i in range(cols)]

    def send_piece(i, k, low, high, part):
        return i, k, low, high, lax.ppermute(part, "col", mirror)

    pieces = [
        (0, 0, 0, width, first),
        send_piece(0, 1, 0, width, turned[0]),
        send_piece(1, 0, 0, width, turned[1]),
        send_piece(1, 1, 0, split, turned[2]),
    ]

    tile_list, count, tile_slot, virt_energy, core, _ = lax.optimization_barrier(
        (domain_tiles[0, 0], domain_count[0, 0], tile_slot, virt_energy, core, turned)
    )
    live_slots = jnp.arange(slot_count, dtype=jnp.int32) < count
    row_live = jnp.repeat(live_slots, tile_width)
    window_index = (
        tile_list[:, None] * tile_width + jnp.arange(tile_width, dtype=jnp.int32)[None, :]
    ).reshape(width)
    picked = jnp.where(row_live, window_index, -1)[None, :]
    virt_levels = virt_energy[window_index]
    mask = row_live.astype(jnp.float32)
    vcol, vrow, mcol, mrow = virt_levels[:, None], virt_levels[None, :], mask[:, None], mask[None, :]
    coret = jnp.transpose(core)

    x, xt, wt = own_ladder(tile_slot[tile_list], mcol, xall, amp4, core)
    tail, wt = lax.optimization_barrier((turned[3], wt))
    pieces.append(send_piece(1, 1, split, width, tail))
    picked, wt = lax.optimization_barrier((picked, wt))
    wd, part = own_cycle(tile_list, picked, wall, amp4)
    updated = acc = None
    for i, k, low, high, b in pieces:
        out = piece(
            i, k, low, high, occ_energy[0, 0], vcol, vrow, mcol, mrow,
            b, xt, x, coret, wt, wd, amp4, part, acc, updated,
        )
        part = out[0]
        if high < width:
            acc = out[1]
        elif k == 1:
            updated = out[1]
    return part.reshape(amps.shape), updated.reshape(amps.shape)


def solution(mesh):
    in_specs = (
        P("row", "col", None, None, None, None),
        P("row", None, None),
        P(),
        P("row", None, None, "col", None),
        P("row", "col", None),
        P("row", "col"),
        P(),
        P("row", "col", None, None),
        P(),
    )
    out_specs = (P("row", "col", None, None, None, None), P("row", "col", None, None, None, None))
    return jax.shard_map(
        per_device, mesh=mesh, in_specs=in_specs, out_specs=out_specs, check_vma=False
    )
```

time: 163 us -> 170 us (1.043)
  Pallas kernels: 127 us -> 146 us
  waiting for transfers between devices: 12.2 us -> 0.01 us
    pallas_call x5 -> x6, Pallas kernels: 88.9 us -> 113 us  [the longest x1 58.5 us: gather_parts(): pl.pallas_call(gather_kernel, out_shape=[jax.ShapeDtypeStruct(shape, bf16...]
    ppermute x6 -> x4, waiting for transfers between devices: 12.2 us -> 0.01 us  [send_piece(): return (i, k, low, high, lax.ppermute(part, 'col', mirror))]
    pallas_call x1, Pallas kernels: 22.7 us -> 19.3 us  [own_cycle(): pl.pallas_call(own_cycle_kernel, out_shape=(jax.ShapeDtypeStruct((4, widt...]
    pallas_call x1, Pallas kernels: 15.5 us -> 13.5 us  [own_ladder(): pl.pallas_call(own_ladder_kernel, out_shape=(jax.ShapeDtypeStruct((width,...]
    ppermute x6 -> x4, starting transfers between devices: 8.23 us -> 7.22 us  [send_piece(): return (i, k, low, high, lax.ppermute(part, 'col', mirror))]
  transfers between devices with their start and end apart: 6 -> 4, of which waited for: 1 -> 0; matrix products, arithmetic and copies ran while one was open for 7% -> 8% of each run, Pallas kernels for 45% -> 44%
where the time goes in v2:
time: 170 us
  Pallas kernels  146 us (86%)
  local copies, waits for them, and re-layouts  12.8 us (8%)
  starting transfers between devices  7.22 us (4%)
  other arithmetic  2.46 us (1%)
    pallas_call x1, Pallas kernels, gather_parts(): pl.pallas_call(gather_kernel, out_shape=[jax.ShapeDtypeStruct(shape, bf16...  58.5 us
    pallas_call x5, Pallas kernels, piece(): pl.pallas_call(functools.partial(piece_kernel, i, k, low, high, end), out...  54.3 us
    pallas_call x1, Pallas kernels, own_cycle(): pl.pallas_call(own_cycle_kernel, out_shape=(jax.ShapeDtypeStruct((4, widt...  19.3 us
    pallas_call x1, Pallas kernels, own_ladder(): pl.pallas_call(own_ladder_kernel, out_shape=(jax.ShapeDtypeStruct((width,...  13.5 us
    ppermute x4, starting transfers between devices, send_piece(): return (i, k, low, high, lax.ppermute(part, 'col', mirror))  7.22 us
  transfers between devices with their start and end apart: 4, of which 0 were waited for; matrix products, arithmetic and copies ran while one was open for 8% of the time, Pallas kernels for 44%

profile of v2, /device:TPU:6, one launch (start us, length us, event | category | flops | bytes accessed | tf_op | source)
XLA Modules:
  0.0 169.7 jit_solution(12761124844405434774)
XLA Ops:
  0.6 0.0 copy-start
  0.6 0.0 copy-start.1
  0.7 0.0 copy-start.5
  0.7 58.5 %gather_parts.1 = (bf16[8,2,64,768]{3,2,1,0:T(8,128)(2,1)}, bf16[16,4,64,1024]{3,2,1,0:T(8,128)(2,1)}, bf16[768,768]{1,0:T(8,128)(2,1)}, bf16[768,768]{1,0:T(8,1...) custom-call(bf16[2,64,768]{2,1,0:T(8,128)(2,1)} %x_ref.1, ...), custom_call_target="tpu_custom_call" | custom-call | tf_op jit(solution)/shard_map/gather_parts/pallas_call | solution.py:177
  59.2 1.5 collective-permute-start.3
  60.7 2.1 %collective-permute-start.2 = (bf16[768,768]{1,0:T(8,128)(2,1)}, bf16[768,768]{1,0:T(8,128)(2,1)S(1)}, u32[]{:S(2)}, u32[]{:S(2)}) collective-permute-start(bf16[768,768]{1,0:T(8,128)(2,1)} %get-tuple-element.30), channel_id=1, source_target_pairs={{0,8},{1,9},{2,10},{3,11},{4,12},{5,13},{6,14},{7,15},{8,0},{9,1},... | collective-permute-start | bytes 3538952 | tf_op jit(solution)/shard_map/ppermute | solution.py:484
  62.8 1.4 collective-permute-start.1
  64.9 0.1 broadcast_in_dim.26
  64.9 1.1 convert_element_type.28.mask_ref.mcol_ref
  66.1 0.0 copy-done.5
  66.1 0.5 compare_select_fusion.1
  66.6 0.0 copy-done.1
  66.6 1.2 gather_fusion.1
  67.8 0.0 copy-start.2
  67.8 13.5 %own_ladder.1 = (bf16[768,768]{1,0:T(8,128)(2,1)}, bf16[768,768]{1,0:T(8,128)(2,1)}, bf16[4,768,768]{2,1,0:T(8,128)(2,1)}) custom-call(s32[12]{0:T(128)} %gather_fusion.1, f32[768,1]{1,0:T(8,128)} %convert_element_type.28.mask_ref.mcol_ref, bf16[16,64,768]{2,1,0:T(8,128)(2,1)} %bitcast.26, bf16[4,768,768]{2,1,0:T(8,128)(2,1)} %bitcast.11, ...), custom_call_target="tpu_custom_call" | custom-call | tf_op jit(solution)/shard_map/own_ladder/pallas_call | solution.py:236
  81.2 2.2 %collective-permute-start = (bf16[768,256]{1,0:T(8,128)(2,1)}, bf16[768,256]{1,0:T(8,128)(2,1)}, u32[]{:S(2)}, u32[]{:S(2)}) collective-permute-start(bf16[768,256]{1,0:T(8,128)(2,1)} %get-tuple-element.40), channel_id=1, source_target_pairs={{0,8},{1,9},{2,10},{3,11},{4,12},{5,13},{6,14},{7,15},{8,0},{9,1},... | collective-permute-start | bytes 1179656 | tf_op jit(solution)/shard_map/ppermute | solution.py:484
  83.4 0.7 convert_element_type.27.mrow_ref
  84.1 1.3 broadcast_select_fusion
  85.4 0.8 add.51
  86.2 0.6 pad_clamp_fusion.1
  86.8 0.0 copy-done
  86.8 3.3 %gather_fusion = f32[768]{0:T(1024)S(1)} fusion(f32[1024]{0:T(1024)S(1)} %copy-done, s32[1024]{0:T(1024)} %pad_clamp_fusion.1), kind=kCustom, calls=%fused_computation | custom fusion | bytes 9216 | tf_op jit(solution)/shard_map/gather | solution.py:502
  90.1 0.6 broadcast_in_dim.25.vrow_ref
  90.7 0.9 broadcast_in_dim.30.vcol_ref
  91.6 0.0 copy-done.2
  91.6 1.5 copy.19
  93.1 0.7 select_n.30.picked_ref
  93.8 19.3 %own_cycle.1 = (bf16[4,768,768]{2,1,0:T(8,128)(2,1)}, f32[4,768,768]{2,1,0:T(8,128)}) custom-call(s32[12]{0:T(128)} %bitcast.33, s32[1,768]{1,0:T(1,128)} %select_n.30.picked_ref, bf16[16,4,64,1024]{3,2,1,0:T(8,128)(2,1)} %get-tuple-element.46.wall_ref, bf16[4,768,768]{2,1,0:T(8,128)(2,1)} %bitcast.12, bf16[4,768,768]{2,1,0:T(8,128)(2,1)} %bitcast.13), custom_call_target="tpu_custom_call" | custom-call | tf_op jit(solution)/shard_map/own_cycle/pallas_call | solution.py:302
  113.1 11.3 %piece_00_0.1.refs_7_ = f32[4,768,768]{2,1,0:T(8,128)} custom-call(f32[2,2]{1,0:T(2,128)} %bitcast.28, f32[768,1]{1,0:T(8,128)} %broadcast_in_dim.30.vcol_ref, f32[1,768]{1,0:T(1,128)} %broadcast_in_dim.25.vrow_ref, f32[768,1]{1,0:T(8,128)} %convert_element_type.28.mask_ref.mcol_ref, ...), custom_call_target="tpu_custom_call", output_to_operand_aliasing={{}: (12, {})} | custom-call | tf_op jit(solution)/shard_map/piece_00_0/pallas_call | solution.py:439
  124.4 0.0 collective-permute-done.3.refs_0_
  124.4 0.0 copy-start.4
  124.4 1.0 copy-done.4
  125.4 12.3 %piece_01_0.1 = (f32[4,768,768]{2,1,0:T(8,128)}, bf16[4,768,768]{2,1,0:T(8,128)(2,1)}) custom-call(f32[2,2]{1,0:T(2,128)} %bitcast.29, f32[768,1]{1,0:T(8,128)} %broadcast_in_dim.30.vcol_ref, f32[1,768]{1,0:T(1,128)} %broadcast_in_dim.25.vrow_ref, f32[768,1]{1,0:T(8,128)} %convert_element_type.28.mask_ref.mcol_ref, ...), custom_call_target="tpu_custom_call", output_to_operand_aliasing={{0}: (12, {})} | custom-call | tf_op jit(solution)/shard_map/piece_01_0/pallas_call | solution.py:439
  137.8 0.0 collective-permute-done.2.refs_0_
  137.8 0.0 copy-start.3
  137.8 1.0 copy-done.3
  138.8 11.3 %piece_10_0.1.refs_7_ = f32[4,768,768]{2,1,0:T(8,128)} custom-call(f32[2,2]{1,0:T(2,128)} %bitcast.30, f32[768,1]{1,0:T(8,128)} %broadcast_in_dim.30.vcol_ref, f32[1,768]{1,0:T(1,128)} %broadcast_in_dim.25.vrow_ref, f32[768,1]{1,0:T(8,128)} %convert_element_type.28.mask_ref.mcol_ref, ...), custom_call_target="tpu_custom_call", output_to_operand_aliasing={{}: (12, {})} | custom-call | tf_op jit(solution)/shard_map/piece_10_0/pallas_call | solution.py:439
  150.1 0.0 collective-permute-done.1.refs_0_
  150.1 7.9 %piece_11_0.1 = (f32[4,768,768]{2,1,0:T(8,128)}, f32[768,768]{1,0:T(8,128)}) custom-call(f32[2,2]{1,0:T(2,128)} %bitcast.31, f32[768,1]{1,0:T(8,128)} %broadcast_in_dim.30.vcol_ref, f32[1,768]{1,0:T(1,128)} %broadcast_in_dim.25.vrow_ref, f32[768,1]{1,0:T(8,128)} %convert_element_type.28.mask_ref.mcol_ref, ...), custom_call_target="tpu_custom_call", output_to_operand_aliasing={{0}: (12, {})} | custom-call | tf_op jit(solution)/shard_map/piece_11_0/pallas_call | solution.py:439
  157.9 0.0 collective-permute-done.refs_0_
  158.0 11.6 %piece_11_512.1 = (f32[4,768,768]{2,1,0:T(8,128)}, bf16[4,768,768]{2,1,0:T(8,128)(2,1)}) custom-call(f32[2,2]{1,0:T(2,128)} %bitcast.32, f32[768,1]{1,0:T(8,128)} %broadcast_in_dim.30.vcol_ref, f32[1,768]{1,0:T(1,128)} %broadcast_in_dim.25.vrow_ref, f32[768,1]{1,0:T(8,128)} %convert_element_type.28.mask_ref.mcol_ref, ...), custom_call_target="tpu_custom_call", output_to_operand_aliasing={{0}: (12, {}), {1}: (14, {})} | custom-call | tf_op jit(solution)/shard_map/piece_11_512/pallas_call | solution.py:439
  (3 shorter events, 0.0 us)
Async XLA Ops:
  0.6 86.2 %copy-start = (f32[1024]{0:T(1024)S(1)}, f32[1024]{0:T(1024)}, u32[]{:S(2)}) copy-start(f32[1024]{0:T(1024)} %param.17) | copy-start | bytes 12292
  0.6 65.9 %copy-start.1 = (s32[16]{0:T(128)S(1)}, s32[16]{0:T(128)}, u32[]{:S(2)}) copy-start(s32[16]{0:T(128)} %param.15) | copy-start | bytes 196
  0.7 65.4 %copy-start.5 = (s32[1,1,12]{2,1,0:T(1,128)S(1)}, s32[1,1,12]{2,1,0:T(1,128)}, u32[]{:S(2)}) copy-start(s32[1,1,12]{2,1,0:T(1,128)} %param.13) | copy-start | bytes 148
  59.2 65.2 %collective-permute-start.3 = (bf16[768,768]{1,0:T(8,128)(2,1)}, bf16[768,768]{1,0:T(8,128)(2,1)S(1)}, u32[]{:S(2)}, u32[]{:S(2)}) collective-permute-start(bf16[768,768]{1,0:T(8,128)(2,1)} %get-tuple-element.29), channel_id=1, source_target_pairs={{0,8},{1,9},{2,10},{3,11},{4,12},{5,13},{6,14},{7,15},{8,0},{9,1},... | collective-permute-start | bytes 3538952 | tf_op jit(solution)/shard_map/ppermute | solution.py:484
  60.7 77.1 %collective-permute-start.2 = (bf16[768,768]{1,0:T(8,128)(2,1)}, bf16[768,768]{1,0:T(8,128)(2,1)S(1)}, u32[]{:S(2)}, u32[]{:S(2)}) collective-permute-start(bf16[768,768]{1,0:T(8,128)(2,1)} %get-tuple-element.30), channel_id=1, source_target_pairs={{0,8},{1,9},{2,10},{3,11},{4,12},{5,13},{6,14},{7,15},{8,0},{9,1},... | collective-permute-start | bytes 3538952 | tf_op jit(solution)/shard_map/ppermute | solution.py:484
  62.8 87.3 %collective-permute-start.1 = (bf16[768,512]{1,0:T(8,128)(2,1)}, bf16[768,512]{1,0:T(8,128)(2,1)}, u32[]{:S(2)}, u32[]{:S(2)}) collective-permute-start(bf16[768,512]{1,0:T(8,128)(2,1)} %get-tuple-element.31), channel_id=1, source_target_pairs={{0,8},{1,9},{2,10},{3,11},{4,12},{5,13},{6,14},{7,15},{8,0},{9,1},... | collective-permute-start | bytes 2359304 | tf_op jit(solution)/shard_map/ppermute | solution.py:484
  67.8 23.9 %copy-start.2 = (bf16[768,768]{1,0:T(8,128)(2,1)S(1)}, bf16[768,768]{1,0:T(8,128)(2,1)}, u32[]{:S(2)}) copy-start(bf16[768,768]{1,0:T(8,128)(2,1)} %core_ref) | copy-start | bytes 3538948
  81.2 76.7 %collective-permute-start = (bf16[768,256]{1,0:T(8,128)(2,1)}, bf16[768,256]{1,0:T(8,128)(2,1)}, u32[]{:S(2)}, u32[]{:S(2)}) collective-permute-start(bf16[768,256]{1,0:T(8,128)(2,1)} %get-tuple-element.40), channel_id=1, source_target_pairs={{0,8},{1,9},{2,10},{3,11},{4,12},{5,13},{6,14},{7,15},{8,0},{9,1},... | collective-permute-start | bytes 1179656 | tf_op jit(solution)/shard_map/ppermute | solution.py:484
  124.4 1.0 copy-start.4
  137.8 1.0 copy-start.3

commit v3 on v2

v3 whole, which is shorter than its diff:
```python
import functools

import jax
import jax.numpy as jnp
from jax import lax
from jax.experimental import pallas as pl
from jax.experimental.pallas import tpu as pltpu
from jax.sharding import PartitionSpec as P

MESH = pl.DeviceIdType.MESH
VMEM_LIMIT = 56 * 1024 * 1024
STRIP = 384


def dot(a, b):
    return jnp.dot(a, b, preferred_element_type=jnp.float32)


def dot_nt(a, b):
    return lax.dot_general(a, b, (((1,), (1,)), ((), ())), preferred_element_type=jnp.float32)


def strips(width, step):
    return [pl.ds(start, step) for start in range(0, width, step)]


def remote(src, dst, sems, index, device):
    return pltpu.make_async_remote_copy(
        src_ref=src, dst_ref=dst, send_sem=sems[0].at[index], recv_sem=sems[1].at[index],
        device_id=device, device_id_type=MESH,
    )


def greet(devices):
    barrier = pltpu.get_barrier_semaphore()
    for device in devices:
        pl.semaphore_signal(barrier, inc=1, device_id=device, device_id_type=MESH)
    pl.semaphore_wait(barrier, len(devices))


def gather_kernel(
    x_ref, w_ref, amps_ref, core_ref, xall_ref, wall_ref, far_ref, first_ref, coret_ref, *refs
):
    cuts, (plain, turned, fixed, wsend, wrecv, xsend, xrecv, msend, mrecv, local, tsem) = refs[:-11], refs[-11:]
    r = lax.axis_index("row")
    c = lax.axis_index("col")
    rows = lax.axis_size("row")
    cols = lax.axis_size("col")
    forth = (r, (c + 4) % cols)
    back = (r, (c + cols - 4) % cols)
    mirror = (r, (c + cols // 2) % cols)
    zside = (r, c + 2 - 4 * ((c // 2) % 2))
    twin = (r, c + 1 - 2 * (c % 2))
    beside = r + 1 - 2 * (r % 2)
    core = c % 2
    half = w_ref.shape[0] // 2
    width = plain.shape[1]
    y_steps = range(1, rows // 2)

    amps_in = [pltpu.make_async_copy(amps_ref.at[q], plain.at[q], tsem.at[q]) for q in range(4)]
    core_in = pltpu.make_async_copy(core_ref, fixed.at[0], tsem.at[4])
    for copy in amps_in + [core_in]:
        copy.start()
    greet(
        [forth, back, mirror, zside, twin, (beside, c)]
        + [((r + 2 * step) % rows, c) for step in y_steps]
    )
    wsems, xsems = (wsend, wrecv), (xsend, xrecv)
    started = []

    def send(*args):
        copy = remote(*args)
        copy.start()
        started.append(copy)

    def arrived(part, sems, index):
        remote(part, part, sems, index, twin).wait_recv()

    def shard(offset, plane, side):
        if offset in (1, 2) and plane + side == 0:
            return far_ref.at[offset - 1]
        x = (c // 4 + offset) % (cols // 4)
        z = (c // 2) % 2
        z = z + plane * (1 - 2 * z)
        k = core + side * (1 - 2 * core)
        return wall_ref.at[x * 4 + z * 2 + k]

    def to_twin(offset):
        x = (c // 4 + offset) % (cols // 4)
        send(shard(offset, 0, 0), wall_ref.at[x * 4 + c % 4], wsems, 6 + offset, twin)

    def transpose(q, p):
        amps_in[q].wait()
        for cut in strips(width, 256):
            turned[p, :, cut] = plain[q, cut, :].T

    own = wall_ref.at[c]
    send(w_ref, own, wsems, 0, forth)
    send(w_ref, far_ref.at[0], wsems, 1, back)
    send(w_ref, own, wsems, 4, zside)
    send(x_ref.at[core], xall_ref.at[r, core], xsems, 0, (beside, c))
    for step in y_steps:
        send(x_ref.at[core], xall_ref.at[r, core], xsems, step, ((r + 2 * step) % rows, c))
    send(w_ref, own, wsems, 6, twin)
    own_w = pltpu.make_async_copy(w_ref, own, local.at[0])
    own_x = pltpu.make_async_copy(x_ref, xall_ref.at[r], local.at[1])
    own_w.start()
    own_x.start()
    transpose(0, 0)

    part = xall_ref.at[beside, core]
    arrived(part, xsems, 0)
    for step in y_steps:
        send(part, part, xsems, 3 + step, ((r + 2 * step) % rows, c))
    send(part, part, xsems, 7, twin)

    part = shard(3, 0, 0)
    arrived(part, wsems, 0)
    send(part.at[:half], far_ref.at[1, :half], wsems, 2, forth)
    send(part, part, wsems, 5, zside)
    arrived(far_ref.at[0], wsems, 1)
    send(far_ref.at[0, half:], far_ref.at[1, half:], wsems, 3, back)
    send(turned.at[0], first_ref, (msend, mrecv), 0, mirror)
    to_twin(3)
    to_twin(1)
    transpose(2, 1)
    for step in y_steps:
        origin = (r + rows - 2 * step) % rows
        arrived(xall_ref.at[origin, core], xsems, step)
        send(xall_ref.at[origin, core], xall_ref.at[origin, core], xsems, 7 + step, twin)
    transpose(1, 2)
    part = shard(0, 1, 0)
    arrived(part, wsems, 4)
    send(part, part, wsems, 10, twin)
    for step in y_steps:
        origin = (r + rows - 2 * step) % rows
        origin = origin + 1 - 2 * (origin % 2)
        arrived(xall_ref.at[origin, core], xsems, 3 + step)
        send(xall_ref.at[origin, core], xall_ref.at[origin, core], xsems, 10 + step, twin)
    arrived(far_ref.at[1, :half], wsems, 2)
    arrived(far_ref.at[1, half:], wsems, 3)
    to_twin(2)
    transpose(3, 3)
    outs = [
        pltpu.make_async_copy(
            turned.at[p, :, pl.ds(low, out.shape[1])], out, local.at[2 + at]
        )
        for at, ((p, low), out) in enumerate(zip(((1, 0), (2, 0), (3, 0), (3, cuts[2].shape[1])), cuts))
    ]
    core_in.wait()
    for cut in strips(width, 256):
        fixed[1, :, cut] = fixed[0, cut, :].T
    outs.append(pltpu.make_async_copy(fixed.at[1], coret_ref, local.at[6]))
    for copy in outs:
        copy.start()
    part = shard(3, 1, 0)
    arrived(part, wsems, 5)
    send(part, part, wsems, 11, twin)

    for offset in range(4):
        arrived(shard(offset, 0, 1), wsems, 6 + offset)
    arrived(shard(0, 1, 1), wsems, 10)
    arrived(shard(3, 1, 1), wsems, 11)
    arrived(xall_ref.at[beside, 1 - core], xsems, 7)
    for step in y_steps:
        origin = (r + rows - 2 * step) % rows
        arrived(xall_ref.at[origin, 1 - core], xsems, 7 + step)
        origin = origin + 1 - 2 * (origin % 2)
        arrived(xall_ref.at[origin, 1 - core], xsems, 10 + step)
    remote(turned.at[0], first_ref, (msend, mrecv), 0, mirror).wait_recv()
    for copy in started:
        copy.wait_send()
    for copy in outs + [own_w, own_x]:
        copy.wait()


def gather_parts(x_factor, shard, amp4, core, split):
    rows = lax.axis_size("row")
    cols = lax.axis_size("col")
    width = amp4.shape[1]
    hbm = pl.BlockSpec(memory_space=pl.ANY)
    bf16 = jnp.bfloat16
    dma = pltpu.SemaphoreType.DMA
    shapes = [(rows,) + x_factor.shape, (cols,) + shard.shape, (2,) + shard.shape, (width, width), core.shape]
    shapes += [(width, width)] * 2
    shapes += [(width, split), (width, width - split)]
    return pl.pallas_call(
        gather_kernel,
        out_shape=[jax.ShapeDtypeStruct(shape, bf16) for shape in shapes],
        in_specs=[hbm] * 4,
        out_specs=[hbm] * len(shapes),
        scratch_shapes=[
            pltpu.VMEM(amp4.shape, bf16),
            pltpu.VMEM(amp4.shape, bf16),
            pltpu.VMEM((2,) + core.shape, bf16),
            dma((12,)),
            dma((12,)),
            dma((14,)),
            dma((14,)),
            dma((1,)),
            dma((1,)),
            dma((7,)),
            dma((5,)),
        ],
        compiler_params=pltpu.CompilerParams(
            collective_id=0, has_side_effects=True, vmem_limit_bytes=VMEM_LIMIT
        ),
        name="gather_parts",
    )(x_factor, shard, amp4, core)


def own_ladder_kernel(
    tiles_ref, count_ref, slot_ref, xall_ref, amps_ref, core_ref, x_ref, xt_ref, wt_ref, gathered, proj, sem
):
    @pl.when(pl.program_id(0) == 0)
    def _():
        tile = xall_ref.shape[1]
        copies = []
        for s in range(tiles_ref.shape[0]):
            copy = pltpu.make_async_copy(
                xall_ref.at[slot_ref[tiles_ref[s]]], gathered.at[pl.ds(s * tile, tile), :], sem.at[s]
            )
            copy.start()
            copies.append(copy)
        for copy in copies:
            copy.wait()
        live = lax.broadcasted_iota(jnp.int32, (x_ref.shape[0], 1), 0) < count_ref[0, 0] * tile
        x_ref[...] = jnp.where(live, gathered[...].astype(jnp.float32), 0.0).astype(x_ref.dtype)
        for cut in strips(x_ref.shape[0], 256):
            xt_ref[:, cut] = x_ref[cut, :].T

    proj[...] = dot(xt_ref[...], amps_ref[0]).astype(proj.dtype)
    inner = dot(proj[...], x_ref[...])
    wt_ref[0] = (core_ref[...].astype(jnp.float32) * inner).astype(wt_ref.dtype)


def own_ladder(tiles, count, tile_slot, xall, amp4, core):
    width = amp4.shape[1]
    points = core.shape[0]
    smem = pl.BlockSpec(memory_space=pltpu.SMEM)
    bf16 = jnp.bfloat16

    def whole(shape):
        return pl.BlockSpec(shape, lambda p: (0, 0))

    return pl.pallas_call(
        own_ladder_kernel,
        out_shape=(
            jax.ShapeDtypeStruct((width, points), bf16),
            jax.ShapeDtypeStruct((points, width), bf16),
            jax.ShapeDtypeStruct((4, points, points), bf16),
        ),
        grid=(4,),
        in_specs=[
            smem, smem, smem, pl.BlockSpec(memory_space=pl.ANY),
            pl.BlockSpec((1, width, width), lambda p: (p, 0, 0)), whole((points, points)),
        ],
        out_specs=(
            whole((width, points)), whole((points, width)),
            pl.BlockSpec((1, points, points), lambda p: (p, 0, 0)),
        ),
        scratch_shapes=[
            pltpu.VMEM((width, points), bf16),
            pltpu.VMEM((points, width), bf16),
            pltpu.SemaphoreType.DMA((tiles.shape[0],)),
        ],
        compiler_params=pltpu.CompilerParams(vmem_limit_bytes=VMEM_LIMIT),
        name="own_ladder",
    )(tiles, count, tile_slot, xall, amp4, core)


def window_index(tiles_ref, count_ref, tile, shape, axis):
    at = lax.broadcasted_iota(jnp.int32, shape, axis)
    index = jnp.full(shape, -1, jnp.int32)
    for s in range(tiles_ref.shape[0]):
        inside = (at >= s * tile) & (at < (s + 1) * tile) & (s < count_ref[0, 0])
        index = jnp.where(inside, at + (tiles_ref[s] - s) * tile, index)
    return index


def own_cycle_kernel(
    tiles_ref, count_ref, virt_ref, wall_ref, far_ref, side_ref, twin_ref, a0_ref, a1_ref,
    wd_ref, cyc_ref, vcol_ref, vrow_ref, wsel, pick, sem,
):
    p = pl.program_id(0)
    tile = wall_ref.shape[2]
    slots = tiles_ref.shape[0]
    width = wd_ref.shape[1]
    window = virt_ref.shape[1]

    @pl.when(p == 0)
    def _():
        me = lax.axis_index("col")
        for first in range(2):
            for s in range(slots):
                number = tiles_ref[s]
                offset = ((number >> 2) + 4 - (me >> 2)) & 3
                plane = ((number >> 1) + (me >> 1)) & 1
                side = (number + me) & 1
                apart = (offset == 1) | (offset == 2)
                dst = wsel.at[pl.ds(2 * first, 2), pl.ds(s * tile, tile), :]

                def fetch(source, at, dst=dst, done=sem.at[first, s], first=first):
                    pltpu.make_async_copy(source.at[at, pl.ds(2 * first, 2)], dst, done).start()

                @pl.when(jnp.logical_not(apart) | ((plane == 0) & (side == 1)))
                def _(number=number, fetch=fetch):
                    fetch(wall_ref, number)

                for source, at_plane, at_side in ((far_ref, 0, 0), (side_ref, 1, 0), (twin_ref, 1, 1)):

                    @pl.when(apart & (plane == at_plane) & (side == at_side))
                    def _(source=source, offset=offset, fetch=fetch):
                        fetch(source, offset - 1)

        along = lax.broadcasted_iota(jnp.int32, pick.shape, 0)
        picked = window_index(tiles_ref, count_ref, tile, (1, width), 1)
        pick[...] = jnp.where(along == picked, 1.0, 0.0).astype(pick.dtype)
        picked = window_index(tiles_ref, count_ref, tile, (width, 1), 0)
        along = lax.broadcasted_iota(jnp.int32, (width, window), 1)
        levels = jnp.sum(jnp.where(along == picked, virt_ref[...], 0.0), axis=1, keepdims=True)
        vcol_ref[...] = levels
        vrow_ref[...] = jnp.broadcast_to(levels, (width, 128)).T[:1, :]

    for first in range(2):

        @pl.when(p == 2 * first)
        def _(first=first):
            for s in range(slots):
                pltpu.make_async_copy(
                    wall_ref.at[0, pl.ds(0, 2)],
                    wsel.at[pl.ds(2 * first, 2), pl.ds(s * tile, tile), :],
                    sem.at[first, s],
                ).wait()
            for k in range(2):
                wd_ref[k] = dot(wsel[2 * first + k], pick[...]).astype(wd_ref.dtype)

    cyc_ref[0] = dot(wd_ref[0], a0_ref[0]) + dot(wd_ref[1], a1_ref[0])


def own_cycle(tiles, count, virt, wall, far, side, twin, amp4):
    width = amp4.shape[1]
    slots, window = tiles.shape[0], wall.shape[3]
    smem = pl.BlockSpec(memory_space=pltpu.SMEM)
    hbm = pl.BlockSpec(memory_space=pl.ANY)
    f32, bf16 = jnp.float32, jnp.bfloat16
    return pl.pallas_call(
        own_cycle_kernel,
        out_shape=(
            jax.ShapeDtypeStruct((4, width, width), bf16),
            jax.ShapeDtypeStruct((4, width, width), f32),
            jax.ShapeDtypeStruct((width, 1), f32),
            jax.ShapeDtypeStruct((1, width), f32),
        ),
        grid=(4,),
        in_specs=[
            smem,
            smem,
            pl.BlockSpec((1, window), lambda p: (0, 0)),
            hbm,
            hbm,
            hbm,
            hbm,
            pl.BlockSpec((1, width, width), lambda p: (p % 2, 0, 0)),
            pl.BlockSpec((1, width, width), lambda p: (2 + p % 2, 0, 0)),
        ],
        out_specs=(
            pl.BlockSpec((2, width, width), lambda p: (p // 2, 0, 0)),
            pl.BlockSpec((1, width, width), lambda p: (p, 0, 0)),
            pl.BlockSpec((width, 1), lambda p: (0, 0)),
            pl.BlockSpec((1, width), lambda p: (0, 0)),
        ),
        scratch_shapes=[
            pltpu.VMEM((4, width, window), bf16),
            pltpu.VMEM((window, width), bf16),
            pltpu.SemaphoreType.DMA((2, slots)),
        ],
        compiler_params=pltpu.CompilerParams(vmem_limit_bytes=VMEM_LIMIT),
        name="own_cycle",
    )(tiles, count, virt, wall, far, side, twin, amp4, amp4)


class Mover:
    def __init__(self, plan, in_sem, out_sem):
        self.out_sem = out_sem
        self.outs = []
        self.loads = {}
        for at, (name, (src, dst)) in enumerate(plan.items()):
            self.loads[name] = pltpu.make_async_copy(src, dst, in_sem.at[at])
            self.loads[name].start()

    def need(self, *names):
        for name in names:
            if name in self.loads:
                self.loads.pop(name).wait()

    def put(self, src, dst):
        copy = pltpu.make_async_copy(src, dst, self.out_sem.at[len(self.outs)])
        copy.start()
        self.outs.append(copy)

    def drain(self):
        for copy in self.outs:
            copy.wait()


def emit(mover, last, pair, j, rows, raw, count_ref, occ_ref, vcol_ref, vrow_ref, part, amps, upd, res_hbm, upd_hbm):
    raw = raw + part[j, rows, :]
    if last:
        count = count_ref[0, 0] * 64
        height, width = raw.shape
        live = (lax.broadcasted_iota(jnp.int32, (height, 1), 0) + rows.start < count) & (
            lax.broadcasted_iota(jnp.int32, (1, width), 1) < count
        )
        raw = jnp.where(live, raw, 0.0)
        own = jnp.where(live, amps[j, rows, :].astype(jnp.float32), 0.0)
        gap = (occ_ref[0, pair // 2] + occ_ref[1, pair % 2]) - vcol_ref[rows, :] - vrow_ref[...]
        upd[j, rows, :] = (own + raw / gap).astype(upd.dtype)
        mover.put(upd.at[j, rows, :], upd_hbm.at[pair, rows, :])
    part[j, rows, :] = raw
    mover.put(part.at[j, rows, :], res_hbm.at[pair, rows, :])


def row_kernel(
    i, count_ref, occ_ref, vcol_ref, vrow_ref, b0_hbm, b1_hbm, xt_hbm, x_hbm, coret_hbm, wt_hbm, wd_hbm,
    amps_hbm, part_hbm, res_hbm, upd_hbm, xt, coret, wt, right, left, part, amps, proj, total, upd, sem, osem,
):
    width, points = x_hbm.shape
    head = pl.ds(0, points)
    blocks = [pl.ds(points + k * width, width) for k in range(2)]
    plan = {
        "b0": (b0_hbm, left.at[:, blocks[0]]),
        "xt": (xt_hbm, xt),
        "x0": (x_hbm, right.at[0, :, head]),
        "wt": (wt_hbm.at[pl.ds(2 * i, 2)], wt),
        "coret": (coret_hbm, coret),
        "b1": (b1_hbm, left.at[:, blocks[1]]),
    }
    for j in range(2):
        for k in range(2):
            plan["w%d%d" % (j, k)] = (wd_hbm.at[2 * j + k], right.at[j, :, blocks[k]])
        plan["part%d" % j] = (part_hbm.at[2 * i + j], part.at[j])
        plan["amps%d" % j] = (amps_hbm.at[2 * i + j], amps.at[j])
        if j == 0:
            plan["x1"] = (x_hbm, right.at[1, :, head])
    mover = Mover(plan, sem, osem)
    for j in range(2):
        mover.need("b%d" % j, "xt")
        proj[...] = dot(xt[...], left[:, blocks[j]]).astype(proj.dtype)
        mover.need("x0", "coret", "wt")
        inner = dot(proj[...], right[0, :, head])
        total[j] = (
            wt[j].astype(jnp.float32) + coret[...].astype(jnp.float32) * inner
        ).astype(total.dtype)
    for j in range(2):
        left[:, head] = dot(right[0, :, head], total[j]).astype(left.dtype)
        mover.need("x%d" % j, "w%d0" % j, "w%d1" % j, "part%d" % j, "amps%d" % j)
        for rows in strips(width, STRIP):
            raw = dot_nt(left[rows, :], right[j])
            emit(
                mover, True, 2 * i + j, j, rows, raw, count_ref, occ_ref, vcol_ref, vrow_ref,
                part, amps, upd, res_hbm, upd_hbm,
            )
    mover.drain()


def row(i, count, occ, vcol, vrow, b0, b1, xt, x, coret, wt, wd, amp4, part):
    width, points = x.shape
    vmem = pl.BlockSpec(memory_space=pltpu.VMEM)
    smem = pl.BlockSpec(memory_space=pltpu.SMEM)
    hbm = pl.BlockSpec(memory_space=pl.ANY)
    f32, bf16 = jnp.float32, jnp.bfloat16
    depth = points + 2 * width
    return pl.pallas_call(
        functools.partial(row_kernel, i),
        out_shape=[jax.ShapeDtypeStruct(part.shape, f32), jax.ShapeDtypeStruct(part.shape, bf16)],
        in_specs=[smem, smem, vmem, vmem] + [hbm] * 9,
        out_specs=[hbm] * 2,
        scratch_shapes=[
            pltpu.VMEM((points, width), bf16),
            pltpu.VMEM((points, points), bf16),
            pltpu.VMEM((2, points, points), bf16),
            pltpu.VMEM((2, width, depth), bf16),
            pltpu.VMEM((width, depth), bf16),
            pltpu.VMEM((2, width, width), f32),
            pltpu.VMEM((2, width, width), bf16),
            pltpu.VMEM((points, width), bf16),
            pltpu.VMEM((2, points, points), bf16),
            pltpu.VMEM((2, width, width), bf16),
            pltpu.SemaphoreType.DMA((15,)),
            pltpu.SemaphoreType.DMA((4 * (width // STRIP),)),
        ],
        input_output_aliases={12: 0},
        compiler_params=pltpu.CompilerParams(vmem_limit_bytes=VMEM_LIMIT),
        name="row_%d" % i,
    )(count, occ, vcol, vrow, b0, b1, xt, x, coret, wt, wd, amp4, part)


def piece_kernel(i, k, low, high, end, count_ref, occ_ref, vcol_ref, vrow_ref, *refs):
    last = k == 1 and end
    scratch = 13
    refs, (xt, coret, wt, right, left, part, amps, acc, proj, total, upd, sem, osem) = (
        refs[:-scratch], refs[-scratch:]
    )
    (b_hbm, xt_hbm, x_hbm, coret_hbm, wt_hbm, wd_hbm, amps_hbm, part_hbm) = refs[:8]
    refs = list(refs[8:])
    acc_in = refs.pop(0) if low > 0 else None
    upd_hbm = refs.pop() if last else None
    acc_out = None if end else refs.pop()
    res_hbm = refs.pop()
    width, points = x_hbm.shape
    head, rest = pl.ds(0, points), pl.ds(points, high - low)
    cut = pl.ds(low, high - low)
    plan = {
        "b": (b_hbm, left.at[:, rest]),
        "xt": (xt_hbm, xt),
        "x": (x_hbm, right.at[k, :, head]),
    }
    if low > 0:
        plan["acc"] = (acc_in, acc)
    if end:
        plan["wt"] = (wt_hbm.at[2 * i + k], wt)
        plan["coret"] = (coret_hbm, coret)
    for j in (1 - k, k):
        plan["w%d" % j] = (wd_hbm.at[2 * j + k, :, cut], right.at[j, :, rest])
        plan["part%d" % j] = (part_hbm.at[2 * i + j], part.at[j])
        if last:
            plan["amps%d" % j] = (amps_hbm.at[2 * i + j], amps.at[j])
    mover = Mover(plan, sem, osem)

    def products(j, columns):
        mover.need("w%d" % j, "part%d" % j, "amps%d" % j)
        for rows in strips(width, STRIP):
            raw = dot_nt(left[rows, columns], right[j, :, columns])
            emit(
                mover, last, 2 * i + j, j, rows, raw, count_ref, occ_ref, vcol_ref, vrow_ref,
                part, amps, upd, res_hbm, upd_hbm,
            )

    mover.need("b", "xt")
    proj[...] = dot(xt[...], left[:, rest]).astype(proj.dtype)
    mover.need("x")
    inner = dot(proj[...], right[k, cut, head])
    if low > 0:
        mover.need("acc")
        inner = inner + acc[...]
    if end:
        mover.need("wt", "coret")
        total[...] = (
            wt[...].astype(jnp.float32) + coret[...].astype(jnp.float32) * inner
        ).astype(total.dtype)
        left[:, head] = dot(right[k, :, head], total[...]).astype(left.dtype)
        products(1 - k, rest)
        products(k, pl.ds(0, points + high - low))
    else:
        acc[...] = inner
        mover.put(acc, acc_out)
        for j in (1 - k, k):
            products(j, rest)
    mover.drain()


def piece(i, k, low, high, count, occ, vcol, vrow, b, xt, x, coret, wt, wd, amp4, part, acc, updated):
    width, points = x.shape
    end = high == width
    last = k == 1 and end
    vmem = pl.BlockSpec(memory_space=pltpu.VMEM)
    smem = pl.BlockSpec(memory_space=pltpu.SMEM)
    hbm = pl.BlockSpec(memory_space=pl.ANY)
    f32, bf16 = jnp.float32, jnp.bfloat16
    operands = [count, occ, vcol, vrow, b, xt, x, coret, wt, wd, amp4, part]
    out_shape = [jax.ShapeDtypeStruct(part.shape, f32)]
    alias = {len(operands) - 1: 0}
    if low > 0:
        operands.append(acc)
    if not end:
        out_shape.append(jax.ShapeDtypeStruct((points, points), f32))
    if last:
        out_shape.append(jax.ShapeDtypeStruct(part.shape, bf16))
        alias[len(operands)] = 1
        operands.append(updated)
    return pl.pallas_call(
        functools.partial(piece_kernel, i, k, low, high, end),
        out_shape=out_shape,
        in_specs=[smem, smem, vmem, vmem] + [hbm] * (len(operands) - 4),
        out_specs=[hbm] * len(out_shape),
        scratch_shapes=[
            pltpu.VMEM((points, width), bf16),
            pltpu.VMEM((points, points), bf16),
            pltpu.VMEM((points, points), bf16),
            pltpu.VMEM((2, width, points + high - low), bf16),
            pltpu.VMEM((width, points + high - low), bf16),
            pltpu.VMEM((2, width, width), f32),
            pltpu.VMEM((2, width, width), bf16),
            pltpu.VMEM((points, points), f32),
            pltpu.VMEM((points, high - low), bf16),
            pltpu.VMEM((points, points), bf16),
            pltpu.VMEM((2, width, width), bf16),
            pltpu.SemaphoreType.DMA((12,)),
            pltpu.SemaphoreType.DMA((9,)),
        ],
        input_output_aliases=alias,
        compiler_params=pltpu.CompilerParams(vmem_limit_bytes=VMEM_LIMIT),
        name="piece_%d%d_%d" % (i, k, low),
    )(*operands)


def per_device(
    amps, x_factor, core, cycle_w, domain_tiles, domain_count, tile_slot, occ_energy, virt_energy
):
    occ = amps.shape[2]
    width = amps.shape[4]
    tile_width = x_factor.shape[1]
    grid_points = x_factor.shape[2]
    window = cycle_w.shape[4]
    cols = lax.axis_size("col")
    amp4 = amps[0, 0].reshape(occ * occ, width, width)
    shard = cycle_w[0].reshape(occ * occ, tile_width, window)

    split = 512
    xall, wall, far, first, coret, *turned = gather_parts(x_factor, shard, amp4, core, split)
    xall = xall.reshape(-1, tile_width, grid_points)
    side = lax.ppermute(far, "col", [(i, i ^ 2) for i in range(cols)])
    mirror = [(i, (i + cols // 2) % cols) for i in range(cols)]
    second, third, fourth = [lax.ppermute(part, "col", mirror) for part in turned[:3]]

    tiles, count = domain_tiles[0, 0], domain_count
    x, xt, wt = own_ladder(tiles, count, tile_slot, xall, amp4, core)
    side, tail, wt = lax.optimization_barrier((side, turned[3], wt))
    fifth = lax.ppermute(tail, "col", mirror)
    twin = lax.ppermute(side, "col", [(i, i ^ 1) for i in range(cols)])
    wd, part, vcol, vrow = own_cycle(tiles, count, virt_energy[None, :], wall, far, side, twin, amp4)
    energies = (count, occ_energy[0, 0], vcol, vrow)
    part, updated = row(0, *energies, first, second, xt, x, coret, wt, wd, amp4, part)
    fixed = (xt, x, coret, wt, wd, amp4)
    part, = piece(1, 0, 0, width, *energies, third, *fixed, part, None, None)
    part, acc = piece(1, 1, 0, split, *energies, fourth, *fixed, part, None, None)
    part, updated = piece(1, 1, split, width, *energies, fifth, *fixed, part, acc, updated)
    return part.reshape(amps.shape), updated.reshape(amps.shape)


def solution(mesh):
    in_specs = (
        P("row", "col", None, None, None, None),
        P("row", None, None),
        P(),
        P("row", None, None, "col", None),
        P("row", "col", None),
        P("row", "col"),
        P(),
        P("row", "col", None, None),
        P(),
    )
    out_specs = (P("row", "col", None, None, None, None), P("row", "col", None, None, None, None))
    return jax.shard_map(
        per_device, mesh=mesh, in_specs=in_specs, out_specs=out_specs, check_vma=False
    )
```

time: 170 us -> 156 us (0.918); the launches traced: 170 us -> 154 us
  Pallas kernels: 146 us -> 134 us
  local copies, waits for them, and re-layouts: 12.8 us -> 4.68 us
  waiting for transfers between devices: 0.01 us -> 4.98 us
  other arithmetic: 2.46 us -> 0 us
    pallas_call x5 -> x3, Pallas kernels: 54.3 us -> 29.1 us  [piece(): pl.pallas_call(functools.partial(piece_kernel, i, k, low, high, end), out...]
    pallas_call x0 -> x1, Pallas kernels: none -> 17.8 us  [row(): pl.pallas_call(functools.partial(row_kernel, i), out_shape=[jax.ShapeDtyp...]
    ppermute x4 -> x6, waiting for transfers between devices: 0.01 us -> 4.98 us  [the longest x1 4.96 us: per_device(): side = lax.ppermute(far, 'col', [(i, i ^ 2) for i in range(cols)])]
    gather x2 -> x0, local copies, waits for them, and re-layouts: 4.49 us -> none  [the longest x1 3.32 us: per_device(): virt_levels = virt_energy[window_index]]
    pallas_call x1, Pallas kernels: 58.5 us -> 54.2 us  [gather_parts(): pl.pallas_call(gather_kernel, out_shape=[jax.ShapeDtypeStruct(shape, bf16...]
    unnamed x12 -> x16, local copies, waits for them, and re-layouts: 2.07 us -> 4.68 us
    select_n x3 -> x0, other arithmetic: 1.85 us -> none  [the longest x1 1.32 us: per_device(): picked = jnp.where(row_live, window_index, -1)[None, :]]
    convert_element_type x2 -> x0, local copies, waits for them, and re-layouts: 1.79 us -> none  [per_device(): mask = row_live.astype(jnp.float32)]
  transfers between devices with their start and end apart: 4 -> 6, of which waited for: 0 -> 1; matrix products, arithmetic and copies ran while one was open for 8% -> 0% of each run, Pallas kernels for 44% -> 46%
where the time goes in v3:
time: 156 us; the launch traced here: 154 us
  Pallas kernels  134 us (86%)
  starting transfers between devices  8.24 us (5%)
  waiting for transfers between devices  4.98 us (3%)
  local copies, waits for them, and re-layouts  4.68 us (3%)
  between operations  1.6 us (1%)
    pallas_call x1, Pallas kernels, gather_parts(): pl.pallas_call(gather_kernel, out_shape=[jax.ShapeDtypeStruct(shape, bf16...  54.2 us
    pallas_call x3, Pallas kernels, piece(): pl.pallas_call(functools.partial(piece_kernel, i, k, low, high, end), out...  29.1 us
    pallas_call x1, Pallas kernels, own_cycle(): pl.pallas_call(own_cycle_kernel, out_shape=(jax.ShapeDtypeStruct((4, widt...  19.9 us
    pallas_call x1, Pallas kernels, row(): pl.pallas_call(functools.partial(row_kernel, i), out_shape=[jax.ShapeDtyp...  17.8 us
    pallas_call x1, Pallas kernels, own_ladder(): pl.pallas_call(own_ladder_kernel, out_shape=(jax.ShapeDtypeStruct((width,...  13.1 us
    ppermute x3, starting transfers between devices, per_device(): lax.ppermute(part, 'col', mirror)  5.73 us
    ppermute x1, waiting for transfers between devices, per_device(): side = lax.ppermute(far, 'col', [(i, i ^ 2) for i in range(cols)])  4.96 us
    unnamed x16, local copies, waits for them, and re-layouts  4.68 us
  transfers between devices with their start and end apart: 6, of which 1 were waited for; matrix products, arithmetic and copies ran while one was open for 0% of the time, Pallas kernels for 46%

profile of v3, /device:TPU:6, one launch (start us, length us, event | category | flops | bytes accessed | tf_op | source)
XLA Modules:
  0.0 153.5 jit_solution(3648849780751361471)
XLA Ops:
  0.6 54.2 %gather_parts.1 = (bf16[8,2,64,768]{3,2,1,0:T(8,128)(2,1)}, bf16[16,4,64,1024]{3,2,1,0:T(8,128)(2,1)}, bf16[2,4,64,1024]{3,2,1,0:T(8,128)(2,1)}, bf16[768,768]{1...) custom-call(bf16[2,64,768]{2,1,0:T(8,128)(2,1)} %x_ref.1, ...), custom_call_target="tpu_custom_call" | custom-call | tf_op jit(solution)/shard_map/gather_parts/pallas_call | solution.py:187
  54.8 0.0 copy-start.6
  54.8 0.0 copy-start.7
  54.8 1.1 collective-permute-start
  55.9 2.1 %collective-permute-start.5 = (bf16[768,768]{1,0:T(8,128)(2,1)}, bf16[768,768]{1,0:T(8,128)(2,1)S(1)}, u32[]{:S(2)}, u32[]{:S(2)}) collective-permute-start(bf16[768,768]{1,0:T(8,128)(2,1)} %get-tuple-element.44), channel_id=1, source_target_pairs={{0,8},{1,9},{2,10},{3,11},{4,12},{5,13},{6,14},{7,15},{8,0},{9,1},... | collective-permute-start | bytes 3538952 | tf_op jit(solution)/shard_map/ppermute | solution.py:625
  58.0 1.4 collective-permute-start.4
  60.1 13.1 %own_ladder.1 = (bf16[768,768]{1,0:T(8,128)(2,1)}, bf16[768,768]{1,0:T(8,128)(2,1)}, bf16[4,768,768]{2,1,0:T(8,128)(2,1)}) custom-call(s32[12]{0:T(128)} %bitcast.25, s32[1,1]{1,0:T(1,128)S(6)} %copy.21.count_ref, s32[16]{0:T(128)} %slot_ref.1, bf16[16,64,768]{2,1,0:T(8,128)(2,1)} %bitcast.18, bf16[4,768,768]{2,1,0:T(8,128)(2,1)} %bitcast.9, ...), custom_call_target="tpu_custom_call" | custom-call | tf_op jit(solution)/shard_map/own_ladder/pallas_call | solution.py:246
  73.2 5.0 %collective-permute-done.side_ref = bf16[2,4,64,1024]{3,2,1,0:T(8,128)(2,1)S(1)} collective-permute-done((bf16[2,4,64,1024]{3,2,1,0:T(8,128)(2,1)}, bf16[2,4,64,1024]{3,2,1,0:T(8,128)(2,1)S(1)}, u32[]{:S(2)}, u32[]{:S(2)}) %collective-permute-start) | collective-permute-done | bytes 1048608 | tf_op jit(solution)/shard_map/ppermute | solution.py:623
  78.2 0.0 copy-start.2
  78.2 0.0 collective-permute-start.1
  78.2 0.0 copy-done.6
  78.2 2.2 %collective-permute-start.3 = (bf16[768,512]{1,0:T(8,128)(2,1)S(1)}, bf16[768,512]{1,0:T(8,128)(2,1)S(1)}, u32[]{:S(2)}, u32[]{:S(2)}) collective-permute-start(bf16[768,512]{1,0:T(8,128)(2,1)S(1)} %copy-done.6), channel_id=1, source_target_pairs={{0,8},{1,9},{2,10},{3,11},{4,12},{5,13},{6,14},{7,15},{8,0},{9,1},... | collective-permute-start | bytes 2359304 | tf_op jit(solution)/shard_map/ppermute | solution.py:625
  80.4 0.0 copy-done.7
  80.4 1.4 collective-permute-start.2
  81.8 0.0 collective-permute-done.1.twin_ref
  81.8 0.0 copy-start.3
  81.8 0.0 copy-done.2
  81.8 0.9 copy-done.3
  82.8 19.9 %own_cycle.1 = (bf16[4,768,768]{2,1,0:T(8,128)(2,1)}, f32[4,768,768]{2,1,0:T(8,128)}, f32[768,1]{1,0:T(8,128)}, f32[1,768]{1,0:T(1,128)}) custom-call(s32[12]{0:T(128)} %bitcast.26, s32[1,1]{1,0:T(1,128)S(6)} %copy.21.count_ref, f32[1,1024]{1,0:T(1,128)} %bitcast.24, bf16[16,4,64,1024]{3,2,1,0:T(8,128)(2,1)} %get-tuple-element.27.wall_ref, ...), custom_call_target="tpu_custom_call" | custom-call | tf_op jit(solution)/shard_map/own_cycle/pallas_call | solution.py:347
  102.6 0.0 collective-permute-done.5.b1_hbm
  102.7 0.0 copy-start.1
  102.7 1.0 copy-done.1
  103.7 17.8 %row_0.1 = (f32[4,768,768]{2,1,0:T(8,128)}, bf16[4,768,768]{2,1,0:T(8,128)(2,1)}) custom-call(s32[1,1]{1,0:T(1,128)S(6)} %copy.21.count_ref, f32[2,2]{1,0:T(2,128)} %bitcast.20, f32[768,1]{1,0:T(8,128)} %get-tuple-element.33.vcol_ref, f32[1,768]{1,0:T(1,128)} %get-tuple-element.34.vrow_ref, ...), custom_call_target="tpu_custom_call", output_to_operand_aliasing={{0}: (12, {})} | custom-call | tf_op jit(solution)/shard_map/row_0/pallas_call | solution.py:474
  121.5 0.0 collective-permute-done.4.refs_0_
  121.5 0.0 copy-start
  121.5 1.0 copy-done
  122.6 11.7 %piece_10_0.1.refs_7_ = f32[4,768,768]{2,1,0:T(8,128)} custom-call(s32[1,1]{1,0:T(1,128)S(6)} %copy.21.count_ref, f32[2,2]{1,0:T(2,128)} %bitcast.21, f32[768,1]{1,0:T(8,128)} %get-tuple-element.33.vcol_ref, f32[1,768]{1,0:T(1,128)} %get-tuple-element.34.vrow_ref, bf16[768,768]{1,0:T(8,128)(2,1)} %copy-done, ...), custom_call_target="tpu_custom_call", output_to_operand_aliasing={{}: (11, {})} | custom-call | tf_op jit(solution)/shard_map/piece_10_0/pallas_call | solution.py:582
  134.2 0.0 collective-permute-done.3.refs_0_
  134.2 0.0 copy-start.4
  134.3 0.9 copy-done.4
  135.1 7.4 %piece_11_0.1 = (f32[4,768,768]{2,1,0:T(8,128)}, f32[768,768]{1,0:T(8,128)}) custom-call(s32[1,1]{1,0:T(1,128)S(6)} %copy.21.count_ref, f32[2,2]{1,0:T(2,128)} %bitcast.22, f32[768,1]{1,0:T(8,128)} %get-tuple-element.33.vcol_ref, f32[1,768]{1,0:T(1,128)} %get-tuple-element.34.vrow_ref, bf16[768,512]{1,0:T(8,128)(2,1)} %copy-done.4, ...), custom_call_target="tpu_custom_call", output_to_operand_aliasing={{0}: (11, {})} | custom-call | tf_op jit(solution)/shard_map/piece_11_0/pallas_call | solution.py:582
  142.6 0.0 collective-permute-done.2.refs_0_
  142.6 0.0 copy-start.5
  142.6 0.8 copy-done.5
  143.4 10.0 %piece_11_512.1 = (f32[4,768,768]{2,1,0:T(8,128)}, bf16[4,768,768]{2,1,0:T(8,128)(2,1)}) custom-call(s32[1,1]{1,0:T(1,128)S(6)} %copy.21.count_ref, f32[2,2]{1,0:T(2,128)} %bitcast.23, f32[768,1]{1,0:T(8,128)} %get-tuple-element.33.vcol_ref, f32[1,768]{1,0:T(1,128)} %get-tuple-element.34.vrow_ref, ...), custom_call_target="tpu_custom_call", output_to_operand_aliasing={{0}: (11, {}), {1}: (13, {})} | custom-call | tf_op jit(solution)/shard_map/piece_11_512/pallas_call | solution.py:582
Async XLA Ops:
  54.8 23.4 %copy-start.6 = (bf16[768,512]{1,0:T(8,128)(2,1)S(1)}, bf16[768,512]{1,0:T(8,128)(2,1)}, u32[]{:S(2)}) copy-start(bf16[768,512]{1,0:T(8,128)(2,1)} %get-tuple-element.41) | copy-start | bytes 2359300
  54.8 25.6 %copy-start.7 = (bf16[768,256]{1,0:T(8,128)(2,1)S(1)}, bf16[768,256]{1,0:T(8,128)(2,1)}, u32[]{:S(2)}) copy-start(bf16[768,256]{1,0:T(8,128)(2,1)} %get-tuple-element.35) | copy-start | bytes 1179652
  54.8 23.4 %collective-permute-start = (bf16[2,4,64,1024]{3,2,1,0:T(8,128)(2,1)}, bf16[2,4,64,1024]{3,2,1,0:T(8,128)(2,1)S(1)}, u32[]{:S(2)}, u32[]{:S(2)}) collective-permute-start(bf16[2,4,64,1024]{3,2,1,0:T(8,128)(2,1)} %get-tuple-element.28.far_ref), channel_id=1, source_target_pairs={{0,2},{1,3},{2,0},{3,1},{4,6},{5,7},{6,4},{7,5},{8,10},{9,11},{10,... | collective-permute-start | bytes 3145736 | tf_op jit(solution)/shard_map/ppermute | solution.py:623
  55.9 46.7 %collective-permute-start.5 = (bf16[768,768]{1,0:T(8,128)(2,1)}, bf16[768,768]{1,0:T(8,128)(2,1)S(1)}, u32[]{:S(2)}, u32[]{:S(2)}) collective-permute-start(bf16[768,768]{1,0:T(8,128)(2,1)} %get-tuple-element.44), channel_id=1, source_target_pairs={{0,8},{1,9},{2,10},{3,11},{4,12},{5,13},{6,14},{7,15},{8,0},{9,1},... | collective-permute-start | bytes 3538952 | tf_op jit(solution)/shard_map/ppermute | solution.py:625
  58.0 63.5 %collective-permute-start.4 = (bf16[768,768]{1,0:T(8,128)(2,1)}, bf16[768,768]{1,0:T(8,128)(2,1)S(1)}, u32[]{:S(2)}, u32[]{:S(2)}) collective-permute-start(bf16[768,768]{1,0:T(8,128)(2,1)} %get-tuple-element.42), channel_id=1, source_target_pairs={{0,8},{1,9},{2,10},{3,11},{4,12},{5,13},{6,14},{7,15},{8,0},{9,1},... | collective-permute-start | bytes 3538952 | tf_op jit(solution)/shard_map/ppermute | solution.py:625
  78.2 3.6 %copy-start.2 = (bf16[2,4,64,1024]{3,2,1,0:T(8,128)(2,1)}, bf16[2,4,64,1024]{3,2,1,0:T(8,128)(2,1)S(1)}, u32[]{:S(2)}) copy-start(bf16[2,4,64,1024]{3,2,1,0:T(8,128)(2,1)S(1)} %collective-permute-done.side_ref) | copy-start | bytes 3145732
  78.2 3.6 %collective-permute-start.1 = (bf16[2,4,64,1024]{3,2,1,0:T(8,128)(2,1)S(1)}, bf16[2,4,64,1024]{3,2,1,0:T(8,128)(2,1)S(1)}, u32[]{:S(2)}, u32[]{:S(2)}) collective-permute-start(bf16[2,4,64,1024]{3,2,1,0:T(8,128)(2,1)S(1)} %collective-permute-done.side_ref), channel_id=1, source_target_pairs={{0,1},{1,0},{2,3},{3,2},{4,5},{5,4},{6,7},{7,6},{8,9},{9,8},{10,11... | collective-permute-start | bytes 3145736 | tf_op jit(solution)/shard_map/ppermute | solution.py:631
  78.2 56.0 %collective-permute-start.3 = (bf16[768,512]{1,0:T(8,128)(2,1)S(1)}, bf16[768,512]{1,0:T(8,128)(2,1)S(1)}, u32[]{:S(2)}, u32[]{:S(2)}) collective-permute-start(bf16[768,512]{1,0:T(8,128)(2,1)S(1)} %copy-done.6), channel_id=1, source_target_pairs={{0,8},{1,9},{2,10},{3,11},{4,12},{5,13},{6,14},{7,15},{8,0},{9,1},... | collective-permute-start | bytes 2359304 | tf_op jit(solution)/shard_map/ppermute | solution.py:625
  80.4 62.2 %collective-permute-start.2 = (bf16[768,256]{1,0:T(8,128)(2,1)S(1)}, bf16[768,256]{1,0:T(8,128)(2,1)S(1)}, u32[]{:S(2)}, u32[]{:S(2)}) collective-permute-start(bf16[768,256]{1,0:T(8,128)(2,1)S(1)} %copy-done.7), channel_id=1, source_target_pairs={{0,8},{1,9},{2,10},{3,11},{4,12},{5,13},{6,14},{7,15},{8,0},{9,1},... | collective-permute-start | bytes 1179656 | tf_op jit(solution)/shard_map/ppermute | solution.py:630
  81.8 1.0 copy-start.3
  102.7 1.1 copy-start.1
  121.5 1.1 copy-start
  134.2 0.9 copy-start.4
  142.6 0.8 copy-start.5

commit v4 on v3

--- a/solution.py
+++ b/solution.py
@@ -8,7 +8,7 @@
 from jax.sharding import PartitionSpec as P
 
 MESH = pl.DeviceIdType.MESH
-VMEM_LIMIT = 56 * 1024 * 1024
+VMEM_LIMIT = 65300 * 1024
 STRIP = 384
 
 
@@ -97,8 +97,8 @@
     own = wall_ref.at[c]
     send(w_ref, own, wsems, 0, forth)
     send(w_ref, far_ref.at[0], wsems, 1, back)
+    send(x_ref.at[core], xall_ref.at[r, core], xsems, 0, (beside, c))
     send(w_ref, own, wsems, 4, zside)
-    send(x_ref.at[core], xall_ref.at[r, core], xsems, 0, (beside, c))
     for step in y_steps:
         send(x_ref.at[core], xall_ref.at[r, core], xsems, step, ((r + 2 * step) % rows, c))
     send(w_ref, own, wsems, 6, twin)
@@ -120,7 +120,7 @@
     send(part, part, wsems, 5, zside)
     arrived(far_ref.at[0], wsems, 1)
     send(far_ref.at[0, half:], far_ref.at[1, half:], wsems, 3, back)
-    send(turned.at[0], first_ref, (msend, mrecv), 0, mirror)
+    send(turned.at[0, :, pl.ds(0, first_ref.shape[1])], first_ref, (msend, mrecv), 0, mirror)
     to_twin(3)
     to_twin(1)
     transpose(2, 1)
@@ -141,16 +141,22 @@
     arrived(far_ref.at[1, half:], wsems, 3)
     to_twin(2)
     transpose(3, 3)
+    early, split = first_ref.shape[1], cuts[2].shape[1]
+    moves = (
+        (0, pl.ds(early, width - early), 0, pl.ds(0, width - early)),
+        (1, pl.ds(0, width), 0, pl.ds(width - early, width)),
+        (2, pl.ds(0, width), 1, pl.ds(0, width)),
+        (3, pl.ds(0, split), 2, pl.ds(0, split)),
+        (3, pl.ds(split, width - split), 3, pl.ds(0, width - split)),
+    )
     outs = [
-        pltpu.make_async_copy(
-            turned.at[p, :, pl.ds(low, out.shape[1])], out, local.at[2 + at]
-        )
-        for at, ((p, low), out) in enumerate(zip(((1, 0), (2, 0), (3, 0), (3, cuts[2].shape[1])), cuts))
+        pltpu.make_async_copy(turned.at[p, :, source], cuts[q].at[:, target], local.at[3 + at])
+        for at, (p, source, q, target) in enumerate(moves)
     ]
     core_in.wait()
     for cut in strips(width, 256):
         fixed[1, :, cut] = fixed[0, cut, :].T
-    outs.append(pltpu.make_async_copy(fixed.at[1], coret_ref, local.at[6]))
+    outs.append(pltpu.make_async_copy(fixed.at[1], coret_ref, local.at[2]))
     for copy in outs:
         copy.start()
     part = shard(3, 1, 0)
@@ -167,22 +173,22 @@
         arrived(xall_ref.at[origin, 1 - core], xsems, 7 + step)
         origin = origin + 1 - 2 * (origin % 2)
         arrived(xall_ref.at[origin, 1 - core], xsems, 10 + step)
-    remote(turned.at[0], first_ref, (msend, mrecv), 0, mirror).wait_recv()
+    remote(first_ref, first_ref, (msend, mrecv), 0, mirror).wait_recv()
     for copy in started:
         copy.wait_send()
     for copy in outs + [own_w, own_x]:
         copy.wait()
 
 
-def gather_parts(x_factor, shard, amp4, core, split):
+def gather_parts(x_factor, shard, amp4, core, early, split):
     rows = lax.axis_size("row")
     cols = lax.axis_size("col")
     width = amp4.shape[1]
     hbm = pl.BlockSpec(memory_space=pl.ANY)
     bf16 = jnp.bfloat16
     dma = pltpu.SemaphoreType.DMA
-    shapes = [(rows,) + x_factor.shape, (cols,) + shard.shape, (2,) + shard.shape, (width, width), core.shape]
-    shapes += [(width, width)] * 2
+    shapes = [(rows,) + x_factor.shape, (cols,) + shard.shape, (2,) + shard.shape, (width, early), core.shape]
+    shapes += [(width, 2 * width - early), (width, width)]
     shapes += [(width, split), (width, width - split)]
     return pl.pallas_call(
         gather_kernel,
@@ -199,7 +205,7 @@
             dma((14,)),
             dma((1,)),
             dma((1,)),
-            dma((7,)),
+            dma((8,)),
             dma((5,)),
         ],
         compiler_params=pltpu.CompilerParams(
@@ -426,15 +432,16 @@
     amps_hbm, part_hbm, res_hbm, upd_hbm, xt, coret, wt, right, left, part, amps, proj, total, upd, sem, osem,
 ):
     width, points = x_hbm.shape
+    early = b0_hbm.shape[1]
     head = pl.ds(0, points)
     blocks = [pl.ds(points + k * width, width) for k in range(2)]
     plan = {
-        "b0": (b0_hbm, left.at[:, blocks[0]]),
+        "b0": (b0_hbm, left.at[:, pl.ds(points, early)]),
+        "b1": (b1_hbm, left.at[:, pl.ds(points + early, 2 * width - early)]),
         "xt": (xt_hbm, xt),
         "x0": (x_hbm, right.at[0, :, head]),
         "wt": (wt_hbm.at[pl.ds(2 * i, 2)], wt),
         "coret": (coret_hbm, coret),
-        "b1": (b1_hbm, left.at[:, blocks[1]]),
     }
     for j in range(2):
         for k in range(2):
@@ -445,7 +452,7 @@
             plan["x1"] = (x_hbm, right.at[1, :, head])
     mover = Mover(plan, sem, osem)
     for j in range(2):
-        mover.need("b%d" % j, "xt")
+        mover.need("b0", "b1", "xt")
         proj[...] = dot(xt[...], left[:, blocks[j]]).astype(proj.dtype)
         mover.need("x0", "coret", "wt")
         inner = dot(proj[...], right[0, :, head])
@@ -617,12 +624,12 @@
     amp4 = amps[0, 0].reshape(occ * occ, width, width)
     shard = cycle_w[0].reshape(occ * occ, tile_width, window)
 
-    split = 512
-    xall, wall, far, first, coret, *turned = gather_parts(x_factor, shard, amp4, core, split)
+    early, split = width // 2, 512
+    xall, wall, far, first, coret, *turned = gather_parts(x_factor, shard, amp4, core, early, split)
     xall = xall.reshape(-1, tile_width, grid_points)
-    side = lax.ppermute(far, "col", [(i, i ^ 2) for i in range(cols)])
     mirror = [(i, (i + cols // 2) % cols) for i in range(cols)]
     second, third, fourth = [lax.ppermute(part, "col", mirror) for part in turned[:3]]
+    side = lax.ppermute(far, "col", [(i, i ^ 2) for i in range(cols)])
 
     tiles, count = domain_tiles[0, 0], domain_count
     x, xt, wt = own_ladder(tiles, count, tile_slot, xall, amp4, core)

time: 156 us -> 146 us (0.936); the launches traced: 154 us -> 146 us
  Pallas kernels: 134 us -> 121 us
  waiting for transfers between devices: 4.98 us -> 15.5 us
  local copies, waits for them, and re-layouts: 4.68 us -> 0 us
    pallas_call x1, Pallas kernels: 54.2 us -> 40.9 us  [gather_parts(): pl.pallas_call(gather_kernel, out_shape=[jax.ShapeDtypeStruct(shape, bf16...]
    ppermute x3, waiting for transfers between devices: 0.01 us -> 8.22 us  [per_device(): lax.ppermute(part, 'col', mirror)]
    unnamed x16 -> x0, local copies, waits for them, and re-layouts: 4.68 us -> none
    ppermute x1, waiting for transfers between devices: 4.96 us -> 7.18 us  [per_device(): side = lax.ppermute(far, 'col', [(i, i ^ 2) for i in range(cols)])]
    ppermute x3, starting transfers between devices: 5.73 us -> 3.53 us  [per_device(): lax.ppermute(part, 'col', mirror)]
    ppermute x1, starting transfers between devices: 1.41 us -> 3.53 us  [per_device(): fifth = lax.ppermute(tail, 'col', mirror)]
  transfers between devices with their start and end apart: 6 -> 6, of which waited for: 1 -> 4; matrix products, arithmetic and copies ran while one was open for 0% -> 0% of each run, Pallas kernels for 46% -> 48%
where the time goes in v4:
time: 146 us
  Pallas kernels  121 us (83%)
  waiting for transfers between devices  15.5 us (11%)
  starting transfers between devices  8.41 us (6%)
  between operations  1.52 us (1%)
    pallas_call x1, Pallas kernels, gather_parts(): pl.pallas_call(gather_kernel, out_shape=[jax.ShapeDtypeStruct(shape, bf16...  40.9 us
    pallas_call x3, Pallas kernels, piece(): pl.pallas_call(functools.partial(piece_kernel, i, k, low, high, end), out...  29.1 us
    pallas_call x1, Pallas kernels, own_cycle(): pl.pallas_call(own_cycle_kernel, out_shape=(jax.ShapeDtypeStruct((4, widt...  19.9 us
    pallas_call x1, Pallas kernels, row(): pl.pallas_call(functools.partial(row_kernel, i), out_shape=[jax.ShapeDtyp...  17.6 us
    pallas_call x1, Pallas kernels, own_ladder(): pl.pallas_call(own_ladder_kernel, out_shape=(jax.ShapeDtypeStruct((width,...  13.1 us
    ppermute x3, waiting for transfers between devices, per_device(): lax.ppermute(part, 'col', mirror)  8.22 us
    ppermute x1, waiting for transfers between devices, per_device(): side = lax.ppermute(far, 'col', [(i, i ^ 2) for i in range(cols)])  7.18 us
    ppermute x3, starting transfers between devices, per_device(): lax.ppermute(part, 'col', mirror)  3.53 us
  transfers between devices with their start and end apart: 6, of which 4 were waited for; matrix products, arithmetic and copies ran while one was open for 0% of the time, Pallas kernels for 48%

profile of v4, /device:TPU:6, one launch (start us, length us, event | category | flops | bytes accessed | tf_op | source)
XLA Modules:
  0.0 146.0 jit_solution(2025267734615638452)
XLA Ops:
  0.6 40.9 %gather_parts.1 = (bf16[8,2,64,768]{3,2,1,0:T(8,128)(2,1)}, bf16[16,4,64,1024]{3,2,1,0:T(8,128)(2,1)}, bf16[2,4,64,1024]{3,2,1,0:T(8,128)(2,1)}, bf16[768,384]{1...) custom-call(bf16[2,64,768]{2,1,0:T(8,128)(2,1)} %x_ref.1, ...), custom_call_target="tpu_custom_call" | custom-call | tf_op jit(solution)/shard_map/gather_parts/pallas_call | solution.py:193
  41.6 1.3 collective-permute-start
  42.9 0.0 collective-permute-start.5
  42.9 3.5 %collective-permute-start.4 = (bf16[768,768]{1,0:T(8,128)(2,1)}, bf16[768,768]{1,0:T(8,128)(2,1)}, u32[]{:S(2)}, u32[]{:S(2)}) collective-permute-start(bf16[768,768]{1,0:T(8,128)(2,1)} %get-tuple-element.42), channel_id=1, source_target_pairs={{0,8},{1,9},{2,10},{3,11},{4,12},{5,13},{6,14},{7,15},{8,0},{9,1},... | collective-permute-start | bytes 3538952 | tf_op jit(solution)/shard_map/ppermute | solution.py:631
  47.1 13.1 %own_ladder.1 = (bf16[768,768]{1,0:T(8,128)(2,1)}, bf16[768,768]{1,0:T(8,128)(2,1)}, bf16[4,768,768]{2,1,0:T(8,128)(2,1)}) custom-call(s32[12]{0:T(128)} %bitcast.25, s32[1,1]{1,0:T(1,128)S(6)} %copy.21.count_ref, s32[16]{0:T(128)} %slot_ref.1, bf16[16,64,768]{2,1,0:T(8,128)(2,1)} %bitcast.18, bf16[4,768,768]{2,1,0:T(8,128)(2,1)} %bitcast.9, ...), custom_call_target="tpu_custom_call" | custom-call | tf_op jit(solution)/shard_map/own_ladder/pallas_call | solution.py:252
  60.2 7.2 %collective-permute-done.side_ref = bf16[2,4,64,1024]{3,2,1,0:T(8,128)(2,1)} collective-permute-done((bf16[2,4,64,1024]{3,2,1,0:T(8,128)(2,1)}, bf16[2,4,64,1024]{3,2,1,0:T(8,128)(2,1)}, u32[]{:S(2)}, u32[]{:S(2)}) %collective-permute-start) | collective-permute-done | bytes 1048608 | tf_op jit(solution)/shard_map/ppermute | solution.py:632
  67.4 0.0 collective-permute-start.1
  67.4 0.0 collective-permute-start.3
  67.4 3.5 %collective-permute-start.2 = (bf16[768,256]{1,0:T(8,128)(2,1)}, bf16[768,256]{1,0:T(8,128)(2,1)}, u32[]{:S(2)}, u32[]{:S(2)}) collective-permute-start(bf16[768,256]{1,0:T(8,128)(2,1)} %get-tuple-element.35), channel_id=1, source_target_pairs={{0,8},{1,9},{2,10},{3,11},{4,12},{5,13},{6,14},{7,15},{8,0},{9,1},... | collective-permute-start | bytes 1179656 | tf_op jit(solution)/shard_map/ppermute | solution.py:637
  70.9 0.0 collective-permute-done.1.twin_ref
  70.9 19.9 %own_cycle.1 = (bf16[4,768,768]{2,1,0:T(8,128)(2,1)}, f32[4,768,768]{2,1,0:T(8,128)}, f32[768,1]{1,0:T(8,128)}, f32[1,768]{1,0:T(1,128)}) custom-call(s32[12]{0:T(128)} %bitcast.26, s32[1,1]{1,0:T(1,128)S(6)} %copy.21.count_ref, f32[1,1024]{1,0:T(1,128)} %bitcast.24, bf16[16,4,64,1024]{3,2,1,0:T(8,128)(2,1)} %get-tuple-element.27.wall_ref, ...), custom_call_target="tpu_custom_call" | custom-call | tf_op jit(solution)/shard_map/own_cycle/pallas_call | solution.py:353
  90.8 0.0 collective-permute-done.5.b1_hbm
  90.8 17.6 %row_0.1 = (f32[4,768,768]{2,1,0:T(8,128)}, bf16[4,768,768]{2,1,0:T(8,128)(2,1)}) custom-call(s32[1,1]{1,0:T(1,128)S(6)} %copy.21.count_ref, f32[2,2]{1,0:T(2,128)} %bitcast.20, f32[768,1]{1,0:T(8,128)} %get-tuple-element.33.vcol_ref, f32[1,768]{1,0:T(1,128)} %get-tuple-element.34.vrow_ref, ...), custom_call_target="tpu_custom_call", output_to_operand_aliasing={{0}: (12, {})} | custom-call | tf_op jit(solution)/shard_map/row_0/pallas_call | solution.py:481
  108.4 3.1 %collective-permute-done.4.refs_0_ = bf16[768,768]{1,0:T(8,128)(2,1)} collective-permute-done((bf16[768,768]{1,0:T(8,128)(2,1)}, bf16[768,768]{1,0:T(8,128)(2,1)}, u32[]{:S(2)}, u32[]{:S(2)}) %collective-permute-start.4) | collective-permute-done | bytes 1179680 | tf_op jit(solution)/shard_map/ppermute | solution.py:631
  111.5 11.7 %piece_10_0.1.refs_7_ = f32[4,768,768]{2,1,0:T(8,128)} custom-call(s32[1,1]{1,0:T(1,128)S(6)} %copy.21.count_ref, f32[2,2]{1,0:T(2,128)} %bitcast.21, f32[768,1]{1,0:T(8,128)} %get-tuple-element.33.vcol_ref, f32[1,768]{1,0:T(1,128)} %get-tuple-element.34.vrow_ref, bf16[768,768]{1,0:T(8,128)(2,1)} %collective-permute-done.4.refs_0_, ...), custom_call_target="tpu_custom_call", output_to_operand_aliasing={{}: (11, {})} | custom-call | tf_op jit(solution)/shard_map/piece_10_0/pallas_call | solution.py:589
  123.2 5.2 %collective-permute-done.3.refs_0_ = bf16[768,512]{1,0:T(8,128)(2,1)} collective-permute-done((bf16[768,512]{1,0:T(8,128)(2,1)}, bf16[768,512]{1,0:T(8,128)(2,1)}, u32[]{:S(2)}, u32[]{:S(2)}) %collective-permute-start.3) | collective-permute-done | bytes 786464 | tf_op jit(solution)/shard_map/ppermute | solution.py:631
  128.3 7.5 %piece_11_0.1 = (f32[4,768,768]{2,1,0:T(8,128)}, f32[768,768]{1,0:T(8,128)}) custom-call(s32[1,1]{1,0:T(1,128)S(6)} %copy.21.count_ref, f32[2,2]{1,0:T(2,128)} %bitcast.22, f32[768,1]{1,0:T(8,128)} %get-tuple-element.33.vcol_ref, f32[1,768]{1,0:T(1,128)} %get-tuple-element.34.vrow_ref, ...), custom_call_target="tpu_custom_call", output_to_operand_aliasing={{0}: (11, {})} | custom-call | tf_op jit(solution)/shard_map/piece_11_0/pallas_call | solution.py:589
  135.8 0.1 collective-permute-done.2.refs_0_
  135.9 10.0 %piece_11_512.1 = (f32[4,768,768]{2,1,0:T(8,128)}, bf16[4,768,768]{2,1,0:T(8,128)(2,1)}) custom-call(s32[1,1]{1,0:T(1,128)S(6)} %copy.21.count_ref, f32[2,2]{1,0:T(2,128)} %bitcast.23, f32[768,1]{1,0:T(8,128)} %get-tuple-element.33.vcol_ref, f32[1,768]{1,0:T(1,128)} %get-tuple-element.34.vrow_ref, ...), custom_call_target="tpu_custom_call", output_to_operand_aliasing={{0}: (11, {}), {1}: (13, {})} | custom-call | tf_op jit(solution)/shard_map/piece_11_512/pallas_call | solution.py:589
Async XLA Ops:
  41.6 25.8 %collective-permute-start = (bf16[2,4,64,1024]{3,2,1,0:T(8,128)(2,1)}, bf16[2,4,64,1024]{3,2,1,0:T(8,128)(2,1)}, u32[]{:S(2)}, u32[]{:S(2)}) collective-permute-start(bf16[2,4,64,1024]{3,2,1,0:T(8,128)(2,1)} %get-tuple-element.28.far_ref), channel_id=1, source_target_pairs={{0,2},{1,3},{2,0},{3,1},{4,6},{5,7},{6,4},{7,5},{8,10},{9,11},{10,... | collective-permute-start | bytes 3145736 | tf_op jit(solution)/shard_map/ppermute | solution.py:632
  42.9 47.9 %collective-permute-start.5 = (bf16[768,1152]{1,0:T(8,128)(2,1)}, bf16[768,1152]{1,0:T(8,128)(2,1)}, u32[]{:S(2)}, u32[]{:S(2)}) collective-permute-start(bf16[768,1152]{1,0:T(8,128)(2,1)} %get-tuple-element.44), channel_id=1, source_target_pairs={{0,8},{1,9},{2,10},{3,11},{4,12},{5,13},{6,14},{7,15},{8,0},{9,1},... | collective-permute-start | bytes 5308424 | tf_op jit(solution)/shard_map/ppermute | solution.py:631
  42.9 68.6 %collective-permute-start.4 = (bf16[768,768]{1,0:T(8,128)(2,1)}, bf16[768,768]{1,0:T(8,128)(2,1)}, u32[]{:S(2)}, u32[]{:S(2)}) collective-permute-start(bf16[768,768]{1,0:T(8,128)(2,1)} %get-tuple-element.42), channel_id=1, source_target_pairs={{0,8},{1,9},{2,10},{3,11},{4,12},{5,13},{6,14},{7,15},{8,0},{9,1},... | collective-permute-start | bytes 3538952 | tf_op jit(solution)/shard_map/ppermute | solution.py:631
  67.4 3.5 %collective-permute-start.1 = (bf16[2,4,64,1024]{3,2,1,0:T(8,128)(2,1)}, bf16[2,4,64,1024]{3,2,1,0:T(8,128)(2,1)}, u32[]{:S(2)}, u32[]{:S(2)}) collective-permute-start(bf16[2,4,64,1024]{3,2,1,0:T(8,128)(2,1)} %collective-permute-done.side_ref), channel_id=1, source_target_pairs={{0,1},{1,0},{2,3},{3,2},{4,5},{5,4},{6,7},{7,6},{8,9},{9,8},{10,11... | collective-permute-start | bytes 3145736 | tf_op jit(solution)/shard_map/ppermute | solution.py:638
  67.4 60.9 %collective-permute-start.3 = (bf16[768,512]{1,0:T(8,128)(2,1)}, bf16[768,512]{1,0:T(8,128)(2,1)}, u32[]{:S(2)}, u32[]{:S(2)}) collective-permute-start(bf16[768,512]{1,0:T(8,128)(2,1)} %get-tuple-element.41), channel_id=1, source_target_pairs={{0,8},{1,9},{2,10},{3,11},{4,12},{5,13},{6,14},{7,15},{8,0},{9,1},... | collective-permute-start | bytes 2359304 | tf_op jit(solution)/shard_map/ppermute | solution.py:631
  67.4 68.5 %collective-permute-start.2 = (bf16[768,256]{1,0:T(8,128)(2,1)}, bf16[768,256]{1,0:T(8,128)(2,1)}, u32[]{:S(2)}, u32[]{:S(2)}) collective-permute-start(bf16[768,256]{1,0:T(8,128)(2,1)} %get-tuple-element.35), channel_id=1, source_target_pairs={{0,8},{1,9},{2,10},{3,11},{4,12},{5,13},{6,14},{7,15},{8,0},{9,1},... | collective-permute-start | bytes 1179656 | tf_op jit(solution)/shard_map/ppermute | solution.py:637

commit v5 on v4

--- a/solution.py
+++ b/solution.py
@@ -387,18 +387,31 @@
 
 
 class Mover:
-    def __init__(self, plan, in_sem, out_sem):
+    def __init__(self, stages, in_sem, out_sem):
+        self.in_sem = in_sem
         self.out_sem = out_sem
         self.outs = []
-        self.loads = {}
-        for at, (name, (src, dst)) in enumerate(plan.items()):
-            self.loads[name] = pltpu.make_async_copy(src, dst, in_sem.at[at])
-            self.loads[name].start()
+        self.stages = stages
+        self.waiting = {}
+        self.begun = 0
+        self.count = 0
+        self.advance(2)
+
+    def advance(self, upto):
+        while self.begun < min(upto, len(self.stages)):
+            for name, (src, dst) in self.stages[self.begun].items():
+                copy = pltpu.make_async_copy(src, dst, self.in_sem.at[self.count])
+                copy.start()
+                self.waiting[name] = (copy, self.begun)
+                self.count += 1
+            self.begun += 1
 
     def need(self, *names):
         for name in names:
-            if name in self.loads:
-                self.loads.pop(name).wait()
+            if name in self.waiting:
+                copy, stage = self.waiting.pop(name)
+                copy.wait()
+                self.advance(stage + 3)
 
     def put(self, src, dst):
         copy = pltpu.make_async_copy(src, dst, self.out_sem.at[len(self.outs)])
@@ -435,22 +448,27 @@
     early = b0_hbm.shape[1]
     head = pl.ds(0, points)
     blocks = [pl.ds(points + k * width, width) for k in range(2)]
-    plan = {
-        "b0": (b0_hbm, left.at[:, pl.ds(points, early)]),
-        "b1": (b1_hbm, left.at[:, pl.ds(points + early, 2 * width - early)]),
-        "xt": (xt_hbm, xt),
-        "x0": (x_hbm, right.at[0, :, head]),
-        "wt": (wt_hbm.at[pl.ds(2 * i, 2)], wt),
-        "coret": (coret_hbm, coret),
-    }
+    ends = []
     for j in range(2):
-        for k in range(2):
-            plan["w%d%d" % (j, k)] = (wd_hbm.at[2 * j + k], right.at[j, :, blocks[k]])
-        plan["part%d" % j] = (part_hbm.at[2 * i + j], part.at[j])
-        plan["amps%d" % j] = (amps_hbm.at[2 * i + j], amps.at[j])
-        if j == 0:
-            plan["x1"] = (x_hbm, right.at[1, :, head])
-    mover = Mover(plan, sem, osem)
+        stage = {"w%d%d" % (j, k): (wd_hbm.at[2 * j + k], right.at[j, :, blocks[k]]) for k in range(2)}
+        stage["part%d" % j] = (part_hbm.at[2 * i + j], part.at[j])
+        stage["amps%d" % j] = (amps_hbm.at[2 * i + j], amps.at[j])
+        if j == 1:
+            stage["x1"] = (x_hbm, right.at[1, :, head])
+        ends.append(stage)
+    stages = [
+        {
+            "xt": (xt_hbm, xt),
+            "b0": (b0_hbm, left.at[:, pl.ds(points, early)]),
+            "b1": (b1_hbm, left.at[:, pl.ds(points + early, 2 * width - early)]),
+        },
+        {
+            "x0": (x_hbm, right.at[0, :, head]),
+            "coret": (coret_hbm, coret),
+            "wt": (wt_hbm.at[pl.ds(2 * i, 2)], wt),
+        },
+    ]
+    mover = Mover(stages + ends, sem, osem)
     for j in range(2):
         mover.need("b0", "b1", "xt")
         proj[...] = dot(xt[...], left[:, blocks[j]]).astype(proj.dtype)
@@ -518,22 +536,20 @@
     width, points = x_hbm.shape
     head, rest = pl.ds(0, points), pl.ds(points, high - low)
     cut = pl.ds(low, high - low)
-    plan = {
-        "b": (b_hbm, left.at[:, rest]),
-        "xt": (xt_hbm, xt),
-        "x": (x_hbm, right.at[k, :, head]),
-    }
+    stages = [{"b": (b_hbm, left.at[:, rest]), "xt": (xt_hbm, xt)}, {"x": (x_hbm, right.at[k, :, head])}]
+    stages.append({"coret": (coret_hbm, coret)})
     if low > 0:
-        plan["acc"] = (acc_in, acc)
-    if end:
-        plan["wt"] = (wt_hbm.at[2 * i + k], wt)
-        plan["coret"] = (coret_hbm, coret)
+        stages[2]["acc"] = (acc_in, acc)
+    else:
+        stages[2]["wt"] = (wt_hbm.at[2 * i + k], wt)
     for j in (1 - k, k):
-        plan["w%d" % j] = (wd_hbm.at[2 * j + k, :, cut], right.at[j, :, rest])
-        plan["part%d" % j] = (part_hbm.at[2 * i + j], part.at[j])
+        stages.append({
+            "w%d" % j: (wd_hbm.at[2 * j + k, :, cut], right.at[j, :, rest]),
+            "part%d" % j: (part_hbm.at[2 * i + j], part.at[j]),
+        })
         if last:
-            plan["amps%d" % j] = (amps_hbm.at[2 * i + j], amps.at[j])
-    mover = Mover(plan, sem, osem)
+            stages[-1]["amps%d" % j] = (amps_hbm.at[2 * i + j], amps.at[j])
+    mover = Mover(stages, sem, osem)
 
     def products(j, columns):
         mover.need("w%d" % j, "part%d" % j, "amps%d" % j)
@@ -548,14 +564,11 @@
     proj[...] = dot(xt[...], left[:, rest]).astype(proj.dtype)
     mover.need("x")
     inner = dot(proj[...], right[k, cut, head])
-    if low > 0:
-        mover.need("acc")
-        inner = inner + acc[...]
+    mover.need("coret", "wt", "acc")
+    before = acc[...] if low > 0 else wt[...].astype(jnp.float32)
+    inner = before + coret[...].astype(jnp.float32) * inner
     if end:
-        mover.need("wt", "coret")
-        total[...] = (
-            wt[...].astype(jnp.float32) + coret[...].astype(jnp.float32) * inner
-        ).astype(total.dtype)
+        total[...] = inner.astype(total.dtype)
         left[:, head] = dot(right[k, :, head], total[...]).astype(left.dtype)
         products(1 - k, rest)
         products(k, pl.ds(0, points + high - low))

time: 146 us -> 148 us (1.014)
  Pallas kernels: 121 us -> 123 us
    pallas_call x3, Pallas kernels: 29.1 us -> 31.1 us  [piece(): pl.pallas_call(functools.partial(piece_kernel, i, k, low, high, end), out...]
  transfers between devices with their start and end apart: 6 -> 6, of which waited for: 4 -> 3; matrix products, arithmetic and copies ran while one was open for 0% -> 0% of each run, Pallas kernels for 48% -> 48%
where the time goes in v5:
time: 148 us
  Pallas kernels  123 us (83%)
  waiting for transfers between devices  15.5 us (10%)
  starting transfers between devices  8.41 us (6%)
  between operations  1.53 us (1%)
    pallas_call x1, Pallas kernels, gather_parts(): pl.pallas_call(gather_kernel, out_shape=[jax.ShapeDtypeStruct(shape, bf16...  40.9 us
    pallas_call x3, Pallas kernels, piece(): pl.pallas_call(functools.partial(piece_kernel, i, k, low, high, end), out...  31.1 us
    pallas_call x1, Pallas kernels, own_cycle(): pl.pallas_call(own_cycle_kernel, out_shape=(jax.ShapeDtypeStruct((4, widt...  19.9 us
    pallas_call x1, Pallas kernels, row(): pl.pallas_call(functools.partial(row_kernel, i), out_shape=[jax.ShapeDtyp...  17.5 us
    pallas_call x1, Pallas kernels, own_ladder(): pl.pallas_call(own_ladder_kernel, out_shape=(jax.ShapeDtypeStruct((width,...  13.1 us
    ppermute x3, waiting for transfers between devices, per_device(): lax.ppermute(part, 'col', mirror)  8.26 us
    ppermute x1, waiting for transfers between devices, per_device(): side = lax.ppermute(far, 'col', [(i, i ^ 2) for i in range(cols)])  7.18 us
    ppermute x3, starting transfers between devices, per_device(): lax.ppermute(part, 'col', mirror)  3.53 us
  transfers between devices with their start and end apart: 6, of which 3 were waited for; matrix products, arithmetic and copies ran while one was open for 0% of the time, Pallas kernels for 48%

profile of v5, /device:TPU:6, one launch (start us, length us, event | category | flops | bytes accessed | tf_op | source)
XLA Modules:
  0.0 147.9 jit_solution(10193855505065781159)
XLA Ops:
  0.6 40.9 %gather_parts.1 = (bf16[8,2,64,768]{3,2,1,0:T(8,128)(2,1)}, bf16[16,4,64,1024]{3,2,1,0:T(8,128)(2,1)}, bf16[2,4,64,1024]{3,2,1,0:T(8,128)(2,1)}, bf16[768,384]{1...) custom-call(bf16[2,64,768]{2,1,0:T(8,128)(2,1)} %x_ref.1, ...), custom_call_target="tpu_custom_call" | custom-call | tf_op jit(solution)/shard_map/gather_parts/pallas_call | solution.py:193
  41.6 1.3 collective-permute-start
  42.9 0.0 collective-permute-start.5
  42.9 3.5 %collective-permute-start.4 = (bf16[768,768]{1,0:T(8,128)(2,1)}, bf16[768,768]{1,0:T(8,128)(2,1)}, u32[]{:S(2)}, u32[]{:S(2)}) collective-permute-start(bf16[768,768]{1,0:T(8,128)(2,1)} %get-tuple-element.42), channel_id=1, source_target_pairs={{0,8},{1,9},{2,10},{3,11},{4,12},{5,13},{6,14},{7,15},{8,0},{9,1},... | collective-permute-start | bytes 3538952 | tf_op jit(solution)/shard_map/ppermute | solution.py:644
  47.1 13.1 %own_ladder.1 = (bf16[768,768]{1,0:T(8,128)(2,1)}, bf16[768,768]{1,0:T(8,128)(2,1)}, bf16[4,768,768]{2,1,0:T(8,128)(2,1)}) custom-call(s32[12]{0:T(128)} %bitcast.25, s32[1,1]{1,0:T(1,128)S(6)} %copy.21.count_ref, s32[16]{0:T(128)} %slot_ref.1, bf16[16,64,768]{2,1,0:T(8,128)(2,1)} %bitcast.18, bf16[4,768,768]{2,1,0:T(8,128)(2,1)} %bitcast.9, ...), custom_call_target="tpu_custom_call" | custom-call | tf_op jit(solution)/shard_map/own_ladder/pallas_call | solution.py:252
  60.2 7.2 %collective-permute-done.side_ref = bf16[2,4,64,1024]{3,2,1,0:T(8,128)(2,1)} collective-permute-done((bf16[2,4,64,1024]{3,2,1,0:T(8,128)(2,1)}, bf16[2,4,64,1024]{3,2,1,0:T(8,128)(2,1)}, u32[]{:S(2)}, u32[]{:S(2)}) %collective-permute-start) | collective-permute-done | bytes 1048608 | tf_op jit(solution)/shard_map/ppermute | solution.py:645
  67.4 0.0 collective-permute-start.1
  67.4 0.0 collective-permute-start.3
  67.4 3.5 %collective-permute-start.2 = (bf16[768,256]{1,0:T(8,128)(2,1)}, bf16[768,256]{1,0:T(8,128)(2,1)}, u32[]{:S(2)}, u32[]{:S(2)}) collective-permute-start(bf16[768,256]{1,0:T(8,128)(2,1)} %get-tuple-element.35), channel_id=1, source_target_pairs={{0,8},{1,9},{2,10},{3,11},{4,12},{5,13},{6,14},{7,15},{8,0},{9,1},... | collective-permute-start | bytes 1179656 | tf_op jit(solution)/shard_map/ppermute | solution.py:650
  70.9 0.0 collective-permute-done.1.twin_ref
  70.9 19.9 %own_cycle.1 = (bf16[4,768,768]{2,1,0:T(8,128)(2,1)}, f32[4,768,768]{2,1,0:T(8,128)}, f32[768,1]{1,0:T(8,128)}, f32[1,768]{1,0:T(1,128)}) custom-call(s32[12]{0:T(128)} %bitcast.26, s32[1,1]{1,0:T(1,128)S(6)} %copy.21.count_ref, f32[1,1024]{1,0:T(1,128)} %bitcast.24, bf16[16,4,64,1024]{3,2,1,0:T(8,128)(2,1)} %get-tuple-element.27.wall_ref, ...), custom_call_target="tpu_custom_call" | custom-call | tf_op jit(solution)/shard_map/own_cycle/pallas_call | solution.py:353
  90.8 0.0 collective-permute-done.5.b1_hbm
  90.8 17.5 %row_0.1 = (f32[4,768,768]{2,1,0:T(8,128)}, bf16[4,768,768]{2,1,0:T(8,128)(2,1)}) custom-call(s32[1,1]{1,0:T(1,128)S(6)} %copy.21.count_ref, f32[2,2]{1,0:T(2,128)} %bitcast.20, f32[768,1]{1,0:T(8,128)} %get-tuple-element.33.vcol_ref, f32[1,768]{1,0:T(1,128)} %get-tuple-element.34.vrow_ref, ...), custom_call_target="tpu_custom_call", output_to_operand_aliasing={{0}: (12, {})} | custom-call | tf_op jit(solution)/shard_map/row_0/pallas_call | solution.py:499
  108.4 3.1 %collective-permute-done.4.refs_0_ = bf16[768,768]{1,0:T(8,128)(2,1)} collective-permute-done((bf16[768,768]{1,0:T(8,128)(2,1)}, bf16[768,768]{1,0:T(8,128)(2,1)}, u32[]{:S(2)}, u32[]{:S(2)}) %collective-permute-start.4) | collective-permute-done | bytes 1179680 | tf_op jit(solution)/shard_map/ppermute | solution.py:644
  111.5 11.7 %piece_10_0.1.refs_7_ = f32[4,768,768]{2,1,0:T(8,128)} custom-call(s32[1,1]{1,0:T(1,128)S(6)} %copy.21.count_ref, f32[2,2]{1,0:T(2,128)} %bitcast.21, f32[768,1]{1,0:T(8,128)} %get-tuple-element.33.vcol_ref, f32[1,768]{1,0:T(1,128)} %get-tuple-element.34.vrow_ref, bf16[768,768]{1,0:T(8,128)(2,1)} %collective-permute-done.4.refs_0_, ...), custom_call_target="tpu_custom_call", output_to_operand_aliasing={{}: (11, {})} | custom-call | tf_op jit(solution)/shard_map/piece_10_0/pallas_call | solution.py:602
  123.2 5.1 %collective-permute-done.3.refs_0_ = bf16[768,512]{1,0:T(8,128)(2,1)} collective-permute-done((bf16[768,512]{1,0:T(8,128)(2,1)}, bf16[768,512]{1,0:T(8,128)(2,1)}, u32[]{:S(2)}, u32[]{:S(2)}) %collective-permute-start.3) | collective-permute-done | bytes 786464 | tf_op jit(solution)/shard_map/ppermute | solution.py:644
  128.3 9.5 %piece_11_0.1 = (f32[4,768,768]{2,1,0:T(8,128)}, f32[768,768]{1,0:T(8,128)}) custom-call(s32[1,1]{1,0:T(1,128)S(6)} %copy.21.count_ref, f32[2,2]{1,0:T(2,128)} %bitcast.22, f32[768,1]{1,0:T(8,128)} %get-tuple-element.33.vcol_ref, f32[1,768]{1,0:T(1,128)} %get-tuple-element.34.vrow_ref, ...), custom_call_target="tpu_custom_call", output_to_operand_aliasing={{0}: (11, {})} | custom-call | tf_op jit(solution)/shard_map/piece_11_0/pallas_call | solution.py:602
  137.8 0.0 collective-permute-done.2.refs_0_
  137.9 9.9 %piece_11_512.1 = (f32[4,768,768]{2,1,0:T(8,128)}, bf16[4,768,768]{2,1,0:T(8,128)(2,1)}) custom-call(s32[1,1]{1,0:T(1,128)S(6)} %copy.21.count_ref, f32[2,2]{1,0:T(2,128)} %bitcast.23, f32[768,1]{1,0:T(8,128)} %get-tuple-element.33.vcol_ref, f32[1,768]{1,0:T(1,128)} %get-tuple-element.34.vrow_ref, ...), custom_call_target="tpu_custom_call", output_to_operand_aliasing={{0}: (11, {}), {1}: (13, {})} | custom-call | tf_op jit(solution)/shard_map/piece_11_512/pallas_call | solution.py:602
Async XLA Ops:
  41.6 25.8 %collective-permute-start = (bf16[2,4,64,1024]{3,2,1,0:T(8,128)(2,1)}, bf16[2,4,64,1024]{3,2,1,0:T(8,128)(2,1)}, u32[]{:S(2)}, u32[]{:S(2)}) collective-permute-start(bf16[2,4,64,1024]{3,2,1,0:T(8,128)(2,1)} %get-tuple-element.28.far_ref), channel_id=1, source_target_pairs={{0,2},{1,3},{2,0},{3,1},{4,6},{5,7},{6,4},{7,5},{8,10},{9,11},{10,... | collective-permute-start | bytes 3145736 | tf_op jit(solution)/shard_map/ppermute | solution.py:645
  42.9 47.9 %collective-permute-start.5 = (bf16[768,1152]{1,0:T(8,128)(2,1)}, bf16[768,1152]{1,0:T(8,128)(2,1)}, u32[]{:S(2)}, u32[]{:S(2)}) collective-permute-start(bf16[768,1152]{1,0:T(8,128)(2,1)} %get-tuple-element.44), channel_id=1, source_target_pairs={{0,8},{1,9},{2,10},{3,11},{4,12},{5,13},{6,14},{7,15},{8,0},{9,1},... | collective-permute-start | bytes 5308424 | tf_op jit(solution)/shard_map/ppermute | solution.py:644
  42.9 68.6 %collective-permute-start.4 = (bf16[768,768]{1,0:T(8,128)(2,1)}, bf16[768,768]{1,0:T(8,128)(2,1)}, u32[]{:S(2)}, u32[]{:S(2)}) collective-permute-start(bf16[768,768]{1,0:T(8,128)(2,1)} %get-tuple-element.42), channel_id=1, source_target_pairs={{0,8},{1,9},{2,10},{3,11},{4,12},{5,13},{6,14},{7,15},{8,0},{9,1},... | collective-permute-start | bytes 3538952 | tf_op jit(solution)/shard_map/ppermute | solution.py:644
  67.4 3.5 %collective-permute-start.1 = (bf16[2,4,64,1024]{3,2,1,0:T(8,128)(2,1)}, bf16[2,4,64,1024]{3,2,1,0:T(8,128)(2,1)}, u32[]{:S(2)}, u32[]{:S(2)}) collective-permute-start(bf16[2,4,64,1024]{3,2,1,0:T(8,128)(2,1)} %collective-permute-done.side_ref), channel_id=1, source_target_pairs={{0,1},{1,0},{2,3},{3,2},{4,5},{5,4},{6,7},{7,6},{8,9},{9,8},{10,11... | collective-permute-start | bytes 3145736 | tf_op jit(solution)/shard_map/ppermute | solution.py:651
  67.4 60.9 %collective-permute-start.3 = (bf16[768,512]{1,0:T(8,128)(2,1)}, bf16[768,512]{1,0:T(8,128)(2,1)}, u32[]{:S(2)}, u32[]{:S(2)}) collective-permute-start(bf16[768,512]{1,0:T(8,128)(2,1)} %get-tuple-element.41), channel_id=1, source_target_pairs={{0,8},{1,9},{2,10},{3,11},{4,12},{5,13},{6,14},{7,15},{8,0},{9,1},... | collective-permute-start | bytes 2359304 | tf_op jit(solution)/shard_map/ppermute | solution.py:644
  67.4 70.5 %collective-permute-start.2 = (bf16[768,256]{1,0:T(8,128)(2,1)}, bf16[768,256]{1,0:T(8,128)(2,1)}, u32[]{:S(2)}, u32[]{:S(2)}) collective-permute-start(bf16[768,256]{1,0:T(8,128)(2,1)} %get-tuple-element.35), channel_id=1, source_target_pairs={{0,8},{1,9},{2,10},{3,11},{4,12},{5,13},{6,14},{7,15},{8,0},{9,1},... | collective-permute-start | bytes 1179656 | tf_op jit(solution)/shard_map/ppermute | solution.py:650

commit v6 on v4

--- a/solution.py
+++ b/solution.py
@@ -39,7 +39,8 @@
 
 
 def gather_kernel(
-    x_ref, w_ref, amps_ref, core_ref, xall_ref, wall_ref, far_ref, first_ref, coret_ref, *refs
+    count_ref, x_ref, w_ref, amps_ref, core_ref,
+    xall_ref, wall_ref, far_ref, first_ref, coret_ref, live_ref, *refs
 ):
     cuts, (plain, turned, fixed, wsend, wrecv, xsend, xrecv, msend, mrecv, local, tsem) = refs[:-11], refs[-11:]
     r = lax.axis_index("row")
@@ -89,9 +90,17 @@
         x = (c // 4 + offset) % (cols // 4)
         send(shard(offset, 0, 0), wall_ref.at[x * 4 + c % 4], wsems, 6 + offset, twin)
 
+    def live(shape, axis):
+        at = lax.broadcasted_iota(jnp.int32, shape, axis)
+        return jnp.where(at < count_ref[0, 0] * x_ref.shape[1], 1.0, 0.0)
+
+    live_rows, live_cols = live((width, 1), 0), live((1, width), 1)
+
     def transpose(q, p):
         amps_in[q].wait()
         for cut in strips(width, 256):
+            mask = live_rows[cut.start:cut.start + cut.size] * live_cols
+            plain[q, cut, :] = (plain[q, cut, :].astype(jnp.float32) * mask).astype(plain.dtype)
             turned[p, :, cut] = plain[q, cut, :].T
 
     own = wall_ref.at[c]
@@ -157,6 +166,7 @@
     for cut in strips(width, 256):
         fixed[1, :, cut] = fixed[0, cut, :].T
     outs.append(pltpu.make_async_copy(fixed.at[1], coret_ref, local.at[2]))
+    outs.append(pltpu.make_async_copy(plain, live_ref, local.at[8]))
     for copy in outs:
         copy.start()
     part = shard(3, 1, 0)
@@ -180,20 +190,20 @@
         copy.wait()
 
 
-def gather_parts(x_factor, shard, amp4, core, early, split):
+def gather_parts(count, x_factor, shard, amp4, core, early, split):
     rows = lax.axis_size("row")
     cols = lax.axis_size("col")
     width = amp4.shape[1]
     hbm = pl.BlockSpec(memory_space=pl.ANY)
     bf16 = jnp.bfloat16
     dma = pltpu.SemaphoreType.DMA
-    shapes = [(rows,) + x_factor.shape, (cols,) + shard.shape, (2,) + shard.shape, (width, early), core.shape]
+    shapes = [(rows,) + x_factor.shape, (cols,) + shard.shape, (2,) + shard.shape, (width, early), core.shape, amp4.shape]
     shapes += [(width, 2 * width - early), (width, width)]
     shapes += [(width, split), (width, width - split)]
     return pl.pallas_call(
         gather_kernel,
         out_shape=[jax.ShapeDtypeStruct(shape, bf16) for shape in shapes],
-        in_specs=[hbm] * 4,
+        in_specs=[pl.BlockSpec(memory_space=pltpu.SMEM)] + [hbm] * 4,
         out_specs=[hbm] * len(shapes),
         scratch_shapes=[
             pltpu.VMEM(amp4.shape, bf16),
@@ -205,14 +215,14 @@
             dma((14,)),
             dma((1,)),
             dma((1,)),
-            dma((8,)),
+            dma((9,)),
             dma((5,)),
         ],
         compiler_params=pltpu.CompilerParams(
             collective_id=0, has_side_effects=True, vmem_limit_bytes=VMEM_LIMIT
         ),
         name="gather_parts",
-    )(x_factor, shard, amp4, core)
+    )(count, x_factor, shard, amp4, core)
 
 
 def own_ladder_kernel(
@@ -338,8 +348,10 @@
                     wsel.at[pl.ds(2 * first, 2), pl.ds(s * tile, tile), :],
                     sem.at[first, s],
                 ).wait()
+            live = lax.broadcasted_iota(jnp.int32, (width, 1), 0) < count_ref[0, 0] * tile
             for k in range(2):
-                wd_ref[k] = dot(wsel[2 * first + k], pick[...]).astype(wd_ref.dtype)
+                picked = dot(wsel[2 * first + k], pick[...])
+                wd_ref[k] = jnp.where(live, picked, 0.0).astype(wd_ref.dtype)
 
     cyc_ref[0] = dot(wd_ref[0], a0_ref[0]) + dot(wd_ref[1], a1_ref[0])
 
@@ -410,25 +422,31 @@
             copy.wait()
 
 
-def emit(mover, last, pair, j, rows, raw, count_ref, occ_ref, vcol_ref, vrow_ref, part, amps, upd, res_hbm, upd_hbm):
+def emit(mover, last, pair, j, rows, raw, occ_ref, vcol_ref, vrow_ref, part, amps, upd, res_hbm, upd_hbm):
     raw = raw + part[j, rows, :]
-    if last:
-        count = count_ref[0, 0] * 64
-        height, width = raw.shape
-        live = (lax.broadcasted_iota(jnp.int32, (height, 1), 0) + rows.start < count) & (
-            lax.broadcasted_iota(jnp.int32, (1, width), 1) < count
-        )
-        raw = jnp.where(live, raw, 0.0)
-        own = jnp.where(live, amps[j, rows, :].astype(jnp.float32), 0.0)
-        gap = (occ_ref[0, pair // 2] + occ_ref[1, pair % 2]) - vcol_ref[rows, :] - vrow_ref[...]
-        upd[j, rows, :] = (own + raw / gap).astype(upd.dtype)
-        mover.put(upd.at[j, rows, :], upd_hbm.at[pair, rows, :])
     part[j, rows, :] = raw
     mover.put(part.at[j, rows, :], res_hbm.at[pair, rows, :])
+    if last:
+        gap = (occ_ref[0, pair // 2] + occ_ref[1, pair % 2]) - vcol_ref[rows, :] - vrow_ref[...]
+        inverse = pl.reciprocal(gap, approx=True)
+        inverse = inverse * (2.0 - gap * inverse)
+        own = amps[j, rows, :].astype(jnp.float32)
+        upd[j, rows, :] = (own + raw * inverse).astype(upd.dtype)
+        mover.put(upd.at[j, rows, :], upd_hbm.at[pair, rows, :])
+
+
+def emit_behind(products, emit_one):
+    waiting = None
+    for j, rows, product in products:
+        raw = product()
+        if waiting is not None:
+            emit_one(*waiting)
+        waiting = (j, rows, raw)
+    emit_one(*waiting)
 
 
 def row_kernel(
-    i, count_ref, occ_ref, vcol_ref, vrow_ref, b0_hbm, b1_hbm, xt_hbm, x_hbm, coret_hbm, wt_hbm, wd_hbm,
+    i, occ_ref, vcol_ref, vrow_ref, b0_hbm, b1_hbm, xt_hbm, x_hbm, coret_hbm, wt_hbm, wd_hbm,
     amps_hbm, part_hbm, res_hbm, upd_hbm, xt, coret, wt, right, left, part, amps, proj, total, upd, sem, osem,
 ):
     width, points = x_hbm.shape
@@ -459,19 +477,29 @@
         total[j] = (
             wt[j].astype(jnp.float32) + coret[...].astype(jnp.float32) * inner
         ).astype(total.dtype)
-    for j in range(2):
-        left[:, head] = dot(right[0, :, head], total[j]).astype(left.dtype)
-        mover.need("x%d" % j, "w%d0" % j, "w%d1" % j, "part%d" % j, "amps%d" % j)
-        for rows in strips(width, STRIP):
-            raw = dot_nt(left[rows, :], right[j])
-            emit(
-                mover, True, 2 * i + j, j, rows, raw, count_ref, occ_ref, vcol_ref, vrow_ref,
-                part, amps, upd, res_hbm, upd_hbm,
-            )
+    def products():
+        for j in range(2):
+            for at, rows in enumerate(strips(width, STRIP)):
+
+                def product(j=j, at=at, rows=rows):
+                    if at == 0:
+                        left[:, head] = dot(right[0, :, head], total[j]).astype(left.dtype)
+                        mover.need("x%d" % j, "w%d0" % j, "w%d1" % j, "part%d" % j, "amps%d" % j)
+                    return dot_nt(left[rows, :], right[j])
+
+                yield j, rows, product
+
+    def emit_one(j, rows, raw):
+        emit(
+            mover, True, 2 * i + j, j, rows, raw, occ_ref, vcol_ref, vrow_ref,
+            part, amps, upd, res_hbm, upd_hbm,
+        )
+
+    emit_behind(products(), emit_one)
     mover.drain()
 
 
-def row(i, count, occ, vcol, vrow, b0, b1, xt, x, coret, wt, wd, amp4, part):
+def row(i, occ, vcol, vrow, b0, b1, xt, x, coret, wt, wd, amp4, part):
     width, points = x.shape
     vmem = pl.BlockSpec(memory_space=pltpu.VMEM)
     smem = pl.BlockSpec(memory_space=pltpu.SMEM)
@@ -481,7 +509,7 @@
     return pl.pallas_call(
         functools.partial(row_kernel, i),
         out_shape=[jax.ShapeDtypeStruct(part.shape, f32), jax.ShapeDtypeStruct(part.shape, bf16)],
-        in_specs=[smem, smem, vmem, vmem] + [hbm] * 9,
+        in_specs=[smem, vmem, vmem] + [hbm] * 9,
         out_specs=[hbm] * 2,
         scratch_shapes=[
             pltpu.VMEM((points, width), bf16),
@@ -497,13 +525,13 @@
             pltpu.SemaphoreType.DMA((15,)),
             pltpu.SemaphoreType.DMA((4 * (width // STRIP),)),
         ],
-        input_output_aliases={12: 0},
+        input_output_aliases={11: 0},
         compiler_params=pltpu.CompilerParams(vmem_limit_bytes=VMEM_LIMIT),
         name="row_%d" % i,
-    )(count, occ, vcol, vrow, b0, b1, xt, x, coret, wt, wd, amp4, part)
-
-
-def piece_kernel(i, k, low, high, end, count_ref, occ_ref, vcol_ref, vrow_ref, *refs):
+    )(occ, vcol, vrow, b0, b1, xt, x, coret, wt, wd, amp4, part)
+
+
+def piece_kernel(i, k, low, high, end, occ_ref, vcol_ref, vrow_ref, *refs):
     last = k == 1 and end
     scratch = 13
     refs, (xt, coret, wt, right, left, part, amps, acc, proj, total, upd, sem, osem) = (
@@ -535,14 +563,21 @@
             plan["amps%d" % j] = (amps_hbm.at[2 * i + j], amps.at[j])
     mover = Mover(plan, sem, osem)
 
-    def products(j, columns):
-        mover.need("w%d" % j, "part%d" % j, "amps%d" % j)
-        for rows in strips(width, STRIP):
-            raw = dot_nt(left[rows, columns], right[j, :, columns])
-            emit(
-                mover, last, 2 * i + j, j, rows, raw, count_ref, occ_ref, vcol_ref, vrow_ref,
-                part, amps, upd, res_hbm, upd_hbm,
-            )
+    def products(plan):
+        for j, columns in plan:
+            for rows in strips(width, STRIP):
+
+                def product(j=j, columns=columns, rows=rows):
+                    mover.need("w%d" % j, "part%d" % j, "amps%d" % j)
+                    return dot_nt(left[rows, columns], right[j, :, columns])
+
+                yield j, rows, product
+
+    def emit_one(j, rows, raw):
+        emit(
+            mover, last, 2 * i + j, j, rows, raw, occ_ref, vcol_ref, vrow_ref,
+            part, amps, upd, res_hbm, upd_hbm,
+        )
 
     mover.need("b", "xt")
     proj[...] = dot(xt[...], left[:, rest]).astype(proj.dtype)
@@ -557,17 +592,15 @@
             wt[...].astype(jnp.float32) + coret[...].astype(jnp.float32) * inner
         ).astype(total.dtype)
         left[:, head] = dot(right[k, :, head], total[...]).astype(left.dtype)
-        products(1 - k, rest)
-        products(k, pl.ds(0, points + high - low))
+        emit_behind(products([(1 - k, rest), (k, pl.ds(0, points + high - low))]), emit_one)
     else:
         acc[...] = inner
         mover.put(acc, acc_out)
-        for j in (1 - k, k):
-            products(j, rest)
+        emit_behind(products([(1 - k, rest), (k, rest)]), emit_one)
     mover.drain()
 
 
-def piece(i, k, low, high, count, occ, vcol, vrow, b, xt, x, coret, wt, wd, amp4, part, acc, updated):
+def piece(i, k, low, high, occ, vcol, vrow, b, xt, x, coret, wt, wd, amp4, part, acc, updated):
     width, points = x.shape
     end = high == width
     last = k == 1 and end
@@ -575,7 +608,7 @@
     smem = pl.BlockSpec(memory_space=pltpu.SMEM)
     hbm = pl.BlockSpec(memory_space=pl.ANY)
     f32, bf16 = jnp.float32, jnp.bfloat16
-    operands = [count, occ, vcol, vrow, b, xt, x, coret, wt, wd, amp4, part]
+    operands = [occ, vcol, vrow, b, xt, x, coret, wt, wd, amp4, part]
     out_shape = [jax.ShapeDtypeStruct(part.shape, f32)]
     alias = {len(operands) - 1: 0}
     if low > 0:
@@ -589,7 +622,7 @@
     return pl.pallas_call(
         functools.partial(piece_kernel, i, k, low, high, end),
         out_shape=out_shape,
-        in_specs=[smem, smem, vmem, vmem] + [hbm] * (len(operands) - 4),
+        in_specs=[smem, vmem, vmem] + [hbm] * (len(operands) - 3),
         out_specs=[hbm] * len(out_shape),
         scratch_shapes=[
             pltpu.VMEM((points, width), bf16),
@@ -625,19 +658,21 @@
     shard = cycle_w[0].reshape(occ * occ, tile_width, window)
 
     early, split = width // 2, 512
-    xall, wall, far, first, coret, *turned = gather_parts(x_factor, shard, amp4, core, early, split)
+    tiles, count = domain_tiles[0, 0], domain_count
+    xall, wall, far, first, coret, amp4, *turned = gather_parts(
+        count, x_factor, shard, amp4, core, early, split
+    )
     xall = xall.reshape(-1, tile_width, grid_points)
     mirror = [(i, (i + cols // 2) % cols) for i in range(cols)]
     second, third, fourth = [lax.ppermute(part, "col", mirror) for part in turned[:3]]
     side = lax.ppermute(far, "col", [(i, i ^ 2) for i in range(cols)])
 
-    tiles, count = domain_tiles[0, 0], domain_count
     x, xt, wt = own_ladder(tiles, count, tile_slot, xall, amp4, core)
     side, tail, wt = lax.optimization_barrier((side, turned[3], wt))
     fifth = lax.ppermute(tail, "col", mirror)
     twin = lax.ppermute(side, "col", [(i, i ^ 1) for i in range(cols)])
     wd, part, vcol, vrow = own_cycle(tiles, count, virt_energy[None, :], wall, far, side, twin, amp4)
-    energies = (count, occ_energy[0, 0], vcol, vrow)
+    energies = (occ_energy[0, 0], vcol, vrow)
     part, updated = row(0, *energies, first, second, xt, x, coret, wt, wd, amp4, part)
     fixed = (xt, x, coret, wt, wd, amp4)
     part, = piece(1, 0, 0, width, *energies, third, *fixed, part, None, None)

time: 146 us -> 148 us (1.014)
    ppermute x3, waiting for transfers between devices: 8.22 us -> 9.72 us  [per_device(): lax.ppermute(part, 'col', mirror)]
    pallas_call x1, Pallas kernels: 40.9 us -> 42.4 us  [gather_parts(): pl.pallas_call(gather_kernel, out_shape=[jax.ShapeDtypeStruct(shape, bf16...]
  transfers between devices with their start and end apart: 6 -> 6, of which waited for: 4 -> 3; matrix products, arithmetic and copies ran while one was open for 0% -> 0% of each run, Pallas kernels for 48% -> 47%
where the time goes in v6:
time: 148 us
  Pallas kernels  122 us (82%)
  waiting for transfers between devices  16.2 us (11%)
  starting transfers between devices  8.39 us (6%)
  between operations  1.55 us (1%)
    pallas_call x1, Pallas kernels, gather_parts(): pl.pallas_call(gather_kernel, out_shape=[jax.ShapeDtypeStruct(shape, bf16...  42.4 us
    pallas_call x3, Pallas kernels, piece(): pl.pallas_call(functools.partial(piece_kernel, i, k, low, high, end), out...  29.1 us
    pallas_call x1, Pallas kernels, own_cycle(): pl.pallas_call(own_cycle_kernel, out_shape=(jax.ShapeDtypeStruct((4, widt...  19.9 us
    pallas_call x1, Pallas kernels, row(): pl.pallas_call(functools.partial(row_kernel, i), out_shape=[jax.ShapeDtyp...  17.6 us
    pallas_call x1, Pallas kernels, own_ladder(): pl.pallas_call(own_ladder_kernel, out_shape=(jax.ShapeDtypeStruct((width,...  13 us
    ppermute x3, waiting for transfers between devices, per_device(): lax.ppermute(part, 'col', mirror)  9.72 us
    ppermute x1, waiting for transfers between devices, per_device(): side = lax.ppermute(far, 'col', [(i, i ^ 2) for i in range(cols)])  6.44 us
    ppermute x3, starting transfers between devices, per_device(): lax.ppermute(part, 'col', mirror)  3.53 us
  transfers between devices with their start and end apart: 6, of which 3 were waited for; matrix products, arithmetic and copies ran while one was open for 0% of the time, Pallas kernels for 47%

profile of v6, /device:TPU:6, one launch (start us, length us, event | category | flops | bytes accessed | tf_op | source)
XLA Modules:
  0.0 148.1 jit_solution(8983795139408708144)
XLA Ops:
  1.3 42.4 %gather_parts.1 = (bf16[8,2,64,768]{3,2,1,0:T(8,128)(2,1)}, bf16[16,4,64,1024]{3,2,1,0:T(8,128)(2,1)}, bf16[2,4,64,1024]{3,2,1,0:T(8,128)(2,1)}, bf16[768,384]{1...) custom-call(s32[1,1]{1,0:T(1,128)S(6)} %copy.21.count_ref, ...), custom_call_target="tpu_custom_call" | custom-call | tf_op jit(solution)/shard_map/gather_parts/pallas_call | solution.py:203
  43.7 1.3 collective-permute-start
  45.0 0.0 collective-permute-start.5
  45.0 3.5 %collective-permute-start.4 = (bf16[768,768]{1,0:T(8,128)(2,1)}, bf16[768,768]{1,0:T(8,128)(2,1)}, u32[]{:S(2)}, u32[]{:S(2)}) collective-permute-start(bf16[768,768]{1,0:T(8,128)(2,1)} %get-tuple-element.44), channel_id=1, source_target_pairs={{0,8},{1,9},{2,10},{3,11},{4,12},{5,13},{6,14},{7,15},{8,0},{9,1},... | collective-permute-start | bytes 3538952 | tf_op jit(solution)/shard_map/ppermute | solution.py:667
  48.6 13.0 %own_ladder.1 = (bf16[768,768]{1,0:T(8,128)(2,1)}, bf16[768,768]{1,0:T(8,128)(2,1)}, bf16[4,768,768]{2,1,0:T(8,128)(2,1)}) custom-call(s32[12]{0:T(128)} %bitcast.18, s32[1,1]{1,0:T(1,128)S(6)} %copy.21.count_ref, s32[16]{0:T(128)} %slot_ref.1, bf16[16,64,768]{2,1,0:T(8,128)(2,1)} %bitcast.11, ...), custom_call_target="tpu_custom_call" | custom-call | tf_op jit(solution)/shard_map/own_ladder/pallas_call | solution.py:262
  61.6 6.4 %collective-permute-done.side_ref = bf16[2,4,64,1024]{3,2,1,0:T(8,128)(2,1)} collective-permute-done((bf16[2,4,64,1024]{3,2,1,0:T(8,128)(2,1)}, bf16[2,4,64,1024]{3,2,1,0:T(8,128)(2,1)}, u32[]{:S(2)}, u32[]{:S(2)}) %collective-permute-start) | collective-permute-done | bytes 1048608 | tf_op jit(solution)/shard_map/ppermute | solution.py:668
  68.0 0.0 collective-permute-start.1
  68.1 0.0 collective-permute-start.3
  68.1 3.5 %collective-permute-start.2 = (bf16[768,256]{1,0:T(8,128)(2,1)}, bf16[768,256]{1,0:T(8,128)(2,1)}, u32[]{:S(2)}, u32[]{:S(2)}) collective-permute-start(bf16[768,256]{1,0:T(8,128)(2,1)} %get-tuple-element.37), channel_id=1, source_target_pairs={{0,8},{1,9},{2,10},{3,11},{4,12},{5,13},{6,14},{7,15},{8,0},{9,1},... | collective-permute-start | bytes 1179656 | tf_op jit(solution)/shard_map/ppermute | solution.py:672
  71.6 0.0 collective-permute-done.1.twin_ref
  71.6 19.9 %own_cycle.1 = (bf16[4,768,768]{2,1,0:T(8,128)(2,1)}, f32[4,768,768]{2,1,0:T(8,128)}, f32[768,1]{1,0:T(8,128)}, f32[1,768]{1,0:T(1,128)}) custom-call(s32[12]{0:T(128)} %bitcast.19, s32[1,1]{1,0:T(1,128)S(6)} %copy.21.count_ref, f32[1,1024]{1,0:T(1,128)} %bitcast.17, bf16[16,4,64,1024]{3,2,1,0:T(8,128)(2,1)} %get-tuple-element.28.wall_ref, ...), custom_call_target="tpu_custom_call" | custom-call | tf_op jit(solution)/shard_map/own_cycle/pallas_call | solution.py:365
  91.5 0.0 collective-permute-done.5.b1_hbm
  91.5 17.6 %row_0.1 = (f32[4,768,768]{2,1,0:T(8,128)}, bf16[4,768,768]{2,1,0:T(8,128)(2,1)}) custom-call(f32[2,2]{1,0:T(2,128)} %bitcast.13, f32[768,1]{1,0:T(8,128)} %get-tuple-element.35.vcol_ref, f32[1,768]{1,0:T(1,128)} %get-tuple-element.36.vrow_ref, bf16[768,384]{1,0:T(8,128)(2,1)} %get-tuple-element.45.b0_hbm, ...), custom_call_target="tpu_custom_call", output_to_operand_aliasing={{0}: (11, {})} | custom-call | tf_op jit(solution)/shard_map/row_0/pallas_call | solution.py:509
  109.1 4.6 %collective-permute-done.4.refs_0_ = bf16[768,768]{1,0:T(8,128)(2,1)} collective-permute-done((bf16[768,768]{1,0:T(8,128)(2,1)}, bf16[768,768]{1,0:T(8,128)(2,1)}, u32[]{:S(2)}, u32[]{:S(2)}) %collective-permute-start.4) | collective-permute-done | bytes 1179680 | tf_op jit(solution)/shard_map/ppermute | solution.py:667
  113.7 11.7 %piece_10_0.1.refs_7_ = f32[4,768,768]{2,1,0:T(8,128)} custom-call(f32[2,2]{1,0:T(2,128)} %bitcast.14, f32[768,1]{1,0:T(8,128)} %get-tuple-element.35.vcol_ref, f32[1,768]{1,0:T(1,128)} %get-tuple-element.36.vrow_ref, bf16[768,768]{1,0:T(8,128)(2,1)} %collective-permute-done.4.refs_0_, ...), custom_call_target="tpu_custom_call", output_to_operand_aliasing={{}: (10, {})} | custom-call | tf_op jit(solution)/shard_map/piece_10_0/pallas_call | solution.py:622
  125.4 5.1 %collective-permute-done.3.refs_0_ = bf16[768,512]{1,0:T(8,128)(2,1)} collective-permute-done((bf16[768,512]{1,0:T(8,128)(2,1)}, bf16[768,512]{1,0:T(8,128)(2,1)}, u32[]{:S(2)}, u32[]{:S(2)}) %collective-permute-start.3) | collective-permute-done | bytes 786464 | tf_op jit(solution)/shard_map/ppermute | solution.py:667
  130.5 7.5 %piece_11_0.1 = (f32[4,768,768]{2,1,0:T(8,128)}, f32[768,768]{1,0:T(8,128)}) custom-call(f32[2,2]{1,0:T(2,128)} %bitcast.15, f32[768,1]{1,0:T(8,128)} %get-tuple-element.35.vcol_ref, f32[1,768]{1,0:T(1,128)} %get-tuple-element.36.vrow_ref, bf16[768,512]{1,0:T(8,128)(2,1)} %collective-permute-done.3.refs_0_, ...), custom_call_target="tpu_custom_call", output_to_operand_aliasing={{0}: (10, {})} | custom-call | tf_op jit(solution)/shard_map/piece_11_0/pallas_call | solution.py:622
  138.0 0.0 collective-permute-done.2.refs_0_
  138.0 9.9 %piece_11_512.1 = (f32[4,768,768]{2,1,0:T(8,128)}, bf16[4,768,768]{2,1,0:T(8,128)(2,1)}) custom-call(f32[2,2]{1,0:T(2,128)} %bitcast.16, f32[768,1]{1,0:T(8,128)} %get-tuple-element.35.vcol_ref, f32[1,768]{1,0:T(1,128)} %get-tuple-element.36.vrow_ref, ...), custom_call_target="tpu_custom_call", output_to_operand_aliasing={{0}: (10, {}), {1}: (12, {})} | custom-call | tf_op jit(solution)/shard_map/piece_11_512/pallas_call | solution.py:622
Async XLA Ops:
  43.7 24.4 %collective-permute-start = (bf16[2,4,64,1024]{3,2,1,0:T(8,128)(2,1)}, bf16[2,4,64,1024]{3,2,1,0:T(8,128)(2,1)}, u32[]{:S(2)}, u32[]{:S(2)}) collective-permute-start(bf16[2,4,64,1024]{3,2,1,0:T(8,128)(2,1)} %get-tuple-element.29.far_ref), channel_id=1, source_target_pairs={{0,2},{1,3},{2,0},{3,1},{4,6},{5,7},{6,4},{7,5},{8,10},{9,11},{10,... | collective-permute-start | bytes 3145736 | tf_op jit(solution)/shard_map/ppermute | solution.py:668
  45.0 46.5 %collective-permute-start.5 = (bf16[768,1152]{1,0:T(8,128)(2,1)}, bf16[768,1152]{1,0:T(8,128)(2,1)}, u32[]{:S(2)}, u32[]{:S(2)}) collective-permute-start(bf16[768,1152]{1,0:T(8,128)(2,1)} %get-tuple-element.46), channel_id=1, source_target_pairs={{0,8},{1,9},{2,10},{3,11},{4,12},{5,13},{6,14},{7,15},{8,0},{9,1},... | collective-permute-start | bytes 5308424 | tf_op jit(solution)/shard_map/ppermute | solution.py:667
  45.0 68.6 %collective-permute-start.4 = (bf16[768,768]{1,0:T(8,128)(2,1)}, bf16[768,768]{1,0:T(8,128)(2,1)}, u32[]{:S(2)}, u32[]{:S(2)}) collective-permute-start(bf16[768,768]{1,0:T(8,128)(2,1)} %get-tuple-element.44), channel_id=1, source_target_pairs={{0,8},{1,9},{2,10},{3,11},{4,12},{5,13},{6,14},{7,15},{8,0},{9,1},... | collective-permute-start | bytes 3538952 | tf_op jit(solution)/shard_map/ppermute | solution.py:667
  68.0 3.5 %collective-permute-start.1 = (bf16[2,4,64,1024]{3,2,1,0:T(8,128)(2,1)}, bf16[2,4,64,1024]{3,2,1,0:T(8,128)(2,1)}, u32[]{:S(2)}, u32[]{:S(2)}) collective-permute-start(bf16[2,4,64,1024]{3,2,1,0:T(8,128)(2,1)} %collective-permute-done.side_ref), channel_id=1, source_target_pairs={{0,1},{1,0},{2,3},{3,2},{4,5},{5,4},{6,7},{7,6},{8,9},{9,8},{10,11... | collective-permute-start | bytes 3145736 | tf_op jit(solution)/shard_map/ppermute | solution.py:673
  68.1 62.5 %collective-permute-start.3 = (bf16[768,512]{1,0:T(8,128)(2,1)}, bf16[768,512]{1,0:T(8,128)(2,1)}, u32[]{:S(2)}, u32[]{:S(2)}) collective-permute-start(bf16[768,512]{1,0:T(8,128)(2,1)} %get-tuple-element.43), channel_id=1, source_target_pairs={{0,8},{1,9},{2,10},{3,11},{4,12},{5,13},{6,14},{7,15},{8,0},{9,1},... | collective-permute-start | bytes 2359304 | tf_op jit(solution)/shard_map/ppermute | solution.py:667
  68.1 69.9 %collective-permute-start.2 = (bf16[768,256]{1,0:T(8,128)(2,1)}, bf16[768,256]{1,0:T(8,128)(2,1)}, u32[]{:S(2)}, u32[]{:S(2)}) collective-permute-start(bf16[768,256]{1,0:T(8,128)(2,1)} %get-tuple-element.37), channel_id=1, source_target_pairs={{0,8},{1,9},{2,10},{3,11},{4,12},{5,13},{6,14},{7,15},{8,0},{9,1},... | collective-permute-start | bytes 1179656 | tf_op jit(solution)/shard_map/ppermute | solution.py:672

commit v7 on v6

--- a/solution.py
+++ b/solution.py
@@ -39,8 +39,7 @@
 
 
 def gather_kernel(
-    count_ref, x_ref, w_ref, amps_ref, core_ref,
-    xall_ref, wall_ref, far_ref, first_ref, coret_ref, live_ref, *refs
+    x_ref, w_ref, amps_ref, core_ref, xall_ref, wall_ref, far_ref, first_ref, coret_ref, *refs
 ):
     cuts, (plain, turned, fixed, wsend, wrecv, xsend, xrecv, msend, mrecv, local, tsem) = refs[:-11], refs[-11:]
     r = lax.axis_index("row")
@@ -90,17 +89,9 @@
         x = (c // 4 + offset) % (cols // 4)
         send(shard(offset, 0, 0), wall_ref.at[x * 4 + c % 4], wsems, 6 + offset, twin)
 
-    def live(shape, axis):
-        at = lax.broadcasted_iota(jnp.int32, shape, axis)
-        return jnp.where(at < count_ref[0, 0] * x_ref.shape[1], 1.0, 0.0)
-
-    live_rows, live_cols = live((width, 1), 0), live((1, width), 1)
-
     def transpose(q, p):
         amps_in[q].wait()
         for cut in strips(width, 256):
-            mask = live_rows[cut.start:cut.start + cut.size] * live_cols
-            plain[q, cut, :] = (plain[q, cut, :].astype(jnp.float32) * mask).astype(plain.dtype)
             turned[p, :, cut] = plain[q, cut, :].T
 
     own = wall_ref.at[c]
@@ -166,7 +157,6 @@
     for cut in strips(width, 256):
         fixed[1, :, cut] = fixed[0, cut, :].T
     outs.append(pltpu.make_async_copy(fixed.at[1], coret_ref, local.at[2]))
-    outs.append(pltpu.make_async_copy(plain, live_ref, local.at[8]))
     for copy in outs:
         copy.start()
     part = shard(3, 1, 0)
@@ -190,20 +180,20 @@
         copy.wait()
 
 
-def gather_parts(count, x_factor, shard, amp4, core, early, split):
+def gather_parts(x_factor, shard, amp4, core, early, split):
     rows = lax.axis_size("row")
     cols = lax.axis_size("col")
     width = amp4.shape[1]
     hbm = pl.BlockSpec(memory_space=pl.ANY)
     bf16 = jnp.bfloat16
     dma = pltpu.SemaphoreType.DMA
-    shapes = [(rows,) + x_factor.shape, (cols,) + shard.shape, (2,) + shard.shape, (width, early), core.shape, amp4.shape]
+    shapes = [(rows,) + x_factor.shape, (cols,) + shard.shape, (2,) + shard.shape, (width, early), core.shape]
     shapes += [(width, 2 * width - early), (width, width)]
     shapes += [(width, split), (width, width - split)]
     return pl.pallas_call(
         gather_kernel,
         out_shape=[jax.ShapeDtypeStruct(shape, bf16) for shape in shapes],
-        in_specs=[pl.BlockSpec(memory_space=pltpu.SMEM)] + [hbm] * 4,
+        in_specs=[hbm] * 4,
         out_specs=[hbm] * len(shapes),
         scratch_shapes=[
             pltpu.VMEM(amp4.shape, bf16),
@@ -215,14 +205,14 @@
             dma((14,)),
             dma((1,)),
             dma((1,)),
-            dma((9,)),
+            dma((8,)),
             dma((5,)),
         ],
         compiler_params=pltpu.CompilerParams(
             collective_id=0, has_side_effects=True, vmem_limit_bytes=VMEM_LIMIT
         ),
         name="gather_parts",
-    )(count, x_factor, shard, amp4, core)
+    )(x_factor, shard, amp4, core)
 
 
 def own_ladder_kernel(
@@ -348,12 +338,10 @@
                     wsel.at[pl.ds(2 * first, 2), pl.ds(s * tile, tile), :],
                     sem.at[first, s],
                 ).wait()
-            live = lax.broadcasted_iota(jnp.int32, (width, 1), 0) < count_ref[0, 0] * tile
             for k in range(2):
-                picked = dot(wsel[2 * first + k], pick[...])
-                wd_ref[k] = jnp.where(live, picked, 0.0).astype(wd_ref.dtype)
-
-    cyc_ref[0] = dot(wd_ref[0], a0_ref[0]) + dot(wd_ref[1], a1_ref[0])
+                wd_ref[k] = dot(wsel[2 * first + k], pick[...]).astype(wd_ref.dtype)
+
+    cyc_ref[0] = (dot(wd_ref[0], a0_ref[0]) + dot(wd_ref[1], a1_ref[0])).astype(cyc_ref.dtype)
 
 
 def own_cycle(tiles, count, virt, wall, far, side, twin, amp4):
@@ -366,7 +354,7 @@
         own_cycle_kernel,
         out_shape=(
             jax.ShapeDtypeStruct((4, width, width), bf16),
-            jax.ShapeDtypeStruct((4, width, width), f32),
+            jax.ShapeDtypeStruct((4, width, width), bf16),
             jax.ShapeDtypeStruct((width, 1), f32),
             jax.ShapeDtypeStruct((1, width), f32),
         ),
@@ -422,17 +410,21 @@
             copy.wait()
 
 
-def emit(mover, last, pair, j, rows, raw, occ_ref, vcol_ref, vrow_ref, part, amps, upd, res_hbm, upd_hbm):
-    raw = raw + part[j, rows, :]
-    part[j, rows, :] = raw
-    mover.put(part.at[j, rows, :], res_hbm.at[pair, rows, :])
-    if last:
-        gap = (occ_ref[0, pair // 2] + occ_ref[1, pair % 2]) - vcol_ref[rows, :] - vrow_ref[...]
-        inverse = pl.reciprocal(gap, approx=True)
-        inverse = inverse * (2.0 - gap * inverse)
-        own = amps[j, rows, :].astype(jnp.float32)
-        upd[j, rows, :] = (own + raw * inverse).astype(upd.dtype)
-        mover.put(upd.at[j, rows, :], upd_hbm.at[pair, rows, :])
+def emit(mover, pair, j, rows, raw, count_ref, occ_ref, vcol_ref, vrow_ref, part, amps, res, upd, res_hbm, upd_hbm):
+    height, width = raw.shape
+    count = count_ref[0, 0] * 64
+    live = (lax.broadcasted_iota(jnp.int32, (height, 1), 0) + rows.start < count) & (
+        lax.broadcasted_iota(jnp.int32, (1, width), 1) < count
+    )
+    raw = jnp.where(live, raw + part[j, rows, :].astype(jnp.float32), 0.0)
+    own = jnp.where(live, amps[j, rows, :].astype(jnp.float32), 0.0)
+    gap = (occ_ref[0, pair // 2] + occ_ref[1, pair % 2]) - vcol_ref[rows, :] - vrow_ref[...]
+    inverse = pl.reciprocal(gap, approx=True)
+    inverse = inverse * (2.0 - gap * inverse)
+    res[j, rows, :] = raw
+    mover.put(res.at[j, rows, :], res_hbm.at[pair, rows, :])
+    upd[j, rows, :] = (own + raw * inverse).astype(upd.dtype)
+    mover.put(upd.at[j, rows, :], upd_hbm.at[pair, rows, :])
 
 
 def emit_behind(products, emit_one):
@@ -446,8 +438,8 @@
 
 
 def row_kernel(
-    i, occ_ref, vcol_ref, vrow_ref, b0_hbm, b1_hbm, xt_hbm, x_hbm, coret_hbm, wt_hbm, wd_hbm,
-    amps_hbm, part_hbm, res_hbm, upd_hbm, xt, coret, wt, right, left, part, amps, proj, total, upd, sem, osem,
+    i, count_ref, occ_ref, vcol_ref, vrow_ref, b0_hbm, b1_hbm, xt_hbm, x_hbm, coret_hbm, wt_hbm, wd_hbm,
+    amps_hbm, part_hbm, res_hbm, upd_hbm, xt, coret, wt, right, left, part, amps, proj, total, res, upd, sem, osem,
 ):
     width, points = x_hbm.shape
     early = b0_hbm.shape[1]
@@ -491,15 +483,15 @@
 
     def emit_one(j, rows, raw):
         emit(
-            mover, True, 2 * i + j, j, rows, raw, occ_ref, vcol_ref, vrow_ref,
-            part, amps, upd, res_hbm, upd_hbm,
+            mover, 2 * i + j, j, rows, raw, count_ref, occ_ref, vcol_ref, vrow_ref,
+            part, amps, res, upd, res_hbm, upd_hbm,
         )
 
     emit_behind(products(), emit_one)
     mover.drain()
 
 
-def row(i, occ, vcol, vrow, b0, b1, xt, x, coret, wt, wd, amp4, part):
+def row(i, count, occ, vcol, vrow, b0, b1, xt, x, coret, wt, wd, amp4, part):
     width, points = x.shape
     vmem = pl.BlockSpec(memory_space=pltpu.VMEM)
     smem = pl.BlockSpec(memory_space=pltpu.SMEM)
@@ -509,7 +501,7 @@
     return pl.pallas_call(
         functools.partial(row_kernel, i),
         out_shape=[jax.ShapeDtypeStruct(part.shape, f32), jax.ShapeDtypeStruct(part.shape, bf16)],
-        in_specs=[smem, vmem, vmem] + [hbm] * 9,
+        in_specs=[smem, smem, vmem, vmem] + [hbm] * 9,
         out_specs=[hbm] * 2,
         scratch_shapes=[
             pltpu.VMEM((points, width), bf16),
@@ -517,45 +509,38 @@
             pltpu.VMEM((2, points, points), bf16),
             pltpu.VMEM((2, width, depth), bf16),
             pltpu.VMEM((width, depth), bf16),
-            pltpu.VMEM((2, width, width), f32),
+            pltpu.VMEM((2, width, width), bf16),
             pltpu.VMEM((2, width, width), bf16),
             pltpu.VMEM((points, width), bf16),
             pltpu.VMEM((2, points, points), bf16),
+            pltpu.VMEM((2, width, width), f32),
             pltpu.VMEM((2, width, width), bf16),
             pltpu.SemaphoreType.DMA((15,)),
             pltpu.SemaphoreType.DMA((4 * (width // STRIP),)),
         ],
-        input_output_aliases={11: 0},
         compiler_params=pltpu.CompilerParams(vmem_limit_bytes=VMEM_LIMIT),
         name="row_%d" % i,
-    )(occ, vcol, vrow, b0, b1, xt, x, coret, wt, wd, amp4, part)
-
-
-def piece_kernel(i, k, low, high, end, occ_ref, vcol_ref, vrow_ref, *refs):
+    )(count, occ, vcol, vrow, b0, b1, xt, x, coret, wt, wd, amp4, part)
+
+
+def piece_kernel(i, k, low, high, end, count_ref, occ_ref, vcol_ref, vrow_ref, *refs):
     last = k == 1 and end
     scratch = 13
-    refs, (xt, coret, wt, right, left, part, amps, acc, proj, total, upd, sem, osem) = (
+    refs, (xt, coret, before, right, left, part, amps, proj, total, res, upd, sem, osem) = (
         refs[:-scratch], refs[-scratch:]
     )
-    (b_hbm, xt_hbm, x_hbm, coret_hbm, wt_hbm, wd_hbm, amps_hbm, part_hbm) = refs[:8]
-    refs = list(refs[8:])
-    acc_in = refs.pop(0) if low > 0 else None
-    upd_hbm = refs.pop() if last else None
-    acc_out = None if end else refs.pop()
-    res_hbm = refs.pop()
+    (b_hbm, xt_hbm, x_hbm, coret_hbm, before_hbm, wd_hbm, amps_hbm, part_hbm) = refs[:8]
+    outs = refs[8:]
     width, points = x_hbm.shape
     head, rest = pl.ds(0, points), pl.ds(points, high - low)
     cut = pl.ds(low, high - low)
     plan = {
         "b": (b_hbm, left.at[:, rest]),
         "xt": (xt_hbm, xt),
-        "x": (x_hbm, right.at[k, :, head]),
+        "x": (x_hbm, right.at[k, :, head]) if end else (x_hbm.at[cut], right.at[k, cut, head]),
+        "coret": (coret_hbm, coret),
+        "before": (before_hbm if low > 0 else before_hbm.at[2 * i + k], before),
     }
-    if low > 0:
-        plan["acc"] = (acc_in, acc)
-    if end:
-        plan["wt"] = (wt_hbm.at[2 * i + k], wt)
-        plan["coret"] = (coret_hbm, coret)
     for j in (1 - k, k):
         plan["w%d" % j] = (wd_hbm.at[2 * j + k, :, cut], right.at[j, :, rest])
         plan["part%d" % j] = (part_hbm.at[2 * i + j], part.at[j])
@@ -574,33 +559,33 @@
                 yield j, rows, product
 
     def emit_one(j, rows, raw):
-        emit(
-            mover, last, 2 * i + j, j, rows, raw, occ_ref, vcol_ref, vrow_ref,
-            part, amps, upd, res_hbm, upd_hbm,
-        )
+        if last:
+            emit(
+                mover, 2 * i + j, j, rows, raw, count_ref, occ_ref, vcol_ref, vrow_ref,
+                part, amps, res, upd, outs[-2], outs[-1],
+            )
+        else:
+            part[j, rows, :] = (raw + part[j, rows, :].astype(jnp.float32)).astype(part.dtype)
+            mover.put(part.at[j, rows, :], outs[0].at[2 * i + j, rows, :])
 
     mover.need("b", "xt")
     proj[...] = dot(xt[...], left[:, rest]).astype(proj.dtype)
     mover.need("x")
     inner = dot(proj[...], right[k, cut, head])
-    if low > 0:
-        mover.need("acc")
-        inner = inner + acc[...]
+    mover.need("coret", "before")
+    total[...] = (
+        before[...].astype(jnp.float32) + coret[...].astype(jnp.float32) * inner
+    ).astype(total.dtype)
     if end:
-        mover.need("wt", "coret")
-        total[...] = (
-            wt[...].astype(jnp.float32) + coret[...].astype(jnp.float32) * inner
-        ).astype(total.dtype)
         left[:, head] = dot(right[k, :, head], total[...]).astype(left.dtype)
         emit_behind(products([(1 - k, rest), (k, pl.ds(0, points + high - low))]), emit_one)
     else:
-        acc[...] = inner
-        mover.put(acc, acc_out)
+        mover.put(total, outs[1])
         emit_behind(products([(1 - k, rest), (k, rest)]), emit_one)
     mover.drain()
 
 
-def piece(i, k, low, high, occ, vcol, vrow, b, xt, x, coret, wt, wd, amp4, part, acc, updated):
+def piece(i, k, low, high, count, occ, vcol, vrow, b, xt, x, coret, before, wd, amp4, part, residual, updated):
     width, points = x.shape
     end = high == width
     last = k == 1 and end
@@ -608,21 +593,20 @@
     smem = pl.BlockSpec(memory_space=pltpu.SMEM)
     hbm = pl.BlockSpec(memory_space=pl.ANY)
     f32, bf16 = jnp.float32, jnp.bfloat16
-    operands = [occ, vcol, vrow, b, xt, x, coret, wt, wd, amp4, part]
-    out_shape = [jax.ShapeDtypeStruct(part.shape, f32)]
-    alias = {len(operands) - 1: 0}
-    if low > 0:
-        operands.append(acc)
-    if not end:
-        out_shape.append(jax.ShapeDtypeStruct((points, points), f32))
+    operands = [count, occ, vcol, vrow, b, xt, x, coret, before, wd, amp4, part]
     if last:
-        out_shape.append(jax.ShapeDtypeStruct(part.shape, bf16))
-        alias[len(operands)] = 1
-        operands.append(updated)
+        out_shape = [jax.ShapeDtypeStruct(part.shape, f32), jax.ShapeDtypeStruct(part.shape, bf16)]
+        alias = {len(operands): 0, len(operands) + 1: 1}
+        operands += [residual, updated]
+    else:
+        out_shape = [jax.ShapeDtypeStruct(part.shape, bf16)]
+        alias = {len(operands) - 1: 0}
+        if not end:
+            out_shape.append(jax.ShapeDtypeStruct((points, points), bf16))
     return pl.pallas_call(
         functools.partial(piece_kernel, i, k, low, high, end),
         out_shape=out_shape,
-        in_specs=[smem, vmem, vmem] + [hbm] * (len(operands) - 3),
+        in_specs=[smem, smem, vmem, vmem] + [hbm] * (len(operands) - 4),
         out_specs=[hbm] * len(out_shape),
         scratch_shapes=[
             pltpu.VMEM((points, width), bf16),
@@ -630,14 +614,14 @@
             pltpu.VMEM((points, points), bf16),
             pltpu.VMEM((2, width, points + high - low), bf16),
             pltpu.VMEM((width, points + high - low), bf16),
+            pltpu.VMEM((2, width, width), bf16),
+            pltpu.VMEM((2, width, width), bf16),
+            pltpu.VMEM((points, high - low), bf16),
+            pltpu.VMEM((points, points), bf16),
             pltpu.VMEM((2, width, width), f32),
             pltpu.VMEM((2, width, width), bf16),
-            pltpu.VMEM((points, points), f32),
-            pltpu.VMEM((points, high - low), bf16),
-            pltpu.VMEM((points, points), bf16),
-            pltpu.VMEM((2, width, width), bf16),
-            pltpu.SemaphoreType.DMA((12,)),
-            pltpu.SemaphoreType.DMA((9,)),
+            pltpu.SemaphoreType.DMA((11,)),
+            pltpu.SemaphoreType.DMA((8,)),
         ],
         input_output_aliases=alias,
         compiler_params=pltpu.CompilerParams(vmem_limit_bytes=VMEM_LIMIT),
@@ -659,9 +643,7 @@
 
     early, split = width // 2, 512
     tiles, count = domain_tiles[0, 0], domain_count
-    xall, wall, far, first, coret, amp4, *turned = gather_parts(
-        count, x_factor, shard, amp4, core, early, split
-    )
+    xall, wall, far, first, coret, *turned = gather_parts(x_factor, shard, amp4, core, early, split)
     xall = xall.reshape(-1, tile_width, grid_points)
     mirror = [(i, (i + cols // 2) % cols) for i in range(cols)]
     second, third, fourth = [lax.ppermute(part, "col", mirror) for part in turned[:3]]
@@ -672,13 +654,15 @@
     fifth = lax.ppermute(tail, "col", mirror)
     twin = lax.ppermute(side, "col", [(i, i ^ 1) for i in range(cols)])
     wd, part, vcol, vrow = own_cycle(tiles, count, virt_energy[None, :], wall, far, side, twin, amp4)
-    energies = (occ_energy[0, 0], vcol, vrow)
-    part, updated = row(0, *energies, first, second, xt, x, coret, wt, wd, amp4, part)
-    fixed = (xt, x, coret, wt, wd, amp4)
-    part, = piece(1, 0, 0, width, *energies, third, *fixed, part, None, None)
-    part, acc = piece(1, 1, 0, split, *energies, fourth, *fixed, part, None, None)
-    part, updated = piece(1, 1, split, width, *energies, fifth, *fixed, part, acc, updated)
-    return part.reshape(amps.shape), updated.reshape(amps.shape)
+    energies = (count, occ_energy[0, 0], vcol, vrow)
+    residual, updated = row(0, *energies, first, second, xt, x, coret, wt, wd, amp4, part)
+    fixed = (xt, x, coret)
+    part, = piece(1, 0, 0, width, *energies, third, *fixed, wt, wd, amp4, part, None, None)
+    part, total = piece(1, 1, 0, split, *energies, fourth, *fixed, wt, wd, amp4, part, None, None)
+    residual, updated = piece(
+        1, 1, split, width, *energies, fifth, *fixed, total, wd, amp4, part, residual, updated
+    )
+    return residual.reshape(amps.shape), updated.reshape(amps.shape)
 
 
 def solution(mesh):

time: 148 us -> 146 us (0.986)
  Pallas kernels: 122 us -> 120 us
where the time goes in v7:
time: 146 us
  Pallas kernels  120 us (82%)
  waiting for transfers between devices  16.1 us (11%)
  starting transfers between devices  8.39 us (6%)
  between operations  1.52 us (1%)
    pallas_call x1, Pallas kernels, gather_parts(): pl.pallas_call(gather_kernel, out_shape=[jax.ShapeDtypeStruct(shape, bf16...  41 us
    pallas_call x3, Pallas kernels, piece(): pl.pallas_call(functools.partial(piece_kernel, i, k, low, high, end), out...  28.7 us
    pallas_call x1, Pallas kernels, own_cycle(): pl.pallas_call(own_cycle_kernel, out_shape=(jax.ShapeDtypeStruct((4, widt...  19.1 us
    pallas_call x1, Pallas kernels, row(): pl.pallas_call(functools.partial(row_kernel, i), out_shape=[jax.ShapeDtyp...  17.9 us
    pallas_call x1, Pallas kernels, own_ladder(): pl.pallas_call(own_ladder_kernel, out_shape=(jax.ShapeDtypeStruct((width,...  13.1 us
    ppermute x3, waiting for transfers between devices, per_device(): lax.ppermute(part, 'col', mirror)  8.88 us
    ppermute x1, waiting for transfers between devices, per_device(): side = lax.ppermute(far, 'col', [(i, i ^ 2) for i in range(cols)])  7.18 us
    ppermute x3, starting transfers between devices, per_device(): lax.ppermute(part, 'col', mirror)  3.53 us
  transfers between devices with their start and end apart: 6, of which 3 were waited for; matrix products, arithmetic and copies ran while one was open for 0% of the time, Pallas kernels for 47%

profile of v7, /device:TPU:6, one launch (start us, length us, event | category | flops | bytes accessed | tf_op | source)
XLA Modules:
  0.0 145.8 jit_solution(7423500131008017889)
XLA Ops:
  0.6 41.0 %gather_parts.1 = (bf16[8,2,64,768]{3,2,1,0:T(8,128)(2,1)}, bf16[16,4,64,1024]{3,2,1,0:T(8,128)(2,1)}, bf16[2,4,64,1024]{3,2,1,0:T(8,128)(2,1)}, bf16[768,384]{1...) custom-call(bf16[2,64,768]{2,1,0:T(8,128)(2,1)} %x_ref.1, ...), custom_call_target="tpu_custom_call" | custom-call | tf_op jit(solution)/shard_map/gather_parts/pallas_call | solution.py:193
  41.6 1.3 collective-permute-start
  42.9 0.0 collective-permute-start.5
  42.9 3.5 %collective-permute-start.4 = (bf16[768,768]{1,0:T(8,128)(2,1)}, bf16[768,768]{1,0:T(8,128)(2,1)}, u32[]{:S(2)}, u32[]{:S(2)}) collective-permute-start(bf16[768,768]{1,0:T(8,128)(2,1)} %get-tuple-element.42), channel_id=1, source_target_pairs={{0,8},{1,9},{2,10},{3,11},{4,12},{5,13},{6,14},{7,15},{8,0},{9,1},... | collective-permute-start | bytes 3538952 | tf_op jit(solution)/shard_map/ppermute | solution.py:649
  47.1 13.1 %own_ladder.1 = (bf16[768,768]{1,0:T(8,128)(2,1)}, bf16[768,768]{1,0:T(8,128)(2,1)}, bf16[4,768,768]{2,1,0:T(8,128)(2,1)}) custom-call(s32[12]{0:T(128)} %bitcast.25, s32[1,1]{1,0:T(1,128)S(6)} %copy.19.count_ref, s32[16]{0:T(128)} %slot_ref.1, bf16[16,64,768]{2,1,0:T(8,128)(2,1)} %bitcast.18, bf16[4,768,768]{2,1,0:T(8,128)(2,1)} %bitcast.9, ...), custom_call_target="tpu_custom_call" | custom-call | tf_op jit(solution)/shard_map/own_ladder/pallas_call | solution.py:252
  60.2 7.2 %collective-permute-done.side_ref = bf16[2,4,64,1024]{3,2,1,0:T(8,128)(2,1)} collective-permute-done((bf16[2,4,64,1024]{3,2,1,0:T(8,128)(2,1)}, bf16[2,4,64,1024]{3,2,1,0:T(8,128)(2,1)}, u32[]{:S(2)}, u32[]{:S(2)}) %collective-permute-start) | collective-permute-done | bytes 1048608 | tf_op jit(solution)/shard_map/ppermute | solution.py:650
  67.4 0.0 collective-permute-start.1
  67.4 0.0 collective-permute-start.3
  67.4 3.5 %collective-permute-start.2 = (bf16[768,256]{1,0:T(8,128)(2,1)}, bf16[768,256]{1,0:T(8,128)(2,1)}, u32[]{:S(2)}, u32[]{:S(2)}) collective-permute-start(bf16[768,256]{1,0:T(8,128)(2,1)} %get-tuple-element.35), channel_id=1, source_target_pairs={{0,8},{1,9},{2,10},{3,11},{4,12},{5,13},{6,14},{7,15},{8,0},{9,1},... | collective-permute-start | bytes 1179656 | tf_op jit(solution)/shard_map/ppermute | solution.py:654
  70.9 0.0 collective-permute-done.1.twin_ref
  70.9 19.1 %own_cycle.1 = (bf16[4,768,768]{2,1,0:T(8,128)(2,1)}, bf16[4,768,768]{2,1,0:T(8,128)(2,1)}, f32[768,1]{1,0:T(8,128)}, f32[1,768]{1,0:T(1,128)}) custom-call(s32[12]{0:T(128)} %bitcast.26, s32[1,1]{1,0:T(1,128)S(6)} %copy.19.count_ref, f32[1,1024]{1,0:T(1,128)} %bitcast.24, bf16[16,4,64,1024]{3,2,1,0:T(8,128)(2,1)} %get-tuple-element.27.wall_ref, ...), custom_call_target="tpu_custom_call" | custom-call | tf_op jit(solution)/shard_map/own_cycle/pallas_call | solution.py:353
  90.1 0.0 collective-permute-done.5.b1_hbm
  90.1 17.9 %row_0.1 = (f32[4,768,768]{2,1,0:T(8,128)}, bf16[4,768,768]{2,1,0:T(8,128)(2,1)}) custom-call(s32[1,1]{1,0:T(1,128)S(6)} %copy.19.count_ref, f32[2,2]{1,0:T(2,128)} %bitcast.20, f32[768,1]{1,0:T(8,128)} %get-tuple-element.33.vcol_ref, f32[1,768]{1,0:T(1,128)} %get-tuple-element.34.vrow_ref, bf16[768,384]{1,0:T(8,128)(2,1)} %get-tuple-element.46.b0_hbm, ...), custom_call_target="tpu_custom_call" | custom-call | tf_op jit(solution)/shard_map/row_0/pallas_call | solution.py:501
  108.0 3.5 %collective-permute-done.4.refs_0_ = bf16[768,768]{1,0:T(8,128)(2,1)} collective-permute-done((bf16[768,768]{1,0:T(8,128)(2,1)}, bf16[768,768]{1,0:T(8,128)(2,1)}, u32[]{:S(2)}, u32[]{:S(2)}) %collective-permute-start.4) | collective-permute-done | bytes 1179680 | tf_op jit(solution)/shard_map/ppermute | solution.py:649
  111.5 11.4 %piece_10_0.1.refs_7_ = bf16[4,768,768]{2,1,0:T(8,128)(2,1)} custom-call(s32[1,1]{1,0:T(1,128)S(6)} %copy.19.count_ref, f32[2,2]{1,0:T(2,128)} %bitcast.21, f32[768,1]{1,0:T(8,128)} %get-tuple-element.33.vcol_ref, f32[1,768]{1,0:T(1,128)} %get-tuple-element.34.vrow_ref, ...), custom_call_target="tpu_custom_call", output_to_operand_aliasing={{}: (11, {})} | custom-call | tf_op jit(solution)/shard_map/piece_10_0/pallas_call | solution.py:606
  123.0 5.4 %collective-permute-done.3.refs_0_ = bf16[768,512]{1,0:T(8,128)(2,1)} collective-permute-done((bf16[768,512]{1,0:T(8,128)(2,1)}, bf16[768,512]{1,0:T(8,128)(2,1)}, u32[]{:S(2)}, u32[]{:S(2)}) %collective-permute-start.3) | collective-permute-done | bytes 786464 | tf_op jit(solution)/shard_map/ppermute | solution.py:649
  128.4 7.5 %piece_11_0.1 = (bf16[4,768,768]{2,1,0:T(8,128)(2,1)}, bf16[768,768]{1,0:T(8,128)(2,1)}) custom-call(s32[1,1]{1,0:T(1,128)S(6)} %copy.19.count_ref, f32[2,2]{1,0:T(2,128)} %bitcast.22, f32[768,1]{1,0:T(8,128)} %get-tuple-element.33.vcol_ref, f32[1,768]{1,0:T(1,128)} %get-tuple-element.34.vrow_ref, ...), custom_call_target="tpu_custom_call", output_to_operand_aliasing={{0}: (11, {})} | custom-call | tf_op jit(solution)/shard_map/piece_11_0/pallas_call | solution.py:606
  135.8 0.0 collective-permute-done.2.refs_0_
  135.9 9.7 %piece_11_512.1 = (f32[4,768,768]{2,1,0:T(8,128)}, bf16[4,768,768]{2,1,0:T(8,128)(2,1)}) custom-call(s32[1,1]{1,0:T(1,128)S(6)} %copy.19.count_ref, f32[2,2]{1,0:T(2,128)} %bitcast.23, f32[768,1]{1,0:T(8,128)} %get-tuple-element.33.vcol_ref, f32[1,768]{1,0:T(1,128)} %get-tuple-element.34.vrow_ref, ...), custom_call_target="tpu_custom_call", output_to_operand_aliasing={{0}: (12, {}), {1}: (13, {})} | custom-call | tf_op jit(solution)/shard_map/piece_11_512/pallas_call | solution.py:606
Async XLA Ops:
  41.6 25.8 %collective-permute-start = (bf16[2,4,64,1024]{3,2,1,0:T(8,128)(2,1)}, bf16[2,4,64,1024]{3,2,1,0:T(8,128)(2,1)}, u32[]{:S(2)}, u32[]{:S(2)}) collective-permute-start(bf16[2,4,64,1024]{3,2,1,0:T(8,128)(2,1)} %get-tuple-element.28.far_ref), channel_id=1, source_target_pairs={{0,2},{1,3},{2,0},{3,1},{4,6},{5,7},{6,4},{7,5},{8,10},{9,11},{10,... | collective-permute-start | bytes 3145736 | tf_op jit(solution)/shard_map/ppermute | solution.py:650
  42.9 47.1 %collective-permute-start.5 = (bf16[768,1152]{1,0:T(8,128)(2,1)}, bf16[768,1152]{1,0:T(8,128)(2,1)}, u32[]{:S(2)}, u32[]{:S(2)}) collective-permute-start(bf16[768,1152]{1,0:T(8,128)(2,1)} %get-tuple-element.47), channel_id=1, source_target_pairs={{0,8},{1,9},{2,10},{3,11},{4,12},{5,13},{6,14},{7,15},{8,0},{9,1},... | collective-permute-start | bytes 5308424 | tf_op jit(solution)/shard_map/ppermute | solution.py:649
  42.9 68.6 %collective-permute-start.4 = (bf16[768,768]{1,0:T(8,128)(2,1)}, bf16[768,768]{1,0:T(8,128)(2,1)}, u32[]{:S(2)}, u32[]{:S(2)}) collective-permute-start(bf16[768,768]{1,0:T(8,128)(2,1)} %get-tuple-element.42), channel_id=1, source_target_pairs={{0,8},{1,9},{2,10},{3,11},{4,12},{5,13},{6,14},{7,15},{8,0},{9,1},... | collective-permute-start | bytes 3538952 | tf_op jit(solution)/shard_map/ppermute | solution.py:649
  67.4 3.5 %collective-permute-start.1 = (bf16[2,4,64,1024]{3,2,1,0:T(8,128)(2,1)}, bf16[2,4,64,1024]{3,2,1,0:T(8,128)(2,1)}, u32[]{:S(2)}, u32[]{:S(2)}) collective-permute-start(bf16[2,4,64,1024]{3,2,1,0:T(8,128)(2,1)} %collective-permute-done.side_ref), channel_id=1, source_target_pairs={{0,1},{1,0},{2,3},{3,2},{4,5},{5,4},{6,7},{7,6},{8,9},{9,8},{10,11... | collective-permute-start | bytes 3145736 | tf_op jit(solution)/shard_map/ppermute | solution.py:655
  67.4 61.0 %collective-permute-start.3 = (bf16[768,512]{1,0:T(8,128)(2,1)}, bf16[768,512]{1,0:T(8,128)(2,1)}, u32[]{:S(2)}, u32[]{:S(2)}) collective-permute-start(bf16[768,512]{1,0:T(8,128)(2,1)} %get-tuple-element.39), channel_id=1, source_target_pairs={{0,8},{1,9},{2,10},{3,11},{4,12},{5,13},{6,14},{7,15},{8,0},{9,1},... | collective-permute-start | bytes 2359304 | tf_op jit(solution)/shard_map/ppermute | solution.py:649
  67.4 68.5 %collective-permute-start.2 = (bf16[768,256]{1,0:T(8,128)(2,1)}, bf16[768,256]{1,0:T(8,128)(2,1)}, u32[]{:S(2)}, u32[]{:S(2)}) collective-permute-start(bf16[768,256]{1,0:T(8,128)(2,1)} %get-tuple-element.35), channel_id=1, source_target_pairs={{0,8},{1,9},{2,10},{3,11},{4,12},{5,13},{6,14},{7,15},{8,0},{9,1},... | collective-permute-start | bytes 1179656 | tf_op jit(solution)/shard_map/ppermute | solution.py:654

commit v8 on v7

--- a/solution.py
+++ b/solution.py
@@ -14,10 +14,6 @@
 
 def dot(a, b):
     return jnp.dot(a, b, preferred_element_type=jnp.float32)
-
-
-def dot_nt(a, b):
-    return lax.dot_general(a, b, (((1,), (1,)), ((), ())), preferred_element_type=jnp.float32)
 
 
 def strips(width, step):
@@ -286,12 +282,12 @@
 
 def own_cycle_kernel(
     tiles_ref, count_ref, virt_ref, wall_ref, far_ref, side_ref, twin_ref, a0_ref, a1_ref,
-    wd_ref, cyc_ref, vcol_ref, vrow_ref, wsel, pick, sem,
+    wdt_ref, cyc_ref, vcol_ref, vrow_ref, wsel, wd, pick, sem,
 ):
     p = pl.program_id(0)
     tile = wall_ref.shape[2]
     slots = tiles_ref.shape[0]
-    width = wd_ref.shape[1]
+    width = wd.shape[1]
     window = virt_ref.shape[1]
 
     @pl.when(p == 0)
@@ -339,9 +335,11 @@
                     sem.at[first, s],
                 ).wait()
             for k in range(2):
-                wd_ref[k] = dot(wsel[2 * first + k], pick[...]).astype(wd_ref.dtype)
-
-    cyc_ref[0] = (dot(wd_ref[0], a0_ref[0]) + dot(wd_ref[1], a1_ref[0])).astype(cyc_ref.dtype)
+                wd[k] = dot(wsel[2 * first + k], pick[...]).astype(wd.dtype)
+                for cut in strips(width, 256):
+                    wdt_ref[k, :, cut] = wd[k, cut, :].T
+
+    cyc_ref[0] = (dot(wd[0], a0_ref[0]) + dot(wd[1], a1_ref[0])).astype(cyc_ref.dtype)
 
 
 def own_cycle(tiles, count, virt, wall, far, side, twin, amp4):
@@ -378,6 +376,7 @@
         ),
         scratch_shapes=[
             pltpu.VMEM((4, width, window), bf16),
+            pltpu.VMEM((2, width, width), bf16),
             pltpu.VMEM((window, width), bf16),
             pltpu.SemaphoreType.DMA((2, slots)),
         ],
@@ -438,8 +437,8 @@
 
 
 def row_kernel(
-    i, count_ref, occ_ref, vcol_ref, vrow_ref, b0_hbm, b1_hbm, xt_hbm, x_hbm, coret_hbm, wt_hbm, wd_hbm,
-    amps_hbm, part_hbm, res_hbm, upd_hbm, xt, coret, wt, right, left, part, amps, proj, total, res, upd, sem, osem,
+    i, count_ref, occ_ref, vcol_ref, vrow_ref, b0_hbm, b1_hbm, xt_hbm, x_hbm, coret_hbm, wt_hbm, wdt_hbm,
+    amps_hbm, part_hbm, res_hbm, upd_hbm, x, coret, wt, right, left, part, amps, proj, total, res, upd, sem, osem,
 ):
     width, points = x_hbm.shape
     early = b0_hbm.shape[1]
@@ -448,24 +447,24 @@
     plan = {
         "b0": (b0_hbm, left.at[:, pl.ds(points, early)]),
         "b1": (b1_hbm, left.at[:, pl.ds(points + early, 2 * width - early)]),
-        "xt": (xt_hbm, xt),
-        "x0": (x_hbm, right.at[0, :, head]),
+        "xt0": (xt_hbm, right.at[0, head, :]),
+        "x": (x_hbm, x),
         "wt": (wt_hbm.at[pl.ds(2 * i, 2)], wt),
         "coret": (coret_hbm, coret),
     }
     for j in range(2):
         for k in range(2):
-            plan["w%d%d" % (j, k)] = (wd_hbm.at[2 * j + k], right.at[j, :, blocks[k]])
+            plan["w%d%d" % (j, k)] = (wdt_hbm.at[2 * j + k], right.at[j, blocks[k], :])
         plan["part%d" % j] = (part_hbm.at[2 * i + j], part.at[j])
         plan["amps%d" % j] = (amps_hbm.at[2 * i + j], amps.at[j])
         if j == 0:
-            plan["x1"] = (x_hbm, right.at[1, :, head])
+            plan["xt1"] = (xt_hbm, right.at[1, head, :])
     mover = Mover(plan, sem, osem)
     for j in range(2):
-        mover.need("b0", "b1", "xt")
-        proj[...] = dot(xt[...], left[:, blocks[j]]).astype(proj.dtype)
-        mover.need("x0", "coret", "wt")
-        inner = dot(proj[...], right[0, :, head])
+        mover.need("b0", "b1", "xt0")
+        proj[...] = dot(right[0, head, :], left[:, blocks[j]]).astype(proj.dtype)
+        mover.need("x", "coret", "wt")
+        inner = dot(proj[...], x[...])
         total[j] = (
             wt[j].astype(jnp.float32) + coret[...].astype(jnp.float32) * inner
         ).astype(total.dtype)
@@ -475,9 +474,9 @@
 
                 def product(j=j, at=at, rows=rows):
                     if at == 0:
-                        left[:, head] = dot(right[0, :, head], total[j]).astype(left.dtype)
-                        mover.need("x%d" % j, "w%d0" % j, "w%d1" % j, "part%d" % j, "amps%d" % j)
-                    return dot_nt(left[rows, :], right[j])
+                        left[:, head] = dot(x[...], total[j]).astype(left.dtype)
+                        mover.need("xt%d" % j, "w%d0" % j, "w%d1" % j, "part%d" % j, "amps%d" % j)
+                    return dot(left[rows, :], right[j])
 
                 yield j, rows, product
 
@@ -491,7 +490,7 @@
     mover.drain()
 
 
-def row(i, count, occ, vcol, vrow, b0, b1, xt, x, coret, wt, wd, amp4, part):
+def row(i, count, occ, vcol, vrow, b0, b1, xt, x, coret, wt, wdt, amp4, part):
     width, points = x.shape
     vmem = pl.BlockSpec(memory_space=pltpu.VMEM)
     smem = pl.BlockSpec(memory_space=pltpu.SMEM)
@@ -507,7 +506,7 @@
             pltpu.VMEM((points, width), bf16),
             pltpu.VMEM((points, points), bf16),
             pltpu.VMEM((2, points, points), bf16),
-            pltpu.VMEM((2, width, depth), bf16),
+            pltpu.VMEM((2, depth, width), bf16),
             pltpu.VMEM((width, depth), bf16),
             pltpu.VMEM((2, width, width), bf16),
             pltpu.VMEM((2, width, width), bf16),
@@ -520,29 +519,29 @@
         ],
         compiler_params=pltpu.CompilerParams(vmem_limit_bytes=VMEM_LIMIT),
         name="row_%d" % i,
-    )(count, occ, vcol, vrow, b0, b1, xt, x, coret, wt, wd, amp4, part)
+    )(count, occ, vcol, vrow, b0, b1, xt, x, coret, wt, wdt, amp4, part)
 
 
 def piece_kernel(i, k, low, high, end, count_ref, occ_ref, vcol_ref, vrow_ref, *refs):
     last = k == 1 and end
     scratch = 13
-    refs, (xt, coret, before, right, left, part, amps, proj, total, res, upd, sem, osem) = (
+    refs, (x, coret, before, right, left, part, amps, proj, total, res, upd, sem, osem) = (
         refs[:-scratch], refs[-scratch:]
     )
-    (b_hbm, xt_hbm, x_hbm, coret_hbm, before_hbm, wd_hbm, amps_hbm, part_hbm) = refs[:8]
+    (b_hbm, xt_hbm, x_hbm, coret_hbm, before_hbm, wdt_hbm, amps_hbm, part_hbm) = refs[:8]
     outs = refs[8:]
     width, points = x_hbm.shape
     head, rest = pl.ds(0, points), pl.ds(points, high - low)
     cut = pl.ds(low, high - low)
     plan = {
         "b": (b_hbm, left.at[:, rest]),
-        "xt": (xt_hbm, xt),
-        "x": (x_hbm, right.at[k, :, head]) if end else (x_hbm.at[cut], right.at[k, cut, head]),
+        "xt": (xt_hbm, right.at[k, head, :]),
+        "x": (x_hbm, x) if end else (x_hbm.at[cut], x.at[cut]),
         "coret": (coret_hbm, coret),
         "before": (before_hbm if low > 0 else before_hbm.at[2 * i + k], before),
     }
     for j in (1 - k, k):
-        plan["w%d" % j] = (wd_hbm.at[2 * j + k, :, cut], right.at[j, :, rest])
+        plan["w%d" % j] = (wdt_hbm.at[2 * j + k, cut, :], right.at[j, rest, :])
         plan["part%d" % j] = (part_hbm.at[2 * i + j], part.at[j])
         if last:
             plan["amps%d" % j] = (amps_hbm.at[2 * i + j], amps.at[j])
@@ -554,7 +553,7 @@
 
                 def product(j=j, columns=columns, rows=rows):
                     mover.need("w%d" % j, "part%d" % j, "amps%d" % j)
-                    return dot_nt(left[rows, columns], right[j, :, columns])
+                    return dot(left[rows, columns], right[j, columns, :])
 
                 yield j, rows, product
 
@@ -569,15 +568,15 @@
             mover.put(part.at[j, rows, :], outs[0].at[2 * i + j, rows, :])
 
     mover.need("b", "xt")
-    proj[...] = dot(xt[...], left[:, rest]).astype(proj.dtype)
+    proj[...] = dot(right[k, head, :], left[:, rest]).astype(proj.dtype)
     mover.need("x")
-    inner = dot(proj[...], right[k, cut, head])
+    inner = dot(proj[...], x[cut, :])
     mover.need("coret", "before")
     total[...] = (
         before[...].astype(jnp.float32) + coret[...].astype(jnp.float32) * inner
     ).astype(total.dtype)
     if end:
-        left[:, head] = dot(right[k, :, head], total[...]).astype(left.dtype)
+        left[:, head] = dot(x[...], total[...]).astype(left.dtype)
         emit_behind(products([(1 - k, rest), (k, pl.ds(0, points + high - low))]), emit_one)
     else:
         mover.put(total, outs[1])
@@ -585,7 +584,7 @@
     mover.drain()
 
 
-def piece(i, k, low, high, count, occ, vcol, vrow, b, xt, x, coret, before, wd, amp4, part, residual, updated):
+def piece(i, k, low, high, count, occ, vcol, vrow, b, xt, x, coret, before, wdt, amp4, part, residual, updated):
     width, points = x.shape
     end = high == width
     last = k == 1 and end
@@ -593,7 +592,7 @@
     smem = pl.BlockSpec(memory_space=pltpu.SMEM)
     hbm = pl.BlockSpec(memory_space=pl.ANY)
     f32, bf16 = jnp.float32, jnp.bfloat16
-    operands = [count, occ, vcol, vrow, b, xt, x, coret, before, wd, amp4, part]
+    operands = [count, occ, vcol, vrow, b, xt, x, coret, before, wdt, amp4, part]
     if last:
         out_shape = [jax.ShapeDtypeStruct(part.shape, f32), jax.ShapeDtypeStruct(part.shape, bf16)]
         alias = {len(operands): 0, len(operands) + 1: 1}
@@ -612,7 +611,7 @@
             pltpu.VMEM((points, width), bf16),
             pltpu.VMEM((points, points), bf16),
             pltpu.VMEM((points, points), bf16),
-            pltpu.VMEM((2, width, points + high - low), bf16),
+            pltpu.VMEM((2, points + high - low, width), bf16),
             pltpu.VMEM((width, points + high - low), bf16),
             pltpu.VMEM((2, width, width), bf16),
             pltpu.VMEM((2, width, width), bf16),
@@ -653,14 +652,14 @@
     side, tail, wt = lax.optimization_barrier((side, turned[3], wt))
     fifth = lax.ppermute(tail, "col", mirror)
     twin = lax.ppermute(side, "col", [(i, i ^ 1) for i in range(cols)])
-    wd, part, vcol, vrow = own_cycle(tiles, count, virt_energy[None, :], wall, far, side, twin, amp4)
+    wdt, part, vcol, vrow = own_cycle(tiles, count, virt_energy[None, :], wall, far, side, twin, amp4)
     energies = (count, occ_energy[0, 0], vcol, vrow)
-    residual, updated = row(0, *energies, first, second, xt, x, coret, wt, wd, amp4, part)
+    residual, updated = row(0, *energies, first, second, xt, x, coret, wt, wdt, amp4, part)
     fixed = (xt, x, coret)
-    part, = piece(1, 0, 0, width, *energies, third, *fixed, wt, wd, amp4, part, None, None)
-    part, total = piece(1, 1, 0, split, *energies, fourth, *fixed, wt, wd, amp4, part, None, None)
+    part, = piece(1, 0, 0, width, *energies, third, *fixed, wt, wdt, amp4, part, None, None)
+    part, total = piece(1, 1, 0, split, *energies, fourth, *fixed, wt, wdt, amp4, part, None, None)
     residual, updated = piece(
-        1, 1, split, width, *energies, fifth, *fixed, total, wd, amp4, part, residual, updated
+        1, 1, split, width, *energies, fifth, *fixed, total, wdt, amp4, part, residual, updated
     )
     return residual.reshape(amps.shape), updated.reshape(amps.shape)
 

time: 146 us -> 146 us (level)
  transfers between devices with their start and end apart: 6 -> 6, of which waited for: 3 -> 4; matrix products, arithmetic and copies ran while one was open for 0% -> 0% of each run, Pallas kernels for 47% -> 48%
where the time goes in v8:
time: 146 us
  Pallas kernels  120 us (82%)
  waiting for transfers between devices  15.3 us (10%)
  starting transfers between devices  8.39 us (6%)
  between operations  1.52 us (1%)
    pallas_call x1, Pallas kernels, gather_parts(): pl.pallas_call(gather_kernel, out_shape=[jax.ShapeDtypeStruct(shape, bf16...  41 us
    pallas_call x3, Pallas kernels, piece(): pl.pallas_call(functools.partial(piece_kernel, i, k, low, high, end), out...  28.3 us
    pallas_call x1, Pallas kernels, own_cycle(): pl.pallas_call(own_cycle_kernel, out_shape=(jax.ShapeDtypeStruct((4, widt...  19.3 us
    pallas_call x1, Pallas kernels, row(): pl.pallas_call(functools.partial(row_kernel, i), out_shape=[jax.ShapeDtyp...  18.6 us
    pallas_call x1, Pallas kernels, own_ladder(): pl.pallas_call(own_ladder_kernel, out_shape=(jax.ShapeDtypeStruct((width,...  13.1 us
    ppermute x3, waiting for transfers between devices, per_device(): lax.ppermute(part, 'col', mirror)  8.07 us
    ppermute x1, waiting for transfers between devices, per_device(): side = lax.ppermute(far, 'col', [(i, i ^ 2) for i in range(cols)])  7.18 us
    ppermute x3, starting transfers between devices, per_device(): lax.ppermute(part, 'col', mirror)  3.53 us
  transfers between devices with their start and end apart: 6, of which 4 were waited for; matrix products, arithmetic and copies ran while one was open for 0% of the time, Pallas kernels for 48%

profile of v8, /device:TPU:6, one launch (start us, length us, event | category | flops | bytes accessed | tf_op | source)
XLA Modules:
  0.0 145.5 jit_solution(14553835765554914055)
XLA Ops:
  0.6 41.0 %gather_parts.1 = (bf16[8,2,64,768]{3,2,1,0:T(8,128)(2,1)}, bf16[16,4,64,1024]{3,2,1,0:T(8,128)(2,1)}, bf16[2,4,64,1024]{3,2,1,0:T(8,128)(2,1)}, bf16[768,384]{1...) custom-call(bf16[2,64,768]{2,1,0:T(8,128)(2,1)} %x_ref.1, ...), custom_call_target="tpu_custom_call" | custom-call | tf_op jit(solution)/shard_map/gather_parts/pallas_call | solution.py:189
  41.6 1.3 collective-permute-start
  42.9 0.0 collective-permute-start.5
  42.9 3.5 %collective-permute-start.4 = (bf16[768,768]{1,0:T(8,128)(2,1)}, bf16[768,768]{1,0:T(8,128)(2,1)}, u32[]{:S(2)}, u32[]{:S(2)}) collective-permute-start(bf16[768,768]{1,0:T(8,128)(2,1)} %get-tuple-element.42), channel_id=1, source_target_pairs={{0,8},{1,9},{2,10},{3,11},{4,12},{5,13},{6,14},{7,15},{8,0},{9,1},... | collective-permute-start | bytes 3538952 | tf_op jit(solution)/shard_map/ppermute | solution.py:648
  47.1 13.1 %own_ladder.1 = (bf16[768,768]{1,0:T(8,128)(2,1)}, bf16[768,768]{1,0:T(8,128)(2,1)}, bf16[4,768,768]{2,1,0:T(8,128)(2,1)}) custom-call(s32[12]{0:T(128)} %bitcast.25, s32[1,1]{1,0:T(1,128)S(6)} %copy.19.count_ref, s32[16]{0:T(128)} %slot_ref.1, bf16[16,64,768]{2,1,0:T(8,128)(2,1)} %bitcast.18, bf16[4,768,768]{2,1,0:T(8,128)(2,1)} %bitcast.9, ...), custom_call_target="tpu_custom_call" | custom-call | tf_op jit(solution)/shard_map/own_ladder/pallas_call | solution.py:248
  60.2 7.2 %collective-permute-done.side_ref = bf16[2,4,64,1024]{3,2,1,0:T(8,128)(2,1)} collective-permute-done((bf16[2,4,64,1024]{3,2,1,0:T(8,128)(2,1)}, bf16[2,4,64,1024]{3,2,1,0:T(8,128)(2,1)}, u32[]{:S(2)}, u32[]{:S(2)}) %collective-permute-start) | collective-permute-done | bytes 1048608 | tf_op jit(solution)/shard_map/ppermute | solution.py:649
  67.4 0.0 collective-permute-start.1
  67.4 0.0 collective-permute-start.3
  67.4 3.5 %collective-permute-start.2 = (bf16[768,256]{1,0:T(8,128)(2,1)}, bf16[768,256]{1,0:T(8,128)(2,1)}, u32[]{:S(2)}, u32[]{:S(2)}) collective-permute-start(bf16[768,256]{1,0:T(8,128)(2,1)} %get-tuple-element.35), channel_id=1, source_target_pairs={{0,8},{1,9},{2,10},{3,11},{4,12},{5,13},{6,14},{7,15},{8,0},{9,1},... | collective-permute-start | bytes 1179656 | tf_op jit(solution)/shard_map/ppermute | solution.py:653
  70.9 0.0 collective-permute-done.1.twin_ref
  70.9 19.3 %own_cycle.1 = (bf16[4,768,768]{2,1,0:T(8,128)(2,1)}, bf16[4,768,768]{2,1,0:T(8,128)(2,1)}, f32[768,1]{1,0:T(8,128)}, f32[1,768]{1,0:T(1,128)}) custom-call(s32[12]{0:T(128)} %bitcast.26, s32[1,1]{1,0:T(1,128)S(6)} %copy.19.count_ref, f32[1,1024]{1,0:T(1,128)} %bitcast.24, bf16[16,4,64,1024]{3,2,1,0:T(8,128)(2,1)} %get-tuple-element.27.wall_ref, ...), custom_call_target="tpu_custom_call" | custom-call | tf_op jit(solution)/shard_map/own_cycle/pallas_call | solution.py:351
  90.2 0.0 collective-permute-done.5.b1_hbm
  90.2 18.6 %row_0.1 = (f32[4,768,768]{2,1,0:T(8,128)}, bf16[4,768,768]{2,1,0:T(8,128)(2,1)}) custom-call(s32[1,1]{1,0:T(1,128)S(6)} %copy.19.count_ref, f32[2,2]{1,0:T(2,128)} %bitcast.20, f32[768,1]{1,0:T(8,128)} %get-tuple-element.33.vcol_ref, f32[1,768]{1,0:T(1,128)} %get-tuple-element.34.vrow_ref, bf16[768,384]{1,0:T(8,128)(2,1)} %get-tuple-element.46.b0_hbm, ...), custom_call_target="tpu_custom_call" | custom-call | tf_op jit(solution)/shard_map/row_0/pallas_call | solution.py:500
  108.9 2.6 %collective-permute-done.4.refs_0_ = bf16[768,768]{1,0:T(8,128)(2,1)} collective-permute-done((bf16[768,768]{1,0:T(8,128)(2,1)}, bf16[768,768]{1,0:T(8,128)(2,1)}, u32[]{:S(2)}, u32[]{:S(2)}) %collective-permute-start.4) | collective-permute-done | bytes 1179680 | tf_op jit(solution)/shard_map/ppermute | solution.py:648
  111.5 11.4 %piece_10_0.1.refs_7_ = bf16[4,768,768]{2,1,0:T(8,128)(2,1)} custom-call(s32[1,1]{1,0:T(1,128)S(6)} %copy.19.count_ref, f32[2,2]{1,0:T(2,128)} %bitcast.21, f32[768,1]{1,0:T(8,128)} %get-tuple-element.33.vcol_ref, f32[1,768]{1,0:T(1,128)} %get-tuple-element.34.vrow_ref, ...), custom_call_target="tpu_custom_call", output_to_operand_aliasing={{}: (11, {})} | custom-call | tf_op jit(solution)/shard_map/piece_10_0/pallas_call | solution.py:605
  122.9 5.5 %collective-permute-done.3.refs_0_ = bf16[768,512]{1,0:T(8,128)(2,1)} collective-permute-done((bf16[768,512]{1,0:T(8,128)(2,1)}, bf16[768,512]{1,0:T(8,128)(2,1)}, u32[]{:S(2)}, u32[]{:S(2)}) %collective-permute-start.3) | collective-permute-done | bytes 786464 | tf_op jit(solution)/shard_map/ppermute | solution.py:648
  128.4 7.4 %piece_11_0.1 = (bf16[4,768,768]{2,1,0:T(8,128)(2,1)}, bf16[768,768]{1,0:T(8,128)(2,1)}) custom-call(s32[1,1]{1,0:T(1,128)S(6)} %copy.19.count_ref, f32[2,2]{1,0:T(2,128)} %bitcast.22, f32[768,1]{1,0:T(8,128)} %get-tuple-element.33.vcol_ref, f32[1,768]{1,0:T(1,128)} %get-tuple-element.34.vrow_ref, ...), custom_call_target="tpu_custom_call", output_to_operand_aliasing={{0}: (11, {})} | custom-call | tf_op jit(solution)/shard_map/piece_11_0/pallas_call | solution.py:605
  135.8 0.1 collective-permute-done.2.refs_0_
  135.9 9.5 %piece_11_512.1 = (f32[4,768,768]{2,1,0:T(8,128)}, bf16[4,768,768]{2,1,0:T(8,128)(2,1)}) custom-call(s32[1,1]{1,0:T(1,128)S(6)} %copy.19.count_ref, f32[2,2]{1,0:T(2,128)} %bitcast.23, f32[768,1]{1,0:T(8,128)} %get-tuple-element.33.vcol_ref, f32[1,768]{1,0:T(1,128)} %get-tuple-element.34.vrow_ref, ...), custom_call_target="tpu_custom_call", output_to_operand_aliasing={{0}: (12, {}), {1}: (13, {})} | custom-call | tf_op jit(solution)/shard_map/piece_11_512/pallas_call | solution.py:605
Async XLA Ops:
  41.6 25.8 %collective-permute-start = (bf16[2,4,64,1024]{3,2,1,0:T(8,128)(2,1)}, bf16[2,4,64,1024]{3,2,1,0:T(8,128)(2,1)}, u32[]{:S(2)}, u32[]{:S(2)}) collective-permute-start(bf16[2,4,64,1024]{3,2,1,0:T(8,128)(2,1)} %get-tuple-element.28.far_ref), channel_id=1, source_target_pairs={{0,2},{1,3},{2,0},{3,1},{4,6},{5,7},{6,4},{7,5},{8,10},{9,11},{10,... | collective-permute-start | bytes 3145736 | tf_op jit(solution)/shard_map/ppermute | solution.py:649
  42.9 47.3 %collective-permute-start.5 = (bf16[768,1152]{1,0:T(8,128)(2,1)}, bf16[768,1152]{1,0:T(8,128)(2,1)}, u32[]{:S(2)}, u32[]{:S(2)}) collective-permute-start(bf16[768,1152]{1,0:T(8,128)(2,1)} %get-tuple-element.47), channel_id=1, source_target_pairs={{0,8},{1,9},{2,10},{3,11},{4,12},{5,13},{6,14},{7,15},{8,0},{9,1},... | collective-permute-start | bytes 5308424 | tf_op jit(solution)/shard_map/ppermute | solution.py:648
  42.9 68.6 %collective-permute-start.4 = (bf16[768,768]{1,0:T(8,128)(2,1)}, bf16[768,768]{1,0:T(8,128)(2,1)}, u32[]{:S(2)}, u32[]{:S(2)}) collective-permute-start(bf16[768,768]{1,0:T(8,128)(2,1)} %get-tuple-element.42), channel_id=1, source_target_pairs={{0,8},{1,9},{2,10},{3,11},{4,12},{5,13},{6,14},{7,15},{8,0},{9,1},... | collective-permute-start | bytes 3538952 | tf_op jit(solution)/shard_map/ppermute | solution.py:648
  67.4 3.5 %collective-permute-start.1 = (bf16[2,4,64,1024]{3,2,1,0:T(8,128)(2,1)}, bf16[2,4,64,1024]{3,2,1,0:T(8,128)(2,1)}, u32[]{:S(2)}, u32[]{:S(2)}) collective-permute-start(bf16[2,4,64,1024]{3,2,1,0:T(8,128)(2,1)} %collective-permute-done.side_ref), channel_id=1, source_target_pairs={{0,1},{1,0},{2,3},{3,2},{4,5},{5,4},{6,7},{7,6},{8,9},{9,8},{10,11... | collective-permute-start | bytes 3145736 | tf_op jit(solution)/shard_map/ppermute | solution.py:654
  67.4 61.0 %collective-permute-start.3 = (bf16[768,512]{1,0:T(8,128)(2,1)}, bf16[768,512]{1,0:T(8,128)(2,1)}, u32[]{:S(2)}, u32[]{:S(2)}) collective-permute-start(bf16[768,512]{1,0:T(8,128)(2,1)} %get-tuple-element.39), channel_id=1, source_target_pairs={{0,8},{1,9},{2,10},{3,11},{4,12},{5,13},{6,14},{7,15},{8,0},{9,1},... | collective-permute-start | bytes 2359304 | tf_op jit(solution)/shard_map/ppermute | solution.py:648
  67.4 68.5 %collective-permute-start.2 = (bf16[768,256]{1,0:T(8,128)(2,1)}, bf16[768,256]{1,0:T(8,128)(2,1)}, u32[]{:S(2)}, u32[]{:S(2)}) collective-permute-start(bf16[768,256]{1,0:T(8,128)(2,1)} %get-tuple-element.35), channel_id=1, source_target_pairs={{0,8},{1,9},{2,10},{3,11},{4,12},{5,13},{6,14},{7,15},{8,0},{9,1},... | collective-permute-start | bytes 1179656 | tf_op jit(solution)/shard_map/ppermute | solution.py:653

commit v9 on v8

--- a/solution.py
+++ b/solution.py
@@ -14,6 +14,10 @@
 
 def dot(a, b):
     return jnp.dot(a, b, preferred_element_type=jnp.float32)
+
+
+def tapered(width):
+    return [pl.ds(0, width // 2), pl.ds(width // 2, width // 3), pl.ds(width // 2 + width // 3, width // 6)]
 
 
 def strips(width, step):
@@ -281,8 +285,8 @@
 
 
 def own_cycle_kernel(
-    tiles_ref, count_ref, virt_ref, wall_ref, far_ref, side_ref, twin_ref, a0_ref, a1_ref,
-    wdt_ref, cyc_ref, vcol_ref, vrow_ref, wsel, wd, pick, sem,
+    tiles_ref, count_ref, occ_ref, virt_ref, wall_ref, far_ref, side_ref, twin_ref, a0_ref, a1_ref,
+    wdt_ref, cyc_ref, down_ref, along_ref, wsel, wd, pick, sem,
 ):
     p = pl.program_id(0)
     tile = wall_ref.shape[2]
@@ -321,8 +325,17 @@
         picked = window_index(tiles_ref, count_ref, tile, (width, 1), 0)
         along = lax.broadcasted_iota(jnp.int32, (width, window), 1)
         levels = jnp.sum(jnp.where(along == picked, virt_ref[...], 0.0), axis=1, keepdims=True)
-        vcol_ref[...] = levels
-        vrow_ref[...] = jnp.broadcast_to(levels, (width, 128)).T[:1, :]
+        lane = lax.broadcasted_iota(jnp.int32, (1, 128), 1)
+        sums = jnp.zeros((1, 128), jnp.float32)
+        for i in range(2):
+            for j in range(2):
+                sums = jnp.where(lane == 2 * i + j, occ_ref[0, i] + occ_ref[1, j], sums)
+        live = jnp.where(picked >= 0, 1.0, 0.0)
+        down_ref[...] = jnp.where(lane < 4, sums - levels, live)
+        line = lax.broadcasted_iota(jnp.int32, (8, 1), 0)
+        wide_levels = jnp.broadcast_to(levels, (width, 128)).T[:8, :]
+        wide_live = jnp.broadcast_to(live, (width, 128)).T[:8, :]
+        along_ref[...] = jnp.where(line == 0, wide_levels, wide_live)
 
     for first in range(2):
 
@@ -342,7 +355,7 @@
     cyc_ref[0] = (dot(wd[0], a0_ref[0]) + dot(wd[1], a1_ref[0])).astype(cyc_ref.dtype)
 
 
-def own_cycle(tiles, count, virt, wall, far, side, twin, amp4):
+def own_cycle(tiles, count, occ, virt, wall, far, side, twin, amp4):
     width = amp4.shape[1]
     slots, window = tiles.shape[0], wall.shape[3]
     smem = pl.BlockSpec(memory_space=pltpu.SMEM)
@@ -353,11 +366,12 @@
         out_shape=(
             jax.ShapeDtypeStruct((4, width, width), bf16),
             jax.ShapeDtypeStruct((4, width, width), bf16),
-            jax.ShapeDtypeStruct((width, 1), f32),
-            jax.ShapeDtypeStruct((1, width), f32),
+            jax.ShapeDtypeStruct((width, 128), f32),
+            jax.ShapeDtypeStruct((8, width), f32),
         ),
         grid=(4,),
         in_specs=[
+            smem,
             smem,
             smem,
             pl.BlockSpec((1, window), lambda p: (0, 0)),
@@ -371,8 +385,8 @@
         out_specs=(
             pl.BlockSpec((2, width, width), lambda p: (p // 2, 0, 0)),
             pl.BlockSpec((1, width, width), lambda p: (p, 0, 0)),
-            pl.BlockSpec((width, 1), lambda p: (0, 0)),
-            pl.BlockSpec((1, width), lambda p: (0, 0)),
+            pl.BlockSpec((width, 128), lambda p: (0, 0)),
+            pl.BlockSpec((8, width), lambda p: (0, 0)),
         ),
         scratch_shapes=[
             pltpu.VMEM((4, width, window), bf16),
@@ -382,7 +396,7 @@
         ],
         compiler_params=pltpu.CompilerParams(vmem_limit_bytes=VMEM_LIMIT),
         name="own_cycle",
-    )(tiles, count, virt, wall, far, side, twin, amp4, amp4)
+    )(tiles, count, occ, virt, wall, far, side, twin, amp4, amp4)
 
 
 class Mover:
@@ -409,15 +423,11 @@
             copy.wait()
 
 
-def emit(mover, pair, j, rows, raw, count_ref, occ_ref, vcol_ref, vrow_ref, part, amps, res, upd, res_hbm, upd_hbm):
-    height, width = raw.shape
-    count = count_ref[0, 0] * 64
-    live = (lax.broadcasted_iota(jnp.int32, (height, 1), 0) + rows.start < count) & (
-        lax.broadcasted_iota(jnp.int32, (1, width), 1) < count
-    )
-    raw = jnp.where(live, raw + part[j, rows, :].astype(jnp.float32), 0.0)
-    own = jnp.where(live, amps[j, rows, :].astype(jnp.float32), 0.0)
-    gap = (occ_ref[0, pair // 2] + occ_ref[1, pair % 2]) - vcol_ref[rows, :] - vrow_ref[...]
+def emit(mover, pair, j, rows, raw, down, along, part, amps, res, upd, res_hbm, upd_hbm):
+    mask = down[rows, 4:5] * along[1:2, :]
+    raw = (raw + part[j, rows, :].astype(jnp.float32)) * mask
+    own = amps[j, rows, :].astype(jnp.float32) * mask
+    gap = down[rows, pair:pair + 1] - along[0:1, :]
     inverse = pl.reciprocal(gap, approx=True)
     inverse = inverse * (2.0 - gap * inverse)
     res[j, rows, :] = raw
@@ -437,8 +447,9 @@
 
 
 def row_kernel(
-    i, count_ref, occ_ref, vcol_ref, vrow_ref, b0_hbm, b1_hbm, xt_hbm, x_hbm, coret_hbm, wt_hbm, wdt_hbm,
-    amps_hbm, part_hbm, res_hbm, upd_hbm, x, coret, wt, right, left, part, amps, proj, total, res, upd, sem, osem,
+    i, down_hbm, along_hbm, b0_hbm, b1_hbm, xt_hbm, x_hbm, coret_hbm, wt_hbm, wdt_hbm,
+    amps_hbm, part_hbm, res_hbm, upd_hbm, x, coret, wt, right, left, part, amps, proj, total, res, upd, down, along,
+    sem, osem,
 ):
     width, points = x_hbm.shape
     early = b0_hbm.shape[1]
@@ -451,6 +462,8 @@
         "x": (x_hbm, x),
         "wt": (wt_hbm.at[pl.ds(2 * i, 2)], wt),
         "coret": (coret_hbm, coret),
+        "down": (down_hbm, down),
+        "along": (along_hbm, along),
     }
     for j in range(2):
         for k in range(2):
@@ -475,32 +488,29 @@
                 def product(j=j, at=at, rows=rows):
                     if at == 0:
                         left[:, head] = dot(x[...], total[j]).astype(left.dtype)
-                        mover.need("xt%d" % j, "w%d0" % j, "w%d1" % j, "part%d" % j, "amps%d" % j)
+                        mover.need("down", "along", "xt%d" % j, "w%d0" % j, "w%d1" % j, "part%d" % j, "amps%d" % j)
                     return dot(left[rows, :], right[j])
 
                 yield j, rows, product
 
     def emit_one(j, rows, raw):
         emit(
-            mover, 2 * i + j, j, rows, raw, count_ref, occ_ref, vcol_ref, vrow_ref,
-            part, amps, res, upd, res_hbm, upd_hbm,
+            mover, 2 * i + j, j, rows, raw, down, along, part, amps, res, upd, res_hbm, upd_hbm,
         )
 
     emit_behind(products(), emit_one)
     mover.drain()
 
 
-def row(i, count, occ, vcol, vrow, b0, b1, xt, x, coret, wt, wdt, amp4, part):
+def row(i, down, along, b0, b1, xt, x, coret, wt, wdt, amp4, part):
     width, points = x.shape
-    vmem = pl.BlockSpec(memory_space=pltpu.VMEM)
-    smem = pl.BlockSpec(memory_space=pltpu.SMEM)
     hbm = pl.BlockSpec(memory_space=pl.ANY)
     f32, bf16 = jnp.float32, jnp.bfloat16
     depth = points + 2 * width
     return pl.pallas_call(
         functools.partial(row_kernel, i),
         out_shape=[jax.ShapeDtypeStruct(part.shape, f32), jax.ShapeDtypeStruct(part.shape, bf16)],
-        in_specs=[smem, smem, vmem, vmem] + [hbm] * 9,
+        in_specs=[hbm] * 11,
         out_specs=[hbm] * 2,
         scratch_shapes=[
             pltpu.VMEM((points, width), bf16),
@@ -514,18 +524,20 @@
             pltpu.VMEM((2, points, points), bf16),
             pltpu.VMEM((2, width, width), f32),
             pltpu.VMEM((2, width, width), bf16),
-            pltpu.SemaphoreType.DMA((15,)),
+            pltpu.VMEM((width, 128), f32),
+            pltpu.VMEM((8, width), f32),
+            pltpu.SemaphoreType.DMA((17,)),
             pltpu.SemaphoreType.DMA((4 * (width // STRIP),)),
         ],
         compiler_params=pltpu.CompilerParams(vmem_limit_bytes=VMEM_LIMIT),
         name="row_%d" % i,
-    )(count, occ, vcol, vrow, b0, b1, xt, x, coret, wt, wdt, amp4, part)
-
-
-def piece_kernel(i, k, low, high, end, count_ref, occ_ref, vcol_ref, vrow_ref, *refs):
+    )(down, along, b0, b1, xt, x, coret, wt, wdt, amp4, part)
+
+
+def piece_kernel(i, k, low, high, end, down_hbm, along_hbm, *refs):
     last = k == 1 and end
-    scratch = 13
-    refs, (x, coret, before, right, left, part, amps, proj, total, res, upd, sem, osem) = (
+    scratch = 15
+    refs, (x, coret, before, right, left, part, amps, proj, total, res, upd, down, along, sem, osem) = (
         refs[:-scratch], refs[-scratch:]
     )
     (b_hbm, xt_hbm, x_hbm, coret_hbm, before_hbm, wdt_hbm, amps_hbm, part_hbm) = refs[:8]
@@ -540,6 +552,9 @@
         "coret": (coret_hbm, coret),
         "before": (before_hbm if low > 0 else before_hbm.at[2 * i + k], before),
     }
+    if last:
+        plan["down"] = (down_hbm, down)
+        plan["along"] = (along_hbm, along)
     for j in (1 - k, k):
         plan["w%d" % j] = (wdt_hbm.at[2 * j + k, cut, :], right.at[j, rest, :])
         plan["part%d" % j] = (part_hbm.at[2 * i + j], part.at[j])
@@ -549,10 +564,10 @@
 
     def products(plan):
         for j, columns in plan:
-            for rows in strips(width, STRIP):
+            for rows in tapered(width) if last and j == k else strips(width, STRIP):
 
                 def product(j=j, columns=columns, rows=rows):
-                    mover.need("w%d" % j, "part%d" % j, "amps%d" % j)
+                    mover.need("down", "along", "w%d" % j, "part%d" % j, "amps%d" % j)
                     return dot(left[rows, columns], right[j, columns, :])
 
                 yield j, rows, product
@@ -560,8 +575,7 @@
     def emit_one(j, rows, raw):
         if last:
             emit(
-                mover, 2 * i + j, j, rows, raw, count_ref, occ_ref, vcol_ref, vrow_ref,
-                part, amps, res, upd, outs[-2], outs[-1],
+                mover, 2 * i + j, j, rows, raw, down, along, part, amps, res, upd, outs[-2], outs[-1],
             )
         else:
             part[j, rows, :] = (raw + part[j, rows, :].astype(jnp.float32)).astype(part.dtype)
@@ -584,15 +598,13 @@
     mover.drain()
 
 
-def piece(i, k, low, high, count, occ, vcol, vrow, b, xt, x, coret, before, wdt, amp4, part, residual, updated):
+def piece(i, k, low, high, down, along, b, xt, x, coret, before, wdt, amp4, part, residual, updated):
     width, points = x.shape
     end = high == width
     last = k == 1 and end
-    vmem = pl.BlockSpec(memory_space=pltpu.VMEM)
-    smem = pl.BlockSpec(memory_space=pltpu.SMEM)
     hbm = pl.BlockSpec(memory_space=pl.ANY)
     f32, bf16 = jnp.float32, jnp.bfloat16
-    operands = [count, occ, vcol, vrow, b, xt, x, coret, before, wdt, amp4, part]
+    operands = [down, along, b, xt, x, coret, before, wdt, amp4, part]
     if last:
         out_shape = [jax.ShapeDtypeStruct(part.shape, f32), jax.ShapeDtypeStruct(part.shape, bf16)]
         alias = {len(operands): 0, len(operands) + 1: 1}
@@ -605,7 +617,7 @@
     return pl.pallas_call(
         functools.partial(piece_kernel, i, k, low, high, end),
         out_shape=out_shape,
-        in_specs=[smem, smem, vmem, vmem] + [hbm] * (len(operands) - 4),
+        in_specs=[hbm] * len(operands),
         out_specs=[hbm] * len(out_shape),
         scratch_shapes=[
             pltpu.VMEM((points, width), bf16),
@@ -619,8 +631,10 @@
             pltpu.VMEM((points, points), bf16),
             pltpu.VMEM((2, width, width), f32),
             pltpu.VMEM((2, width, width), bf16),
-            pltpu.SemaphoreType.DMA((11,)),
-            pltpu.SemaphoreType.DMA((8,)),
+            pltpu.VMEM((width, 128), f32),
+            pltpu.VMEM((8, width), f32),
+            pltpu.SemaphoreType.DMA((13,)),
+            pltpu.SemaphoreType.DMA((10,)),
         ],
         input_output_aliases=alias,
         compiler_params=pltpu.CompilerParams(vmem_limit_bytes=VMEM_LIMIT),
@@ -640,7 +654,7 @@
     amp4 = amps[0, 0].reshape(occ * occ, width, width)
     shard = cycle_w[0].reshape(occ * occ, tile_width, window)
 
-    early, split = width // 2, 512
+    early, split = 256, 512
     tiles, count = domain_tiles[0, 0], domain_count
     xall, wall, far, first, coret, *turned = gather_parts(x_factor, shard, amp4, core, early, split)
     xall = xall.reshape(-1, tile_width, grid_points)
@@ -652,8 +666,8 @@
     side, tail, wt = lax.optimization_barrier((side, turned[3], wt))
     fifth = lax.ppermute(tail, "col", mirror)
     twin = lax.ppermute(side, "col", [(i, i ^ 1) for i in range(cols)])
-    wdt, part, vcol, vrow = own_cycle(tiles, count, virt_energy[None, :], wall, far, side, twin, amp4)
-    energies = (count, occ_energy[0, 0], vcol, vrow)
+    wdt, part, down, along = own_cycle(tiles, count, occ_energy[0, 0], virt_energy[None, :], wall, far, side, twin, amp4)
+    energies = (down, along)
     residual, updated = row(0, *energies, first, second, xt, x, coret, wt, wdt, amp4, part)
     fixed = (xt, x, coret)
     part, = piece(1, 0, 0, width, *energies, third, *fixed, wt, wdt, amp4, part, None, None)

time: 146 us -> 145 us (level)
  Pallas kernels: 120 us -> 112 us
  waiting for transfers between devices: 15.3 us -> 22.1 us
    ppermute x3, waiting for transfers between devices: 8.07 us -> 14.1 us  [per_device(): lax.ppermute(part, 'col', mirror)]
    pallas_call x1, Pallas kernels: 41 us -> 36.8 us  [gather_parts(): pl.pallas_call(gather_kernel, out_shape=[jax.ShapeDtypeStruct(shape, bf16...]
    pallas_call x3, Pallas kernels: 28.3 us -> 25.2 us  [piece(): pl.pallas_call(functools.partial(piece_kernel, i, k, low, high, end), out...]
  transfers between devices with their start and end apart: 6 -> 6, of which waited for: 4 -> 4; matrix products, arithmetic and copies ran while one was open for 0% -> 0% of each run, Pallas kernels for 48% -> 47%
where the time goes in v9:
time: 145 us; the launch traced here: 144 us
  Pallas kernels  112 us (77%)
  waiting for transfers between devices  22.1 us (15%)
  starting transfers between devices  8.39 us (6%)
  between operations  1.54 us (1%)
    pallas_call x1, Pallas kernels, gather_parts(): pl.pallas_call(gather_kernel, out_shape=[jax.ShapeDtypeStruct(shape, bf16...  36.8 us
    pallas_call x3, Pallas kernels, piece(): pl.pallas_call(functools.partial(piece_kernel, i, k, low, high, end), out...  25.2 us
    pallas_call x1, Pallas kernels, own_cycle(): pl.pallas_call(own_cycle_kernel, out_shape=(jax.ShapeDtypeStruct((4, widt...  19.8 us
    pallas_call x1, Pallas kernels, row(): pl.pallas_call(functools.partial(row_kernel, i), out_shape=[jax.ShapeDtyp...  17.4 us
    ppermute x3, waiting for transfers between devices, per_device(): lax.ppermute(part, 'col', mirror)  14.1 us
    pallas_call x1, Pallas kernels, own_ladder(): pl.pallas_call(own_ladder_kernel, out_shape=(jax.ShapeDtypeStruct((width,...  13.1 us
    ppermute x1, waiting for transfers between devices, per_device(): side = lax.ppermute(far, 'col', [(i, i ^ 2) for i in range(cols)])  7.11 us
    ppermute x3, starting transfers between devices, per_device(): lax.ppermute(part, 'col', mirror)  3.53 us
  transfers between devices with their start and end apart: 6, of which 4 were waited for; matrix products, arithmetic and copies ran while one was open for 0% of the time, Pallas kernels for 47%

profile of v9, /device:TPU:6, one launch (start us, length us, event | category | flops | bytes accessed | tf_op | source)
XLA Modules:
  0.0 144.4 jit_solution(2366290959182524603)
XLA Ops:
  0.6 36.8 %gather_parts.1 = (bf16[8,2,64,768]{3,2,1,0:T(8,128)(2,1)}, bf16[16,4,64,1024]{3,2,1,0:T(8,128)(2,1)}, bf16[2,4,64,1024]{3,2,1,0:T(8,128)(2,1)}, bf16[768,256]{1...) custom-call(bf16[2,64,768]{2,1,0:T(8,128)(2,1)} %x_ref.1, ...), custom_call_target="tpu_custom_call" | custom-call | tf_op jit(solution)/shard_map/gather_parts/pallas_call | solution.py:193
  37.5 1.3 collective-permute-start
  38.8 0.0 collective-permute-start.5
  38.8 3.5 %collective-permute-start.4 = (bf16[768,768]{1,0:T(8,128)(2,1)}, bf16[768,768]{1,0:T(8,128)(2,1)}, u32[]{:S(2)}, u32[]{:S(2)}) collective-permute-start(bf16[768,768]{1,0:T(8,128)(2,1)} %get-tuple-element.42), channel_id=1, source_target_pairs={{0,8},{1,9},{2,10},{3,11},{4,12},{5,13},{6,14},{7,15},{8,0},{9,1},... | collective-permute-start | bytes 3538952 | tf_op jit(solution)/shard_map/ppermute | solution.py:662
  43.0 13.1 %own_ladder.1 = (bf16[768,768]{1,0:T(8,128)(2,1)}, bf16[768,768]{1,0:T(8,128)(2,1)}, bf16[4,768,768]{2,1,0:T(8,128)(2,1)}) custom-call(s32[12]{0:T(128)} %bitcast.21, s32[1,1]{1,0:T(1,128)S(6)} %copy.19.count_ref, s32[16]{0:T(128)} %slot_ref.1, bf16[16,64,768]{2,1,0:T(8,128)(2,1)} %bitcast.18, bf16[4,768,768]{2,1,0:T(8,128)(2,1)} %bitcast.9, ...), custom_call_target="tpu_custom_call" | custom-call | tf_op jit(solution)/shard_map/own_ladder/pallas_call | solution.py:252
  56.1 7.1 %collective-permute-done.side_ref = bf16[2,4,64,1024]{3,2,1,0:T(8,128)(2,1)} collective-permute-done((bf16[2,4,64,1024]{3,2,1,0:T(8,128)(2,1)}, bf16[2,4,64,1024]{3,2,1,0:T(8,128)(2,1)}, u32[]{:S(2)}, u32[]{:S(2)}) %collective-permute-start) | collective-permute-done | bytes 1048608 | tf_op jit(solution)/shard_map/ppermute | solution.py:663
  63.2 0.0 collective-permute-start.1
  63.2 0.0 collective-permute-start.3
  63.2 3.5 %collective-permute-start.2 = (bf16[768,256]{1,0:T(8,128)(2,1)}, bf16[768,256]{1,0:T(8,128)(2,1)}, u32[]{:S(2)}, u32[]{:S(2)}) collective-permute-start(bf16[768,256]{1,0:T(8,128)(2,1)} %get-tuple-element.35), channel_id=1, source_target_pairs={{0,8},{1,9},{2,10},{3,11},{4,12},{5,13},{6,14},{7,15},{8,0},{9,1},... | collective-permute-start | bytes 1179656 | tf_op jit(solution)/shard_map/ppermute | solution.py:667
  66.7 0.0 collective-permute-done.1.twin_ref
  66.7 19.8 %own_cycle.1 = (bf16[4,768,768]{2,1,0:T(8,128)(2,1)}, bf16[4,768,768]{2,1,0:T(8,128)(2,1)}, f32[768,128]{1,0:T(8,128)}, f32[8,768]{1,0:T(8,128)}) custom-call(s32[12]{0:T(128)} %bitcast.22, s32[1,1]{1,0:T(1,128)S(6)} %copy.19.count_ref, f32[2,2]{1,0:T(2,128)} %bitcast.23, f32[1,1024]{1,0:T(1,128)} %bitcast.20, ...), custom_call_target="tpu_custom_call" | custom-call | tf_op jit(solution)/shard_map/own_cycle/pallas_call | solution.py:364
  86.5 0.0 collective-permute-done.5.b1_hbm
  86.5 17.4 %row_0.1 = (f32[4,768,768]{2,1,0:T(8,128)}, bf16[4,768,768]{2,1,0:T(8,128)(2,1)}) custom-call(f32[768,128]{1,0:T(8,128)} %get-tuple-element.33.down_hbm, f32[8,768]{1,0:T(8,128)} %get-tuple-element.34.along_hbm, bf16[768,256]{1,0:T(8,128)(2,1)} %get-tuple-element.46.b0_hbm, bf16[768,1280]{1,0:T(8,128)(2,1)} %collective-permute-done.5.b1_hbm, ...), custom_call_target="tpu_custom_call" | custom-call | tf_op jit(solution)/shard_map/row_0/pallas_call | solution.py:510
  103.9 7.7 %collective-permute-done.4.refs_0_ = bf16[768,768]{1,0:T(8,128)(2,1)} collective-permute-done((bf16[768,768]{1,0:T(8,128)(2,1)}, bf16[768,768]{1,0:T(8,128)(2,1)}, u32[]{:S(2)}, u32[]{:S(2)}) %collective-permute-start.4) | collective-permute-done | bytes 1179680 | tf_op jit(solution)/shard_map/ppermute | solution.py:662
  111.6 10.4 %piece_10_0.1.refs_7_ = bf16[4,768,768]{2,1,0:T(8,128)(2,1)} custom-call(f32[768,128]{1,0:T(8,128)} %get-tuple-element.33.down_hbm, f32[8,768]{1,0:T(8,128)} %get-tuple-element.34.along_hbm, bf16[768,768]{1,0:T(8,128)(2,1)} %collective-permute-done.4.refs_0_, bf16[768,768]{1,0:T(8,128)(2,1)} %get-tuple-element.36.refs_1_.xt_hbm, ...), custom_call_target="tpu_custom_call", output_to_operand_aliasing={{}: (9, {})} | custom-call | tf_op jit(solution)/shard_map/piece_10_0/pallas_call | solution.py:617
  122.0 6.4 %collective-permute-done.3.refs_0_ = bf16[768,512]{1,0:T(8,128)(2,1)} collective-permute-done((bf16[768,512]{1,0:T(8,128)(2,1)}, bf16[768,512]{1,0:T(8,128)(2,1)}, u32[]{:S(2)}, u32[]{:S(2)}) %collective-permute-start.3) | collective-permute-done | bytes 786464 | tf_op jit(solution)/shard_map/ppermute | solution.py:662
  128.4 6.5 %piece_11_0.1 = (bf16[4,768,768]{2,1,0:T(8,128)(2,1)}, bf16[768,768]{1,0:T(8,128)(2,1)}) custom-call(f32[768,128]{1,0:T(8,128)} %get-tuple-element.33.down_hbm, f32[8,768]{1,0:T(8,128)} %get-tuple-element.34.along_hbm, bf16[768,512]{1,0:T(8,128)(2,1)} %collective-permute-done.3.refs_0_, ...), custom_call_target="tpu_custom_call", output_to_operand_aliasing={{0}: (9, {})} | custom-call | tf_op jit(solution)/shard_map/piece_11_0/pallas_call | solution.py:617
  134.9 1.0 collective-permute-done.2.refs_0_
  135.9 8.3 %piece_11_512.1 = (f32[4,768,768]{2,1,0:T(8,128)}, bf16[4,768,768]{2,1,0:T(8,128)(2,1)}) custom-call(f32[768,128]{1,0:T(8,128)} %get-tuple-element.33.down_hbm, f32[8,768]{1,0:T(8,128)} %get-tuple-element.34.along_hbm, bf16[768,256]{1,0:T(8,128)(2,1)} %collective-permute-done.2.refs_0_, ...), custom_call_target="tpu_custom_call", output_to_operand_aliasing={{0}: (10, {}), {1}: (11, {})} | custom-call | tf_op jit(solution)/shard_map/piece_11_512/pallas_call | solution.py:617
Async XLA Ops:
  37.5 25.7 %collective-permute-start = (bf16[2,4,64,1024]{3,2,1,0:T(8,128)(2,1)}, bf16[2,4,64,1024]{3,2,1,0:T(8,128)(2,1)}, u32[]{:S(2)}, u32[]{:S(2)}) collective-permute-start(bf16[2,4,64,1024]{3,2,1,0:T(8,128)(2,1)} %get-tuple-element.28.far_ref), channel_id=1, source_target_pairs={{0,2},{1,3},{2,0},{3,1},{4,6},{5,7},{6,4},{7,5},{8,10},{9,11},{10,... | collective-permute-start | bytes 3145736 | tf_op jit(solution)/shard_map/ppermute | solution.py:663
  38.8 47.7 %collective-permute-start.5 = (bf16[768,1280]{1,0:T(8,128)(2,1)}, bf16[768,1280]{1,0:T(8,128)(2,1)}, u32[]{:S(2)}, u32[]{:S(2)}) collective-permute-start(bf16[768,1280]{1,0:T(8,128)(2,1)} %get-tuple-element.47), channel_id=1, source_target_pairs={{0,8},{1,9},{2,10},{3,11},{4,12},{5,13},{6,14},{7,15},{8,0},{9,1},... | collective-permute-start | bytes 5898248 | tf_op jit(solution)/shard_map/ppermute | solution.py:662
  38.8 72.8 %collective-permute-start.4 = (bf16[768,768]{1,0:T(8,128)(2,1)}, bf16[768,768]{1,0:T(8,128)(2,1)}, u32[]{:S(2)}, u32[]{:S(2)}) collective-permute-start(bf16[768,768]{1,0:T(8,128)(2,1)} %get-tuple-element.42), channel_id=1, source_target_pairs={{0,8},{1,9},{2,10},{3,11},{4,12},{5,13},{6,14},{7,15},{8,0},{9,1},... | collective-permute-start | bytes 3538952 | tf_op jit(solution)/shard_map/ppermute | solution.py:662
  63.2 3.5 %collective-permute-start.1 = (bf16[2,4,64,1024]{3,2,1,0:T(8,128)(2,1)}, bf16[2,4,64,1024]{3,2,1,0:T(8,128)(2,1)}, u32[]{:S(2)}, u32[]{:S(2)}) collective-permute-start(bf16[2,4,64,1024]{3,2,1,0:T(8,128)(2,1)} %collective-permute-done.side_ref), channel_id=1, source_target_pairs={{0,1},{1,0},{2,3},{3,2},{4,5},{5,4},{6,7},{7,6},{8,9},{9,8},{10,11... | collective-permute-start | bytes 3145736 | tf_op jit(solution)/shard_map/ppermute | solution.py:668
  63.2 65.3 %collective-permute-start.3 = (bf16[768,512]{1,0:T(8,128)(2,1)}, bf16[768,512]{1,0:T(8,128)(2,1)}, u32[]{:S(2)}, u32[]{:S(2)}) collective-permute-start(bf16[768,512]{1,0:T(8,128)(2,1)} %get-tuple-element.39), channel_id=1, source_target_pairs={{0,8},{1,9},{2,10},{3,11},{4,12},{5,13},{6,14},{7,15},{8,0},{9,1},... | collective-permute-start | bytes 2359304 | tf_op jit(solution)/shard_map/ppermute | solution.py:662
  63.2 72.7 %collective-permute-start.2 = (bf16[768,256]{1,0:T(8,128)(2,1)}, bf16[768,256]{1,0:T(8,128)(2,1)}, u32[]{:S(2)}, u32[]{:S(2)}) collective-permute-start(bf16[768,256]{1,0:T(8,128)(2,1)} %get-tuple-element.35), channel_id=1, source_target_pairs={{0,8},{1,9},{2,10},{3,11},{4,12},{5,13},{6,14},{7,15},{8,0},{9,1},... | collective-permute-start | bytes 1179656 | tf_op jit(solution)/shard_map/ppermute | solution.py:667

commit v10 on v9

--- a/solution.py
+++ b/solution.py
@@ -108,6 +108,12 @@
     own_x.start()
     transpose(0, 0)
 
+    def send_first(at):
+        columns = pl.ds(at * (first_ref.shape[1] // 2), first_ref.shape[1] // 2)
+        send(turned.at[0, :, columns], first_ref.at[:, columns], (msend, mrecv), at, mirror)
+
+    send_first(0)
+
     part = xall_ref.at[beside, core]
     arrived(part, xsems, 0)
     for step in y_steps:
@@ -120,7 +126,7 @@
     send(part, part, wsems, 5, zside)
     arrived(far_ref.at[0], wsems, 1)
     send(far_ref.at[0, half:], far_ref.at[1, half:], wsems, 3, back)
-    send(turned.at[0, :, pl.ds(0, first_ref.shape[1])], first_ref, (msend, mrecv), 0, mirror)
+    send_first(1)
     to_twin(3)
     to_twin(1)
     transpose(2, 1)
@@ -173,7 +179,9 @@
         arrived(xall_ref.at[origin, 1 - core], xsems, 7 + step)
         origin = origin + 1 - 2 * (origin % 2)
         arrived(xall_ref.at[origin, 1 - core], xsems, 10 + step)
-    remote(first_ref, first_ref, (msend, mrecv), 0, mirror).wait_recv()
+    for at in range(2):
+        part = first_ref.at[:, pl.ds(at * (first_ref.shape[1] // 2), first_ref.shape[1] // 2)]
+        arrived(part, (msend, mrecv), at)
     for copy in started:
         copy.wait_send()
     for copy in outs + [own_w, own_x]:
@@ -203,8 +211,8 @@
             dma((12,)),
             dma((14,)),
             dma((14,)),
-            dma((1,)),
-            dma((1,)),
+            dma((2,)),
+            dma((2,)),
             dma((8,)),
             dma((5,)),
         ],

time: 145 us -> 141 us (0.972)
  Pallas kernels: 112 us -> 109 us
    pallas_call x1, Pallas kernels: 36.8 us -> 33.1 us  [gather_parts(): pl.pallas_call(gather_kernel, out_shape=[jax.ShapeDtypeStruct(shape, bf16...]
  transfers between devices with their start and end apart: 6 -> 6, of which waited for: 4 -> 4; matrix products, arithmetic and copies ran while one was open for 0% -> 0% of each run, Pallas kernels for 47% -> 48%
where the time goes in v10:
time: 141 us; the launch traced here: 140 us
  Pallas kernels  109 us (77%)
  waiting for transfers between devices  22.3 us (16%)
  starting transfers between devices  7.92 us (6%)
  between operations  1.54 us (1%)
    pallas_call x1, Pallas kernels, gather_parts(): pl.pallas_call(gather_kernel, out_shape=[jax.ShapeDtypeStruct(shape, bf16...  33.1 us
    pallas_call x3, Pallas kernels, piece(): pl.pallas_call(functools.partial(piece_kernel, i, k, low, high, end), out...  25.2 us
    pallas_call x1, Pallas kernels, own_cycle(): pl.pallas_call(own_cycle_kernel, out_shape=(jax.ShapeDtypeStruct((4, widt...  19.8 us
    pallas_call x1, Pallas kernels, row(): pl.pallas_call(functools.partial(row_kernel, i), out_shape=[jax.ShapeDtyp...  17.4 us
    ppermute x3, waiting for transfers between devices, per_device(): lax.ppermute(part, 'col', mirror)  13.4 us
    pallas_call x1, Pallas kernels, own_ladder(): pl.pallas_call(own_ladder_kernel, out_shape=(jax.ShapeDtypeStruct((width,...  13.1 us
    ppermute x1, waiting for transfers between devices, per_device(): side = lax.ppermute(far, 'col', [(i, i ^ 2) for i in range(cols)])  7.78 us
    ppermute x3, starting transfers between devices, per_device(): lax.ppermute(part, 'col', mirror)  4.94 us
  transfers between devices with their start and end apart: 6, of which 4 were waited for; matrix products, arithmetic and copies ran while one was open for 0% of the time, Pallas kernels for 48%

profile of v10, /device:TPU:6, one launch (start us, length us, event | category | flops | bytes accessed | tf_op | source)
XLA Modules:
  0.0 140.4 jit_solution(13459541516842023008)
XLA Ops:
  0.6 33.1 %gather_parts.1 = (bf16[8,2,64,768]{3,2,1,0:T(8,128)(2,1)}, bf16[16,4,64,1024]{3,2,1,0:T(8,128)(2,1)}, bf16[2,4,64,1024]{3,2,1,0:T(8,128)(2,1)}, bf16[768,256]{1...) custom-call(bf16[2,64,768]{2,1,0:T(8,128)(2,1)} %x_ref.1, ...), custom_call_target="tpu_custom_call" | custom-call | tf_op jit(solution)/shard_map/gather_parts/pallas_call | solution.py:201
  33.7 0.9 collective-permute-start
  34.6 1.7 %collective-permute-start.5 = (bf16[768,1280]{1,0:T(8,128)(2,1)}, bf16[768,1280]{1,0:T(8,128)(2,1)}, u32[]{:S(2)}, u32[]{:S(2)}) collective-permute-start(bf16[768,1280]{1,0:T(8,128)(2,1)} %get-tuple-element.47), channel_id=1, source_target_pairs={{0,8},{1,9},{2,10},{3,11},{4,12},{5,13},{6,14},{7,15},{8,0},{9,1},... | collective-permute-start | bytes 5898248 | tf_op jit(solution)/shard_map/ppermute | solution.py:670
  36.3 1.8 %collective-permute-start.4 = (bf16[768,768]{1,0:T(8,128)(2,1)}, bf16[768,768]{1,0:T(8,128)(2,1)}, u32[]{:S(2)}, u32[]{:S(2)}) collective-permute-start(bf16[768,768]{1,0:T(8,128)(2,1)} %get-tuple-element.42), channel_id=1, source_target_pairs={{0,8},{1,9},{2,10},{3,11},{4,12},{5,13},{6,14},{7,15},{8,0},{9,1},... | collective-permute-start | bytes 3538952 | tf_op jit(solution)/shard_map/ppermute | solution.py:670
  38.8 13.1 %own_ladder.1 = (bf16[768,768]{1,0:T(8,128)(2,1)}, bf16[768,768]{1,0:T(8,128)(2,1)}, bf16[4,768,768]{2,1,0:T(8,128)(2,1)}) custom-call(s32[12]{0:T(128)} %bitcast.21, s32[1,1]{1,0:T(1,128)S(6)} %copy.19.count_ref, s32[16]{0:T(128)} %slot_ref.1, bf16[16,64,768]{2,1,0:T(8,128)(2,1)} %bitcast.18, bf16[4,768,768]{2,1,0:T(8,128)(2,1)} %bitcast.9, ...), custom_call_target="tpu_custom_call" | custom-call | tf_op jit(solution)/shard_map/own_ladder/pallas_call | solution.py:260
  51.9 7.8 %collective-permute-done.side_ref = bf16[2,4,64,1024]{3,2,1,0:T(8,128)(2,1)} collective-permute-done((bf16[2,4,64,1024]{3,2,1,0:T(8,128)(2,1)}, bf16[2,4,64,1024]{3,2,1,0:T(8,128)(2,1)}, u32[]{:S(2)}, u32[]{:S(2)}) %collective-permute-start) | collective-permute-done | bytes 1048608 | tf_op jit(solution)/shard_map/ppermute | solution.py:671
  59.6 0.0 collective-permute-start.1
  59.6 1.4 %collective-permute-start.3 = (bf16[768,512]{1,0:T(8,128)(2,1)}, bf16[768,512]{1,0:T(8,128)(2,1)}, u32[]{:S(2)}, u32[]{:S(2)}) collective-permute-start(bf16[768,512]{1,0:T(8,128)(2,1)} %get-tuple-element.39), channel_id=1, source_target_pairs={{0,8},{1,9},{2,10},{3,11},{4,12},{5,13},{6,14},{7,15},{8,0},{9,1},... | collective-permute-start | bytes 2359304 | tf_op jit(solution)/shard_map/ppermute | solution.py:670
  61.0 2.1 %collective-permute-start.2 = (bf16[768,256]{1,0:T(8,128)(2,1)}, bf16[768,256]{1,0:T(8,128)(2,1)}, u32[]{:S(2)}, u32[]{:S(2)}) collective-permute-start(bf16[768,256]{1,0:T(8,128)(2,1)} %get-tuple-element.35), channel_id=1, source_target_pairs={{0,8},{1,9},{2,10},{3,11},{4,12},{5,13},{6,14},{7,15},{8,0},{9,1},... | collective-permute-start | bytes 1179656 | tf_op jit(solution)/shard_map/ppermute | solution.py:675
  63.2 0.0 collective-permute-done.1.twin_ref
  63.2 19.8 %own_cycle.1 = (bf16[4,768,768]{2,1,0:T(8,128)(2,1)}, bf16[4,768,768]{2,1,0:T(8,128)(2,1)}, f32[768,128]{1,0:T(8,128)}, f32[8,768]{1,0:T(8,128)}) custom-call(s32[12]{0:T(128)} %bitcast.22, s32[1,1]{1,0:T(1,128)S(6)} %copy.19.count_ref, f32[2,2]{1,0:T(2,128)} %bitcast.23, f32[1,1024]{1,0:T(1,128)} %bitcast.20, ...), custom_call_target="tpu_custom_call" | custom-call | tf_op jit(solution)/shard_map/own_cycle/pallas_call | solution.py:372
  83.0 0.0 collective-permute-done.5.b1_hbm
  83.0 17.4 %row_0.1 = (f32[4,768,768]{2,1,0:T(8,128)}, bf16[4,768,768]{2,1,0:T(8,128)(2,1)}) custom-call(f32[768,128]{1,0:T(8,128)} %get-tuple-element.33.down_hbm, f32[8,768]{1,0:T(8,128)} %get-tuple-element.34.along_hbm, bf16[768,256]{1,0:T(8,128)(2,1)} %get-tuple-element.46.b0_hbm, bf16[768,1280]{1,0:T(8,128)(2,1)} %collective-permute-done.5.b1_hbm, ...), custom_call_target="tpu_custom_call" | custom-call | tf_op jit(solution)/shard_map/row_0/pallas_call | solution.py:518
  100.4 7.0 %collective-permute-done.4.refs_0_ = bf16[768,768]{1,0:T(8,128)(2,1)} collective-permute-done((bf16[768,768]{1,0:T(8,128)(2,1)}, bf16[768,768]{1,0:T(8,128)(2,1)}, u32[]{:S(2)}, u32[]{:S(2)}) %collective-permute-start.4) | collective-permute-done | bytes 1179680 | tf_op jit(solution)/shard_map/ppermute | solution.py:670
  107.4 10.4 %piece_10_0.1.refs_7_ = bf16[4,768,768]{2,1,0:T(8,128)(2,1)} custom-call(f32[768,128]{1,0:T(8,128)} %get-tuple-element.33.down_hbm, f32[8,768]{1,0:T(8,128)} %get-tuple-element.34.along_hbm, bf16[768,768]{1,0:T(8,128)(2,1)} %collective-permute-done.4.refs_0_, bf16[768,768]{1,0:T(8,128)(2,1)} %get-tuple-element.36.refs_1_.xt_hbm, ...), custom_call_target="tpu_custom_call", output_to_operand_aliasing={{}: (9, {})} | custom-call | tf_op jit(solution)/shard_map/piece_10_0/pallas_call | solution.py:625
  117.8 6.4 %collective-permute-done.3.refs_0_ = bf16[768,512]{1,0:T(8,128)(2,1)} collective-permute-done((bf16[768,512]{1,0:T(8,128)(2,1)}, bf16[768,512]{1,0:T(8,128)(2,1)}, u32[]{:S(2)}, u32[]{:S(2)}) %collective-permute-start.3) | collective-permute-done | bytes 786464 | tf_op jit(solution)/shard_map/ppermute | solution.py:670
  124.2 6.5 %piece_11_0.1 = (bf16[4,768,768]{2,1,0:T(8,128)(2,1)}, bf16[768,768]{1,0:T(8,128)(2,1)}) custom-call(f32[768,128]{1,0:T(8,128)} %get-tuple-element.33.down_hbm, f32[8,768]{1,0:T(8,128)} %get-tuple-element.34.along_hbm, bf16[768,512]{1,0:T(8,128)(2,1)} %collective-permute-done.3.refs_0_, ...), custom_call_target="tpu_custom_call", output_to_operand_aliasing={{0}: (9, {})} | custom-call | tf_op jit(solution)/shard_map/piece_11_0/pallas_call | solution.py:625
  130.7 1.2 collective-permute-done.2.refs_0_
  131.9 8.3 %piece_11_512.1 = (f32[4,768,768]{2,1,0:T(8,128)}, bf16[4,768,768]{2,1,0:T(8,128)(2,1)}) custom-call(f32[768,128]{1,0:T(8,128)} %get-tuple-element.33.down_hbm, f32[8,768]{1,0:T(8,128)} %get-tuple-element.34.along_hbm, bf16[768,256]{1,0:T(8,128)(2,1)} %collective-permute-done.2.refs_0_, ...), custom_call_target="tpu_custom_call", output_to_operand_aliasing={{0}: (10, {}), {1}: (11, {})} | custom-call | tf_op jit(solution)/shard_map/piece_11_512/pallas_call | solution.py:625
Async XLA Ops:
  33.7 25.9 %collective-permute-start = (bf16[2,4,64,1024]{3,2,1,0:T(8,128)(2,1)}, bf16[2,4,64,1024]{3,2,1,0:T(8,128)(2,1)}, u32[]{:S(2)}, u32[]{:S(2)}) collective-permute-start(bf16[2,4,64,1024]{3,2,1,0:T(8,128)(2,1)} %get-tuple-element.28.far_ref), channel_id=1, source_target_pairs={{0,2},{1,3},{2,0},{3,1},{4,6},{5,7},{6,4},{7,5},{8,10},{9,11},{10,... | collective-permute-start | bytes 3145736 | tf_op jit(solution)/shard_map/ppermute | solution.py:671
  34.6 48.4 %collective-permute-start.5 = (bf16[768,1280]{1,0:T(8,128)(2,1)}, bf16[768,1280]{1,0:T(8,128)(2,1)}, u32[]{:S(2)}, u32[]{:S(2)}) collective-permute-start(bf16[768,1280]{1,0:T(8,128)(2,1)} %get-tuple-element.47), channel_id=1, source_target_pairs={{0,8},{1,9},{2,10},{3,11},{4,12},{5,13},{6,14},{7,15},{8,0},{9,1},... | collective-permute-start | bytes 5898248 | tf_op jit(solution)/shard_map/ppermute | solution.py:670
  36.3 71.1 %collective-permute-start.4 = (bf16[768,768]{1,0:T(8,128)(2,1)}, bf16[768,768]{1,0:T(8,128)(2,1)}, u32[]{:S(2)}, u32[]{:S(2)}) collective-permute-start(bf16[768,768]{1,0:T(8,128)(2,1)} %get-tuple-element.42), channel_id=1, source_target_pairs={{0,8},{1,9},{2,10},{3,11},{4,12},{5,13},{6,14},{7,15},{8,0},{9,1},... | collective-permute-start | bytes 3538952 | tf_op jit(solution)/shard_map/ppermute | solution.py:670
  59.6 3.5 %collective-permute-start.1 = (bf16[2,4,64,1024]{3,2,1,0:T(8,128)(2,1)}, bf16[2,4,64,1024]{3,2,1,0:T(8,128)(2,1)}, u32[]{:S(2)}, u32[]{:S(2)}) collective-permute-start(bf16[2,4,64,1024]{3,2,1,0:T(8,128)(2,1)} %collective-permute-done.side_ref), channel_id=1, source_target_pairs={{0,1},{1,0},{2,3},{3,2},{4,5},{5,4},{6,7},{7,6},{8,9},{9,8},{10,11... | collective-permute-start | bytes 3145736 | tf_op jit(solution)/shard_map/ppermute | solution.py:676
  59.6 64.6 %collective-permute-start.3 = (bf16[768,512]{1,0:T(8,128)(2,1)}, bf16[768,512]{1,0:T(8,128)(2,1)}, u32[]{:S(2)}, u32[]{:S(2)}) collective-permute-start(bf16[768,512]{1,0:T(8,128)(2,1)} %get-tuple-element.39), channel_id=1, source_target_pairs={{0,8},{1,9},{2,10},{3,11},{4,12},{5,13},{6,14},{7,15},{8,0},{9,1},... | collective-permute-start | bytes 2359304 | tf_op jit(solution)/shard_map/ppermute | solution.py:670
  61.0 70.8 %collective-permute-start.2 = (bf16[768,256]{1,0:T(8,128)(2,1)}, bf16[768,256]{1,0:T(8,128)(2,1)}, u32[]{:S(2)}, u32[]{:S(2)}) collective-permute-start(bf16[768,256]{1,0:T(8,128)(2,1)} %get-tuple-element.35), channel_id=1, source_target_pairs={{0,8},{1,9},{2,10},{3,11},{4,12},{5,13},{6,14},{7,15},{8,0},{9,1},... | collective-permute-start | bytes 1179656 | tf_op jit(solution)/shard_map/ppermute | solution.py:675

commit v11 on v10

--- a/solution.py
+++ b/solution.py
@@ -108,8 +108,10 @@
     own_x.start()
     transpose(0, 0)
 
+    chunks = first_ref.shape[1] // 128
+
     def send_first(at):
-        columns = pl.ds(at * (first_ref.shape[1] // 2), first_ref.shape[1] // 2)
+        columns = pl.ds(at * 128, 128)
         send(turned.at[0, :, columns], first_ref.at[:, columns], (msend, mrecv), at, mirror)
 
     send_first(0)
@@ -126,7 +128,8 @@
     send(part, part, wsems, 5, zside)
     arrived(far_ref.at[0], wsems, 1)
     send(far_ref.at[0, half:], far_ref.at[1, half:], wsems, 3, back)
-    send_first(1)
+    for at in range(1, chunks):
+        send_first(at)
     to_twin(3)
     to_twin(1)
     transpose(2, 1)
@@ -179,9 +182,8 @@
         arrived(xall_ref.at[origin, 1 - core], xsems, 7 + step)
         origin = origin + 1 - 2 * (origin % 2)
         arrived(xall_ref.at[origin, 1 - core], xsems, 10 + step)
-    for at in range(2):
-        part = first_ref.at[:, pl.ds(at * (first_ref.shape[1] // 2), first_ref.shape[1] // 2)]
-        arrived(part, (msend, mrecv), at)
+    for at in range(chunks):
+        arrived(first_ref.at[:, pl.ds(at * 128, 128)], (msend, mrecv), at)
     for copy in started:
         copy.wait_send()
     for copy in outs + [own_w, own_x]:
@@ -211,8 +213,8 @@
             dma((12,)),
             dma((14,)),
             dma((14,)),
-            dma((2,)),
-            dma((2,)),
+            dma((early // 128,)),
+            dma((early // 128,)),
             dma((8,)),
             dma((5,)),
         ],
@@ -662,7 +664,7 @@
     amp4 = amps[0, 0].reshape(occ * occ, width, width)
     shard = cycle_w[0].reshape(occ * occ, tile_width, window)
 
-    early, split = 256, 512
+    early, split = 384, 512
     tiles, count = domain_tiles[0, 0], domain_count
     xall, wall, far, first, coret, *turned = gather_parts(x_factor, shard, amp4, core, early, split)
     xall = xall.reshape(-1, tile_width, grid_points)

time: 141 us -> 141 us (level); the launches traced: 140 us -> 139 us
  waiting for transfers between devices: 22.3 us -> 16.9 us
  Pallas kernels: 109 us -> 112 us
    pallas_call x1, Pallas kernels: 33.1 us -> 36.4 us  [gather_parts(): pl.pallas_call(gather_kernel, out_shape=[jax.ShapeDtypeStruct(shape, bf16...]
    ppermute x3, waiting for transfers between devices: 13.4 us -> 11.1 us  [per_device(): lax.ppermute(part, 'col', mirror)]
    ppermute x1, waiting for transfers between devices: 7.78 us -> 5.83 us  [per_device(): side = lax.ppermute(far, 'col', [(i, i ^ 2) for i in range(cols)])]
  transfers between devices with their start and end apart: 6 -> 6, of which waited for: 4 -> 3; matrix products, arithmetic and copies ran while one was open for 0% -> 0% of each run, Pallas kernels for 48% -> 48%
where the time goes in v11:
time: 141 us; the launch traced here: 139 us
  Pallas kernels  112 us (79%)
  waiting for transfers between devices  16.9 us (12%)
  starting transfers between devices  8.39 us (6%)
  between operations  1.55 us (1%)
    pallas_call x1, Pallas kernels, gather_parts(): pl.pallas_call(gather_kernel, out_shape=[jax.ShapeDtypeStruct(shape, bf16...  36.4 us
    pallas_call x3, Pallas kernels, piece(): pl.pallas_call(functools.partial(piece_kernel, i, k, low, high, end), out...  25.2 us
    pallas_call x1, Pallas kernels, own_cycle(): pl.pallas_call(own_cycle_kernel, out_shape=(jax.ShapeDtypeStruct((4, widt...  19.8 us
    pallas_call x1, Pallas kernels, row(): pl.pallas_call(functools.partial(row_kernel, i), out_shape=[jax.ShapeDtyp...  17.5 us
    pallas_call x1, Pallas kernels, own_ladder(): pl.pallas_call(own_ladder_kernel, out_shape=(jax.ShapeDtypeStruct((width,...  13.1 us
    ppermute x3, waiting for transfers between devices, per_device(): lax.ppermute(part, 'col', mirror)  11.1 us
    ppermute x1, waiting for transfers between devices, per_device(): side = lax.ppermute(far, 'col', [(i, i ^ 2) for i in range(cols)])  5.83 us
    ppermute x3, starting transfers between devices, per_device(): lax.ppermute(part, 'col', mirror)  5.7 us
  transfers between devices with their start and end apart: 6, of which 3 were waited for; matrix products, arithmetic and copies ran while one was open for 0% of the time, Pallas kernels for 48%

profile of v11, /device:TPU:6, one launch (start us, length us, event | category | flops | bytes accessed | tf_op | source)
XLA Modules:
  0.0 138.9 jit_solution(3620561604124337228)
XLA Ops:
  0.6 36.4 %gather_parts.1 = (bf16[8,2,64,768]{3,2,1,0:T(8,128)(2,1)}, bf16[16,4,64,1024]{3,2,1,0:T(8,128)(2,1)}, bf16[2,4,64,1024]{3,2,1,0:T(8,128)(2,1)}, bf16[768,384]{1...) custom-call(bf16[2,64,768]{2,1,0:T(8,128)(2,1)} %x_ref.1, ...), custom_call_target="tpu_custom_call" | custom-call | tf_op jit(solution)/shard_map/gather_parts/pallas_call | solution.py:203
  37.0 1.3 collective-permute-start
  38.3 2.2 %collective-permute-start.5 = (bf16[768,1152]{1,0:T(8,128)(2,1)}, bf16[768,1152]{1,0:T(8,128)(2,1)}, u32[]{:S(2)}, u32[]{:S(2)}) collective-permute-start(bf16[768,1152]{1,0:T(8,128)(2,1)} %get-tuple-element.47), channel_id=1, source_target_pairs={{0,8},{1,9},{2,10},{3,11},{4,12},{5,13},{6,14},{7,15},{8,0},{9,1},... | collective-permute-start | bytes 5308424 | tf_op jit(solution)/shard_map/ppermute | solution.py:672
  40.5 1.4 collective-permute-start.4
  42.5 13.1 %own_ladder.1 = (bf16[768,768]{1,0:T(8,128)(2,1)}, bf16[768,768]{1,0:T(8,128)(2,1)}, bf16[4,768,768]{2,1,0:T(8,128)(2,1)}) custom-call(s32[12]{0:T(128)} %bitcast.21, s32[1,1]{1,0:T(1,128)S(6)} %copy.19.count_ref, s32[16]{0:T(128)} %slot_ref.1, bf16[16,64,768]{2,1,0:T(8,128)(2,1)} %bitcast.18, bf16[4,768,768]{2,1,0:T(8,128)(2,1)} %bitcast.9, ...), custom_call_target="tpu_custom_call" | custom-call | tf_op jit(solution)/shard_map/own_ladder/pallas_call | solution.py:262
  55.6 5.8 %collective-permute-done.side_ref = bf16[2,4,64,1024]{3,2,1,0:T(8,128)(2,1)} collective-permute-done((bf16[2,4,64,1024]{3,2,1,0:T(8,128)(2,1)}, bf16[2,4,64,1024]{3,2,1,0:T(8,128)(2,1)}, u32[]{:S(2)}, u32[]{:S(2)}) %collective-permute-start) | collective-permute-done | bytes 1048608 | tf_op jit(solution)/shard_map/ppermute | solution.py:673
  61.4 0.0 collective-permute-start.1
  61.4 2.2 %collective-permute-start.3 = (bf16[768,512]{1,0:T(8,128)(2,1)}, bf16[768,512]{1,0:T(8,128)(2,1)}, u32[]{:S(2)}, u32[]{:S(2)}) collective-permute-start(bf16[768,512]{1,0:T(8,128)(2,1)} %get-tuple-element.39), channel_id=1, source_target_pairs={{0,8},{1,9},{2,10},{3,11},{4,12},{5,13},{6,14},{7,15},{8,0},{9,1},... | collective-permute-start | bytes 2359304 | tf_op jit(solution)/shard_map/ppermute | solution.py:672
  63.6 1.4 collective-permute-start.2
  65.0 0.0 collective-permute-done.1.twin_ref
  65.0 19.8 %own_cycle.1 = (bf16[4,768,768]{2,1,0:T(8,128)(2,1)}, bf16[4,768,768]{2,1,0:T(8,128)(2,1)}, f32[768,128]{1,0:T(8,128)}, f32[8,768]{1,0:T(8,128)}) custom-call(s32[12]{0:T(128)} %bitcast.22, s32[1,1]{1,0:T(1,128)S(6)} %copy.19.count_ref, f32[2,2]{1,0:T(2,128)} %bitcast.23, f32[1,1024]{1,0:T(1,128)} %bitcast.20, ...), custom_call_target="tpu_custom_call" | custom-call | tf_op jit(solution)/shard_map/own_cycle/pallas_call | solution.py:374
  84.8 0.0 collective-permute-done.5.b1_hbm
  84.8 17.5 %row_0.1 = (f32[4,768,768]{2,1,0:T(8,128)}, bf16[4,768,768]{2,1,0:T(8,128)(2,1)}) custom-call(f32[768,128]{1,0:T(8,128)} %get-tuple-element.33.down_hbm, f32[8,768]{1,0:T(8,128)} %get-tuple-element.34.along_hbm, bf16[768,384]{1,0:T(8,128)(2,1)} %get-tuple-element.46.b0_hbm, bf16[768,1152]{1,0:T(8,128)(2,1)} %collective-permute-done.5.b1_hbm, ...), custom_call_target="tpu_custom_call" | custom-call | tf_op jit(solution)/shard_map/row_0/pallas_call | solution.py:520
  102.3 4.7 %collective-permute-done.4.refs_0_ = bf16[768,768]{1,0:T(8,128)(2,1)} collective-permute-done((bf16[768,768]{1,0:T(8,128)(2,1)}, bf16[768,768]{1,0:T(8,128)(2,1)}, u32[]{:S(2)}, u32[]{:S(2)}) %collective-permute-start.4) | collective-permute-done | bytes 1179680 | tf_op jit(solution)/shard_map/ppermute | solution.py:672
  107.0 10.4 %piece_10_0.1.refs_7_ = bf16[4,768,768]{2,1,0:T(8,128)(2,1)} custom-call(f32[768,128]{1,0:T(8,128)} %get-tuple-element.33.down_hbm, f32[8,768]{1,0:T(8,128)} %get-tuple-element.34.along_hbm, bf16[768,768]{1,0:T(8,128)(2,1)} %collective-permute-done.4.refs_0_, bf16[768,768]{1,0:T(8,128)(2,1)} %get-tuple-element.36.refs_1_.xt_hbm, ...), custom_call_target="tpu_custom_call", output_to_operand_aliasing={{}: (9, {})} | custom-call | tf_op jit(solution)/shard_map/piece_10_0/pallas_call | solution.py:627
  117.4 6.4 %collective-permute-done.3.refs_0_ = bf16[768,512]{1,0:T(8,128)(2,1)} collective-permute-done((bf16[768,512]{1,0:T(8,128)(2,1)}, bf16[768,512]{1,0:T(8,128)(2,1)}, u32[]{:S(2)}, u32[]{:S(2)}) %collective-permute-start.3) | collective-permute-done | bytes 786464 | tf_op jit(solution)/shard_map/ppermute | solution.py:672
  123.8 6.5 %piece_11_0.1 = (bf16[4,768,768]{2,1,0:T(8,128)(2,1)}, bf16[768,768]{1,0:T(8,128)(2,1)}) custom-call(f32[768,128]{1,0:T(8,128)} %get-tuple-element.33.down_hbm, f32[8,768]{1,0:T(8,128)} %get-tuple-element.34.along_hbm, bf16[768,512]{1,0:T(8,128)(2,1)} %collective-permute-done.3.refs_0_, ...), custom_call_target="tpu_custom_call", output_to_operand_aliasing={{0}: (9, {})} | custom-call | tf_op jit(solution)/shard_map/piece_11_0/pallas_call | solution.py:627
  130.3 0.0 collective-permute-done.2.refs_0_
  130.3 8.3 %piece_11_512.1 = (f32[4,768,768]{2,1,0:T(8,128)}, bf16[4,768,768]{2,1,0:T(8,128)(2,1)}) custom-call(f32[768,128]{1,0:T(8,128)} %get-tuple-element.33.down_hbm, f32[8,768]{1,0:T(8,128)} %get-tuple-element.34.along_hbm, bf16[768,256]{1,0:T(8,128)(2,1)} %collective-permute-done.2.refs_0_, ...), custom_call_target="tpu_custom_call", output_to_operand_aliasing={{0}: (10, {}), {1}: (11, {})} | custom-call | tf_op jit(solution)/shard_map/piece_11_512/pallas_call | solution.py:627
Async XLA Ops:
  37.0 24.4 %collective-permute-start = (bf16[2,4,64,1024]{3,2,1,0:T(8,128)(2,1)}, bf16[2,4,64,1024]{3,2,1,0:T(8,128)(2,1)}, u32[]{:S(2)}, u32[]{:S(2)}) collective-permute-start(bf16[2,4,64,1024]{3,2,1,0:T(8,128)(2,1)} %get-tuple-element.28.far_ref), channel_id=1, source_target_pairs={{0,2},{1,3},{2,0},{3,1},{4,6},{5,7},{6,4},{7,5},{8,10},{9,11},{10,... | collective-permute-start | bytes 3145736 | tf_op jit(solution)/shard_map/ppermute | solution.py:673
  38.3 46.4 %collective-permute-start.5 = (bf16[768,1152]{1,0:T(8,128)(2,1)}, bf16[768,1152]{1,0:T(8,128)(2,1)}, u32[]{:S(2)}, u32[]{:S(2)}) collective-permute-start(bf16[768,1152]{1,0:T(8,128)(2,1)} %get-tuple-element.47), channel_id=1, source_target_pairs={{0,8},{1,9},{2,10},{3,11},{4,12},{5,13},{6,14},{7,15},{8,0},{9,1},... | collective-permute-start | bytes 5308424 | tf_op jit(solution)/shard_map/ppermute | solution.py:672
  40.5 66.5 %collective-permute-start.4 = (bf16[768,768]{1,0:T(8,128)(2,1)}, bf16[768,768]{1,0:T(8,128)(2,1)}, u32[]{:S(2)}, u32[]{:S(2)}) collective-permute-start(bf16[768,768]{1,0:T(8,128)(2,1)} %get-tuple-element.42), channel_id=1, source_target_pairs={{0,8},{1,9},{2,10},{3,11},{4,12},{5,13},{6,14},{7,15},{8,0},{9,1},... | collective-permute-start | bytes 3538952 | tf_op jit(solution)/shard_map/ppermute | solution.py:672
  61.4 3.5 %collective-permute-start.1 = (bf16[2,4,64,1024]{3,2,1,0:T(8,128)(2,1)}, bf16[2,4,64,1024]{3,2,1,0:T(8,128)(2,1)}, u32[]{:S(2)}, u32[]{:S(2)}) collective-permute-start(bf16[2,4,64,1024]{3,2,1,0:T(8,128)(2,1)} %collective-permute-done.side_ref), channel_id=1, source_target_pairs={{0,1},{1,0},{2,3},{3,2},{4,5},{5,4},{6,7},{7,6},{8,9},{9,8},{10,11... | collective-permute-start | bytes 3145736 | tf_op jit(solution)/shard_map/ppermute | solution.py:678
  61.4 62.4 %collective-permute-start.3 = (bf16[768,512]{1,0:T(8,128)(2,1)}, bf16[768,512]{1,0:T(8,128)(2,1)}, u32[]{:S(2)}, u32[]{:S(2)}) collective-permute-start(bf16[768,512]{1,0:T(8,128)(2,1)} %get-tuple-element.39), channel_id=1, source_target_pairs={{0,8},{1,9},{2,10},{3,11},{4,12},{5,13},{6,14},{7,15},{8,0},{9,1},... | collective-permute-start | bytes 2359304 | tf_op jit(solution)/shard_map/ppermute | solution.py:672
  63.6 66.7 %collective-permute-start.2 = (bf16[768,256]{1,0:T(8,128)(2,1)}, bf16[768,256]{1,0:T(8,128)(2,1)}, u32[]{:S(2)}, u32[]{:S(2)}) collective-permute-start(bf16[768,256]{1,0:T(8,128)(2,1)} %get-tuple-element.35), channel_id=1, source_target_pairs={{0,8},{1,9},{2,10},{3,11},{4,12},{5,13},{6,14},{7,15},{8,0},{9,1},... | collective-permute-start | bytes 1179656 | tf_op jit(solution)/shard_map/ppermute | solution.py:677
